TPU v7x, 32 devices: a whole 2x2x4 slice. The times are simulated.
32 devices in a mesh: level: 4 (over z), blocks: 8 (over y, x, core).
Axes of the slice: x: 2, y: 2, z: 4, core: 2. Of those that a mesh axis runs over, the one named last changes fastest.
Arguments:
- populations: float32 [4, 19, 64, 1024], P('level', None, 'blocks'), may hold values from 0.3 to 2, as said below
- solid: int32 [4, 64, 1024], P('level', 'blocks'), may hold values from 0 to 1, as said below
Outputs:
- evolved: float32 [4, 19, 64, 1024], P('level', None, 'blocks')
Inputs may be any that keep to these rules, and one draw needn't show every extreme that they name: Normalized populations of a state near equilibrium. `solid`: 1 marks a cell of a level whose centre lies inside one of 32 large or 64 small spheres, radii in the ratio 8, the same spheres on every level.
All inputs are finite; a program needn't handle non-finite values.
Results may differ from a plain program's by a relative error of at most 0.0001.
Values sent between devices are 32-bit elements; how exact they have to be, the bound alone decides.
No kernel may reach another device: no remote copies, remote signals or barrier semaphores. Data moves between devices by JAX's collectives and lax.ppermute only.
A program may use at most 192 MiB of HBM per device.

v0:
```python
import jax
import jax.numpy as jnp
import numpy as np
from jax import lax
from jax.sharding import PartitionSpec as P

NY = 32
NZ = 32


VELOCITY = (
    (0, 0, 0),
    (1, 0, 0),
    (-1, 0, 0),
    (0, 1, 0),
    (0, -1, 0),
    (0, 0, 1),
    (0, 0, -1),
    (1, 1, 0),
    (-1, -1, 0),
    (1, -1, 0),
    (-1, 1, 0),
    (1, 0, 1),
    (-1, 0, -1),
    (1, 0, -1),
    (-1, 0, 1),
    (0, 1, 1),
    (0, -1, -1),
    (0, 1, -1),
    (0, -1, 1),
)
WEIGHTS = (1.0 / 3.0,) + (1.0 / 18.0,) * 6 + (1.0 / 36.0,) * 12
OPPOSITE = (0, 2, 1, 4, 3, 6, 5, 8, 7, 10, 9, 12, 11, 14, 13, 16, 15, 18, 17)
TAU_BASE = 1.0


def padded(block, sides, width):
    for axis, dim in sides:
        count = lax.axis_size(axis)
        forward = [(i, i + 1) for i in range(count - 1)]
        forward.append((count - 1, 0))
        backward = [(target, source) for source, target in forward]
        low = lax.ppermute(
            lax.slice_in_dim(block, block.shape[dim] - width, None, axis=dim), axis, forward
        )
        high = lax.ppermute(lax.slice_in_dim(block, 0, width, axis=dim), axis, backward)
        block = jnp.concatenate([low, block, high], axis=dim)
    return block


def passed_along(value, axis, steps):
    count = lax.axis_size(axis)
    first, last = (max(0, -steps), min(count, count - steps))
    return lax.ppermute(value, axis, [(source, source + steps) for source in range(first, last)])


def relaxation(level_id):
    return 2.0**level_id * (TAU_BASE - 0.5) + 0.5


def equilibrium(values):
    density = sum((WEIGHTS[direction] * values[direction] for direction in range(19)))
    velocity_list = []
    for component in range(3):
        momentum = sum(
            (
                WEIGHTS[direction] * VELOCITY[direction][component] * values[direction]
                for direction in range(19)
                if VELOCITY[direction][component] != 0
            )
        )
        velocity_list.append(momentum / density)
    speed_sq = velocity_list[0] ** 2 + velocity_list[1] ** 2 + velocity_list[2] ** 2
    result = []
    for direction in range(19):
        projection = sum(
            (
                VELOCITY[direction][component] * velocity_list[component]
                for component in range(3)
                if VELOCITY[direction][component] != 0
            )
        )
        result.append(
            density * (1.0 + 3.0 * projection + 4.5 * projection * projection - 1.5 * speed_sq)
        )
    return jnp.stack(result)


def collide(values, solid_level, tau_value):
    balance = equilibrium(values)
    relaxed = values + (balance - values) / tau_value
    flipped = jnp.stack([values[OPPOSITE[direction]] for direction in range(19)])
    return jnp.where(solid_level[None] == 1, flipped, relaxed)


def finish_stream(sources, collided, ny_cells, nz_level):
    positions = jnp.arange(ny_cells * nz_level, dtype=jnp.int32)
    y_index = positions // nz_level
    z_index = positions % nz_level
    result = []
    for direction in range(19):
        step_y = VELOCITY[direction][1]
        step_z = VELOCITY[direction][2]
        shifted = jnp.roll(sources[direction], step_y * nz_level + step_z, axis=1)
        inside = (
            (y_index - step_y >= 0)
            & (y_index - step_y < ny_cells)
            & (z_index - step_z >= 0)
            & (z_index - step_z < nz_level)
        )
        result.append(jnp.where(inside[None, :], shifted, collided[OPPOSITE[direction]]))
    return jnp.stack(result)


def interface_plan(ny_cells, child_nz):
    quarter = child_nz // 2
    targets = list(range(child_nz)) + list(range((ny_cells - 1) * child_nz, ny_cells * child_nz))
    targets += [y_row * child_nz + child_nz - 1 for y_row in range(1, ny_cells - 1)]
    picks = [z_row // 2 for z_row in range(child_nz)] + [
        quarter + z_row // 2 for z_row in range(child_nz)
    ]
    picks += [2 * quarter + y_row // 2 for y_row in range(1, ny_cells - 1)]
    return (np.array(targets, np.int32), np.array(picks, np.int32))


def make_packet(level_field, ny_cells, parent_nz, level_id):
    grid_view = level_field.reshape(19, level_field.shape[1], ny_cells, parent_nz)
    quarter = parent_nz // 4
    rim_values = jnp.concatenate(
        [
            grid_view[:, :, ny_cells // 4, :quarter],
            grid_view[:, :, 3 * ny_cells // 4 - 1, :quarter],
            grid_view[:, :, ny_cells // 4 : 3 * ny_cells // 4, quarter - 1],
        ],
        axis=2,
    )
    balance = equilibrium(rim_values)
    scaling = relaxation(level_id + 1) / (2.0 * relaxation(level_id))
    return balance + scaling * (rim_values - balance)


def apply_interface(level_field, packet, ny_cells, child_nz):
    targets, picks = interface_plan(ny_cells, child_nz)
    widened = jnp.repeat(packet, 2, axis=1)
    return level_field.at[:, :, targets].set(widened[:, :, picks])


def restrict_packet(level_field, ny_cells, child_nz, level_id):
    parent_rows = level_field.shape[1] // 2
    grid_view = level_field.reshape(19, parent_rows, 2, ny_cells // 2, 2, child_nz // 2, 2)
    averaged = grid_view.sum(axis=(2, 4, 6)) / 8.0
    balance = equilibrium(averaged)
    scaling = 2.0 * relaxation(level_id - 1) / relaxation(level_id)
    restored = balance + scaling * (averaged - balance)
    return restored.reshape(19, parent_rows, ny_cells // 2 * (child_nz // 2))


def overwrite(level_field, packet, ny_cells, parent_nz):
    parent_rows = level_field.shape[1]
    quarter = parent_nz // 4
    grid_view = level_field.reshape(19, parent_rows, ny_cells, parent_nz)
    grid_view = grid_view.at[:, :, ny_cells // 4 : 3 * ny_cells // 4, :quarter].set(
        packet.reshape(19, parent_rows, ny_cells // 2, quarter)
    )
    return grid_view.reshape(19, parent_rows, ny_cells * parent_nz)


def roster(level_id, level_count):
    events = [("step", level_id)]
    if level_id + 1 < level_count:
        for repeat in range(2):
            events += roster(level_id + 1, level_count)
        events.append(("restrict", level_id + 1))
    return events


def level_run(populations, solid):
    stored = populations[0]
    solid_store = solid[0]
    slab_rows = stored.shape[1]
    plane_size = stored.shape[2]
    level_count = lax.axis_size("level")
    my_level = lax.axis_index("level")
    packets = {}
    for event_kind, level_id in roster(0, level_count):
        factor = 2**level_id
        rows_level = slab_rows * factor
        nz_level = NZ // factor
        current = stored.reshape(19, rows_level, plane_size // factor)
        if event_kind == "step":
            solid_level = solid_store.reshape(rows_level, plane_size // factor)
            incoming = packets.get(level_id)

            def prepare(level_field):
                if incoming is not None:
                    level_field = apply_interface(level_field, incoming, NY, nz_level)
                return collide(level_field, solid_level, relaxation(level_id))

            def unchanged(level_field):
                return level_field

            collided = lax.cond(my_level == level_id, prepare, unchanged, current)
            extended = padded(collided, (("blocks", 1),), 1)

            def advance():
                sources = [
                    extended[
                        direction,
                        1 - VELOCITY[direction][0] : 1 - VELOCITY[direction][0] + rows_level,
                    ]
                    for direction in range(19)
                ]
                return finish_stream(sources, collided, NY, nz_level)

            passed = lax.cond(my_level == level_id, advance, lambda: collided)
            stored = passed.reshape(19, slab_rows, plane_size)
            if level_id + 1 < level_count:
                outgoing = make_packet(passed, NY, nz_level, level_id)
                packets[level_id + 1] = passed_along(outgoing, "level", 1)
        else:
            outgoing = restrict_packet(current, NY, nz_level, level_id)
            arrived = passed_along(outgoing, "level", -1)
            parent_view = stored.reshape(19, rows_level // 2, plane_size * 2 // factor)

            def refine_back():
                return overwrite(parent_view, arrived, NY, 2 * nz_level).reshape(
                    19, slab_rows, plane_size
                )

            previous = stored
            stored = lax.cond(my_level == level_id - 1, refine_back, lambda: previous)
    return stored[None]


def shards(populations, solid):
    return level_run(populations, solid)


def solution(mesh):
    in_specs = (P("level", None, "blocks", None), P("level", "blocks", None))
    out_specs = P("level", None, "blocks", None)
    return jax.shard_map(shards, mesh=mesh, in_specs=in_specs, out_specs=out_specs, check_vma=False)
```

profile of v0, /device:TPU:0, one launch (start us, length us, event | category | flops | bytes accessed | tf_op | source)
XLA Modules:
  0.0 774.3 jit_solution(5486723733598977995)
XLA Ops:
  3.0 2.9 collective-permute-start.1
  8.1 3.2 conditional.38
  24.9 3.2 reshape.4369
  30.0 4.0 slice.8009
  34.0 3.5 copy.7581
  38.2 23.4 %collective-permute-start.5 = (f32[19,16,24]{2,1,0:T(8,128)S(1)}, f32[19,16,24]{2,1,0:T(8,128)S(1)}, u32[]{:S(2)}, u32[]{:S(2)}) collective-permute-start(f32[19,16,24]{2,1,0:T(8,128)S(1)} %multiply_add_fusion.11), channel_id=1, source_target_pairs={{0,8},{8,16},{16,24},{1,9},{9,17},{17,25},{2,10},{10,18},{18,26},{... | collective-permute-start | bytes 87560 | tf_op jit(solution)/shard_map/ppermute | solution.py:54
  61.8 3.7 collective-permute-done.5
  71.3 4.4 collective-permute-start.8
  75.7 5.0 collective-permute-done.8
  88.7 3.5 pad_maximum_fusion
  100.4 3.5 pad_maximum_fusion.1
  104.0 5.6 copy.7295
  109.7 5.1 reduce_sum.117
  117.6 21.3 %collective-permute-done.13 = f32[19,32,32]{1,2,0:T(8,128)S(1)} collective-permute-done((f32[19,32,32]{1,2,0:T(8,128)S(1)}, f32[19,32,32]{1,2,0:T(8,128)S(1)}, u32[]{:S(2)}, u32[]{:S(2)}) %collective-permute-start.13) | collective-permute-done | bytes 77856 | tf_op jit(solution)/shard_map/ppermute | solution.py:54
  147.4 4.1 collective-permute-start.16
  151.6 5.1 collective-permute-done.16
  163.5 3.5 pad_maximum_fusion.2
  173.2 10.4 %conditional.53 = (f32[19,64,128]{2,1,0:T(8,128)S(1)}, f32[19,32,16,2]{0,3,2,1:T(2,128)}, f32[19,8,1024]{2,1,0:T(8,128)S(1)}, f32[19,32,32]{1,2,0:T(8,128)S(1)}) conditional(s32[]{:T(128)} %convert_element_type.11, f32[19,64,128]{2,1,0:T(8,128)S(1)} %get-tuple-element.2926, (f32[19,64,128]{2,1,0:T(8,128)S(1)}, f32[19,66,128]{2,1,0:T(8,128)S(1)}) %tuple.399), branch_computations={%region_40.42_spmd, %region_42.44_spmd} | conditional | flops 438144 | bytes 9058468 | solution.py:215
  176.1 5.9 reduce_sum.104
  187.2 92.7 %collective-permute-done.21 = f32[19,32,32]{1,2,0:T(8,128)S(1)} collective-permute-done((f32[19,32,32]{1,2,0:T(8,128)S(1)}, f32[19,32,32]{1,2,0:T(8,128)S(1)}, u32[]{:S(2)}, u32[]{:S(2)}) %collective-permute-start.21) | collective-permute-done | bytes 77856 | tf_op jit(solution)/shard_map/ppermute | solution.py:54
  282.7 5.1 reduce_sum.118
  294.4 6.3 collective-permute-done.22
  300.7 3.2 conditional.55
  300.7 3.0 copy.7585
  308.7 3.0 conditional.57
  311.7 3.2 reshape.4372
  323.5 103.1 %collective-permute-start.25 = (f32[19,16,24]{2,1,0:T(8,128)S(1)}, f32[19,16,24]{2,1,0:T(8,128)}, u32[]{:S(2)}, u32[]{:S(2)}) collective-permute-start(f32[19,16,24]{2,1,0:T(8,128)S(1)} %multiply_add_fusion.9), channel_id=1, source_target_pairs={{0,8},{8,16},{16,24},{1,9},{9,17},{17,25},{2,10},{10,18},{18,26},{... | collective-permute-start | bytes 87560 | tf_op jit(solution)/shard_map/ppermute | solution.py:54
  438.1 4.5 collective-permute-start.28
  442.6 5.6 collective-permute-done.28
  453.0 3.1 pad_maximum_fusion.3
  463.9 3.5 pad_maximum_fusion.4
  467.6 5.6 copy.7428
  473.2 5.1 reduce_sum.119
  481.1 23.5 %collective-permute-done.33 = f32[19,32,32]{1,2,0:T(8,128)S(1)} collective-permute-done((f32[19,32,32]{1,2,0:T(8,128)S(1)}, f32[19,32,32]{1,2,0:T(8,128)S(1)}, u32[]{:S(2)}, u32[]{:S(2)}) %collective-permute-start.33) | collective-permute-done | bytes 77856 | tf_op jit(solution)/shard_map/ppermute | solution.py:54
  513.4 4.4 collective-permute-start.36
  517.8 5.3 collective-permute-done.36
  530.3 3.5 pad_maximum_fusion.5
  539.8 10.5 %conditional.70 = (f32[19,64,128]{2,1,0:T(8,128)S(1)}, f32[19,32,16,2]{0,3,2,1:T(2,128)}, f32[19,8,1024]{2,1,0:T(8,128)S(1)}, f32[19,32,32]{1,2,0:T(8,128)S(1)}) conditional(s32[]{:T(128)} %convert_element_type.11, f32[19,64,128]{2,1,0:T(8,128)S(1)} %get-tuple-element.2940, (f32[19,64,128]{2,1,0:T(8,128)S(1)}, f32[19,66,128]{2,1,0:T(8,128)S(1)}) %tuple.416), branch_computations={%region_85.87_spmd, %region_87.89_spmd} | conditional | flops 438144 | bytes 9058468 | solution.py:215
  542.7 5.9 reduce_sum.108
  553.9 88.8 %collective-permute-done.41 = f32[19,32,32]{1,2,0:T(8,128)S(1)} collective-permute-done((f32[19,32,32]{1,2,0:T(8,128)S(1)}, f32[19,32,32]{1,2,0:T(8,128)S(1)}, u32[]{:S(2)}, u32[]{:S(2)}) %collective-permute-start.41) | collective-permute-done | bytes 77856 | tf_op jit(solution)/shard_map/ppermute | solution.py:54
  645.5 5.1 reduce_sum.120
  657.1 6.2 collective-permute-done.42
  663.3 3.2 conditional.72
  663.3 3.0 copy.7570
  666.5 2.9 copy.7532
  678.9 87.3 %collective-permute-done.43 = f32[19,8,128]{2,1,0:T(8,128)S(1)} collective-permute-done((f32[19,8,128]{2,1,0:T(8,128)S(1)}, f32[19,8,128]{2,1,0:T(8,128)S(1)}, u32[]{:S(2)}, u32[]{:S(2)}) %collective-permute-start.43) | collective-permute-done | bytes 77856 | tf_op jit(solution)/shard_map/ppermute | solution.py:54
  766.2 6.9 conditional.73
  770.1 3.0 copy.7572
  (822 shorter events, 196.7 us)
Async XLA Ops:
  2.5 5.5 collective-permute-start
  3.0 5.0 collective-permute-start.1
  16.6 3.3 collective-permute-start.2
  20.0 4.5 collective-permute-start.3
  20.9 3.7 collective-permute-start.4
  37.9 27.6 %copy-start.12 = (s32[46]{0:T(128)S(1)}, s32[46]{0:T(128)}, u32[]{:S(2)}) copy-start(s32[46]{0:T(128)} %constant.1880.clone) | copy-start | bytes 556
  37.9 27.6 %copy-start.13 = (s32[46]{0:T(128)S(1)}, s32[46]{0:T(128)}, u32[]{:S(2)}) copy-start(s32[46]{0:T(128)} %constant.1879.clone) | copy-start | bytes 556
  38.2 27.2 %collective-permute-start.5 = (f32[19,16,24]{2,1,0:T(8,128)S(1)}, f32[19,16,24]{2,1,0:T(8,128)S(1)}, u32[]{:S(2)}, u32[]{:S(2)}) collective-permute-start(f32[19,16,24]{2,1,0:T(8,128)S(1)} %multiply_add_fusion.11), channel_id=1, source_target_pairs={{0,8},{8,16},{16,24},{1,9},{9,17},{17,25},{2,10},{10,18},{18,26},{... | collective-permute-start | bytes 87560 | tf_op jit(solution)/shard_map/ppermute | solution.py:54
  65.5 4.1 collective-permute-start.6
  65.6 4.1 collective-permute-start.7
  71.0 9.8 %copy-start.10 = (s32[38]{0:T(128)S(1)}, s32[38]{0:T(128)}, u32[]{:S(2)}) copy-start(s32[38]{0:T(128)} %constant.1882.clone) | copy-start | bytes 460
  71.0 9.8 %copy-start.11 = (s32[38]{0:T(128)S(1)}, s32[38]{0:T(128)}, u32[]{:S(2)}) copy-start(s32[38]{0:T(128)} %constant.1881.clone) | copy-start | bytes 460
  71.3 9.5 %collective-permute-start.8 = (f32[19,32,20]{1,2,0:T(8,128)S(1)}, f32[19,32,20]{1,2,0:T(8,128)S(1)}, u32[]{:S(2)}, u32[]{:S(2)}) collective-permute-start(f32[19,32,20]{1,2,0:T(8,128)S(1)} %multiply_add_fusion.7), channel_id=1, source_target_pairs={{0,8},{8,16},{16,24},{1,9},{9,17},{17,25},{2,10},{10,18},{18,26},{... | collective-permute-start | bytes 145928 | tf_op jit(solution)/shard_map/ppermute | solution.py:54
  80.8 3.8 collective-permute-start.10
  83.1 4.0 collective-permute-start.9
  94.3 2.1 collective-permute-start.12
  94.9 4.0 collective-permute-start.11
  116.3 22.6 %collective-permute-start.13 = (f32[19,32,32]{1,2,0:T(8,128)S(1)}, f32[19,32,32]{1,2,0:T(8,128)S(1)}, u32[]{:S(2)}, u32[]{:S(2)}) collective-permute-start(f32[19,32,32]{1,2,0:T(8,128)S(1)} %multiply_add_fusion.3), channel_id=1, source_target_pairs={{8,0},{16,8},{24,16},{9,1},{17,9},{25,17},{10,2},{18,10},{26,18},{... | collective-permute-start | bytes 233480 | tf_op jit(solution)/shard_map/ppermute | solution.py:54
  141.7 4.1 collective-permute-start.14
  141.8 4.1 collective-permute-start.15
  147.4 9.3 %collective-permute-start.16 = (f32[19,32,20]{1,2,0:T(8,128)S(1)}, f32[19,32,20]{1,2,0:T(8,128)S(1)}, u32[]{:S(2)}, u32[]{:S(2)}) collective-permute-start(f32[19,32,20]{1,2,0:T(8,128)S(1)} %multiply_add_fusion.6), channel_id=1, source_target_pairs={{0,8},{8,16},{16,24},{1,9},{9,17},{17,25},{2,10},{10,18},{18,26},{... | collective-permute-start | bytes 145928 | tf_op jit(solution)/shard_map/ppermute | solution.py:54
  156.7 2.7 collective-permute-start.18
  157.9 4.0 collective-permute-start.17
  169.1 4.0 collective-permute-start.19
  169.1 4.0 collective-permute-start.20
  185.9 94.0 %collective-permute-start.21 = (f32[19,32,32]{1,2,0:T(8,128)S(1)}, f32[19,32,32]{1,2,0:T(8,128)S(1)}, u32[]{:S(2)}, u32[]{:S(2)}) collective-permute-start(f32[19,32,32]{1,2,0:T(8,128)S(1)} %multiply_add_fusion.2), channel_id=1, source_target_pairs={{8,0},{16,8},{24,16},{9,1},{17,9},{25,17},{10,2},{18,10},{26,18},{... | collective-permute-start | bytes 233480 | tf_op jit(solution)/shard_map/ppermute | solution.py:54
  293.1 7.6 collective-permute-start.22
  303.9 4.7 collective-permute-start.23
  304.0 4.6 collective-permute-start.24
  323.5 105.1 %collective-permute-start.25 = (f32[19,16,24]{2,1,0:T(8,128)S(1)}, f32[19,16,24]{2,1,0:T(8,128)}, u32[]{:S(2)}, u32[]{:S(2)}) collective-permute-start(f32[19,16,24]{2,1,0:T(8,128)S(1)} %multiply_add_fusion.9), channel_id=1, source_target_pairs={{0,8},{8,16},{16,24},{1,9},{9,17},{17,25},{2,10},{10,18},{18,26},{... | collective-permute-start | bytes 87560 | tf_op jit(solution)/shard_map/ppermute | solution.py:54
  428.6 4.2 collective-permute-start.26
  428.7 4.1 collective-permute-start.27
  438.1 10.2 %collective-permute-start.28 = (f32[19,32,20]{1,2,0:T(8,128)S(1)}, f32[19,32,20]{1,2,0:T(8,128)S(1)}, u32[]{:S(2)}, u32[]{:S(2)}) collective-permute-start(f32[19,32,20]{1,2,0:T(8,128)S(1)} %multiply_add_fusion.5), channel_id=1, source_target_pairs={{0,8},{8,16},{16,24},{1,9},{9,17},{17,25},{2,10},{10,18},{18,26},{... | collective-permute-start | bytes 145928 | tf_op jit(solution)/shard_map/ppermute | solution.py:54
  448.3 2.2 collective-permute-start.30
  448.3 4.2 collective-permute-start.29
  457.8 2.1 collective-permute-start.32
  458.4 4.0 collective-permute-start.31
  479.8 24.8 %collective-permute-start.33 = (f32[19,32,32]{1,2,0:T(8,128)S(1)}, f32[19,32,32]{1,2,0:T(8,128)S(1)}, u32[]{:S(2)}, u32[]{:S(2)}) collective-permute-start(f32[19,32,32]{1,2,0:T(8,128)S(1)} %multiply_add_fusion.1), channel_id=1, source_target_pairs={{8,0},{16,8},{24,16},{9,1},{17,9},{25,17},{10,2},{18,10},{26,18},{... | collective-permute-start | bytes 233480 | tf_op jit(solution)/shard_map/ppermute | solution.py:54
  507.7 4.1 collective-permute-start.34
  507.7 4.1 collective-permute-start.35
  513.4 9.8 %collective-permute-start.36 = (f32[19,32,20]{1,2,0:T(8,128)S(1)}, f32[19,32,20]{1,2,0:T(8,128)S(1)}, u32[]{:S(2)}, u32[]{:S(2)}) collective-permute-start(f32[19,32,20]{1,2,0:T(8,128)S(1)} %multiply_add_fusion.4), channel_id=1, source_target_pairs={{0,8},{8,16},{16,24},{1,9},{9,17},{17,25},{2,10},{10,18},{18,26},{... | collective-permute-start | bytes 145928 | tf_op jit(solution)/shard_map/ppermute | solution.py:54
  523.2 3.1 collective-permute-start.38
  524.7 4.0 collective-permute-start.37
  535.6 4.0 collective-permute-start.39
  535.7 4.0 collective-permute-start.40
  552.6 90.1 %collective-permute-start.41 = (f32[19,32,32]{1,2,0:T(8,128)S(1)}, f32[19,32,32]{1,2,0:T(8,128)S(1)}, u32[]{:S(2)}, u32[]{:S(2)}) collective-permute-start(f32[19,32,32]{1,2,0:T(8,128)S(1)} %multiply_add_fusion), channel_id=1, source_target_pairs={{8,0},{16,8},{24,16},{9,1},{17,9},{25,17},{10,2},{18,10},{26,18},{... | collective-permute-start | bytes 233480 | tf_op jit(solution)/shard_map/ppermute | solution.py:54
  655.8 7.5 collective-permute-start.42
  677.6 88.6 %collective-permute-start.43 = (f32[19,8,128]{2,1,0:T(8,128)S(1)}, f32[19,8,128]{2,1,0:T(8,128)S(1)}, u32[]{:S(2)}, u32[]{:S(2)}) collective-permute-start(f32[19,8,128]{2,1,0:T(8,128)S(1)} %multiply_add_fusion.12), channel_id=1, source_target_pairs={{8,0},{16,8},{24,16},{9,1},{17,9},{25,17},{10,2},{18,10},{26,18},{... | collective-permute-start | bytes 233480 | tf_op jit(solution)/shard_map/ppermute | solution.py:54
  (6 other events, 12.3 us)
where the time goes:
time: 787 us; the launch traced here: 774 us
  waiting for transfers between devices  380 us (48%)
  starting transfers between devices  187 us (24%)
  local copies, waits for them, and re-layouts  132 us (17%)
  other arithmetic  64.6 us (8%)
    ppermute x14, waiting for transfers between devices, passed_along(): lax.ppermute(value, axis, [(source, source + steps) for source in range(f...  355 us
    ppermute x14, starting transfers between devices, passed_along(): lax.ppermute(value, axis, [(source, source + steps) for source in range(f...  154 us
    reduce_sum x7, other arithmetic, restrict_packet(): averaged = grid_view.sum(axis=(2, 4, 6)) / 8.0  35 us
    ppermute x15, starting transfers between devices, padded(): lax.ppermute(lax.slice_in_dim(block, 0, width, axis=dim), axis, backward)  29.8 us
    cond x14, local copies, waits for them, and re-layouts, level_run(): passed = lax.cond(my_level == level_id, advance, lambda: collided)  28.5 us
    ppermute x15, waiting for transfers between devices, padded(): lax.ppermute(lax.slice_in_dim(block, block.shape[dim] - width, None, axis...  25.2 us
    concatenate x15, other arithmetic, padded(): block = jnp.concatenate([low, block, high], axis=dim)  21.2 us
  transfers between devices with their start and end apart: 44, of which 29 were waited for; matrix products, arithmetic and copies ran while one was open for 2% of the time, Pallas kernels for 0%

commit v1 on v0

v1 whole, which is shorter than its diff:
```python
import jax
import jax.numpy as jnp
import numpy as np
from jax import lax
from jax.experimental import pallas as pl
from jax.experimental.pallas import tpu as pltpu
from jax.sharding import PartitionSpec as P

NY = 32
NZ = 32
LEVELS = 4
SLAB = 8
LANES = 128
VELOCITY = (
    (0, 0, 0),
    (1, 0, 0),
    (-1, 0, 0),
    (0, 1, 0),
    (0, -1, 0),
    (0, 0, 1),
    (0, 0, -1),
    (1, 1, 0),
    (-1, -1, 0),
    (1, -1, 0),
    (-1, 1, 0),
    (1, 0, 1),
    (-1, 0, -1),
    (1, 0, -1),
    (-1, 0, 1),
    (0, 1, 1),
    (0, -1, -1),
    (0, 1, -1),
    (0, -1, 1),
)
OPPOSITE = (0, 2, 1, 4, 3, 6, 5, 8, 7, 10, 9, 12, 11, 14, 13, 16, 15, 18, 17)
TAU_BASE = 1.0
F32 = jnp.float32
BF16 = jnp.bfloat16

PAD = 8
MARGIN = (8, 8, 8, 16)
FACTOR = (1, 2, 4, 8)
CHUNKS = (8, 4, 2, 1)
DEPTH = (32, 16, 8, 4)
OWN = tuple(SLAB * f for f in FACTOR)
ROW0 = tuple(PAD + m for m in MARGIN)
ROWS = tuple(OWN[l] + 2 * ROW0[l] for l in range(LEVELS))

Y_LOW = NY // 4
Y_HIGH = 3 * NY // 4 - 1


def zone_lane(level, y, z):
    if level == 0:
        return (y - 8) * 8 + z
    if level == 1:
        return z * 20 + y - 6
    return z * 25 + y - 4


ZONE_CELLS = (
    [(y, z) for y in range(8, 24) for z in range(8)],
    [(y, z) for y in range(6, 26) for z in range(6)],
    [(y, z) for y in range(5, 27) for z in range(5)],
)
ZONE_PITCH = (None, 20, 25)


def level_lane(level, y, z):
    return y * DEPTH[level] + z


def one_hot(pairs, inputs, outputs, weight=1.0):
    m = np.zeros((inputs, outputs), np.float32)
    for i, o in pairs:
        m[i, o] = weight
    return m


def pack_matrix(level):
    return one_hot(
        [(level_lane(level, y, z), zone_lane(level, y, z)) for y, z in ZONE_CELLS[level]],
        CHUNKS[level] * LANES,
        LANES,
    )


def interface_matrix(child):
    nz = DEPTH[child]
    pairs = [
        (zone_lane(child - 1, 8 + y // 2, z // 2), level_lane(child, y, z))
        for y in range(NY)
        for z in range(nz)
        if y in (0, NY - 1) or z == nz - 1
    ]
    return one_hot(pairs, LANES, CHUNKS[child] * LANES)


def restrict_matrix(child):
    pairs = [
        (level_lane(child, y, z), zone_lane(child - 1, 8 + y // 2, z // 2))
        for y in range(NY)
        for z in range(DEPTH[child])
    ]
    return one_hot(pairs, CHUNKS[child] * LANES, LANES, 0.125)


def compact_matrix():
    m = np.zeros((4, LANES, LANES), np.float32)
    for i in range(4):
        for y in range(NY):
            for z in range(4):
                m[i, level_lane(3, y, z), 32 * i + (y // 2) * 2 + z // 2] = 0.125
    return m


def spread_matrix():
    m = np.zeros((LANES, 4, 2 * LANES), np.float32)
    for i in range(4):
        for y in range(16):
            for z in range(2):
                m[32 * i + y * 2 + z, i, level_lane(2, 8 + y, z)] = 1.0
    return m.reshape(LANES, 4 * 2 * LANES)


Z_OUT = (5, 11, 14, 15, 18)
Y_DOWN = (4, 8, 9, 16, 18)
Y_UP = (3, 7, 10, 15, 17)
FLOW_DIRECTIONS = tuple(sorted(set(Z_OUT + Y_DOWN + Y_UP)))


def flow_cells(q):
    cells = {}
    if q in Z_OUT:
        for y in range(8, 24):
            cells[(y, 1)] = 16 * Z_OUT.index(q) + y - 8
    for group, y, first in ((Y_DOWN, 8, 80), (Y_UP, 23, 85)):
        if q in group:
            for z in range(2):
                cells.setdefault((y, z), first + group.index(q) + 25 * z)
    return cells


def flow_matrix():
    m = np.zeros((LANES, len(FLOW_DIRECTIONS), 2 * LANES), np.float32)
    for k, q in enumerate(FLOW_DIRECTIONS):
        for (y, z), lane in flow_cells(q).items():
            m[lane, k, level_lane(2, y, z)] = 1.0
    return m.reshape(LANES, -1)


def spread_zone_matrix():
    pairs = [
        (zone_lane(1, y, z), level_lane(1, y, z)) for y in range(7, 25) for z in range(5)
    ]
    return one_hot(pairs, LANES, 4 * LANES)


def relaxation(level_id):
    return 2.0**level_id * (TAU_BASE - 0.5) + 0.5


def parent_scale(child):
    return relaxation(child) / (2.0 * relaxation(child - 1))


def child_scale(child):
    return 2.0 * relaxation(child - 1) / relaxation(child)


def relax(v, a, b):
    s = [None] + [v[2 * k - 1] + v[2 * k] for k in range(1, 10)]
    d = [None] + [v[2 * k - 1] - v[2 * k] for k in range(1, 10)]
    rho = (
        (1.0 / 3.0) * v[0]
        + (1.0 / 18.0) * (s[1] + s[2] + s[3])
        + (1.0 / 36.0) * ((s[4] + s[5]) + (s[6] + s[7]) + (s[8] + s[9]))
    )
    mx = (1.0 / 18.0) * d[1] + (1.0 / 36.0) * ((d[4] + d[5]) + (d[6] + d[7]))
    my = (1.0 / 18.0) * d[2] + (1.0 / 36.0) * ((d[4] - d[5]) + (d[8] + d[9]))
    mz = (1.0 / 18.0) * d[3] + (1.0 / 36.0) * ((d[6] - d[7]) + (d[8] - d[9]))
    inv = 1.0 / rho
    ux, uy, uz = mx * inv, my * inv, mz * inv
    ra = a * rho
    base = ra - (1.5 * ra) * (ux * ux + uy * uy + uz * uz)
    r45 = 4.5 * ra
    ra3 = 3.0 * ra

    def kept(q):
        return v[q] if b == 1.0 else b * v[q]

    out = [base if b == 0.0 else base + kept(0)]
    cus = (ux, uy, uz, ux + uy, ux - uy, ux + uz, ux - uz, uy + uz, uy - uz)
    for k in range(1, 10):
        cu = cus[k - 1]
        even = base + r45 * (cu * cu)
        odd = ra3 * cu
        plus, minus = even + odd, even - odd
        if b != 0.0:
            plus, minus = plus + kept(2 * k - 1), minus + kept(2 * k)
        out += [plus, minus]
    return out


def collided(v, solid, level):
    inv_tau = 1.0 / relaxation(level)
    relaxed = relax(v, inv_tau, 1.0 - inv_tau)
    flag = solid != 0.0
    return [jnp.where(flag, v[OPPOSITE[q]], relaxed[q]) for q in range(19)]


def lanes():
    return lax.broadcasted_iota(jnp.int32, (8, LANES), 1)


def interface_mask(level, c):
    lane = lanes()
    nz = DEPTH[level]
    mask = (lane & (nz - 1)) == nz - 1
    if c == 0:
        mask = mask | (lane < nz)
    if c == CHUNKS[level] - 1:
        mask = mask | (lane >= LANES - nz)
    return mask


def pulled(post, level, row, c):
    lane = lanes()
    nz, count = DEPTH[level], CHUNKS[level]
    out = []
    for q in range(19):
        cx, cy, cz = VELOCITY[q]
        shift = cy * nz + cz
        value = post[q, c, pl.ds(row - cx, 8), :]
        if shift != 0:
            value = pltpu.roll(value, shift % LANES, 1)
            outside = None
            if cy == 1:
                if c > 0:
                    other = pltpu.roll(post[q, c - 1, pl.ds(row - cx, 8), :], shift, 1)
                    value = jnp.where(lane < shift, other, value)
                else:
                    outside = lane < nz
            if cy == -1:
                if c < count - 1:
                    other = pltpu.roll(post[q, c + 1, pl.ds(row - cx, 8), :], shift % LANES, 1)
                    value = jnp.where(lane >= LANES + shift, other, value)
                else:
                    outside = lane >= LANES - nz
            if cz != 0:
                edge = (lane & (nz - 1)) == (0 if cz == 1 else nz - 1)
                outside = edge if outside is None else outside | edge
            if outside is not None:
                value = jnp.where(outside, post[OPPOSITE[q], c, pl.ds(row, 8), :], value)
        out.append(value)
    return out


def zone_pulled(post, level, row):
    lane = lanes()
    pitch = ZONE_PITCH[level]
    out = []
    for q in range(19):
        cx, cy, cz = VELOCITY[q]
        shift = cz * pitch + cy
        value = post[q, pl.ds(row - cx, 8), :]
        if shift != 0:
            value = pltpu.roll(value, shift % LANES, 1)
            if cz == 1:
                value = jnp.where(lane < pitch, post[OPPOSITE[q], pl.ds(row, 8), :], value)
        out.append(value)
    return out


def zone_masks(level, reach):
    lane = lanes()
    pitch, first = ZONE_PITCH[level], 6 if level == 1 else 4
    top = DEPTH[level] // 4 - 1
    inside = None
    rim = None
    for z in range(top + reach + 1):
        start = z * pitch - first
        row = (lane >= start + Y_LOW - reach) & (lane <= start + Y_HIGH + reach)
        inside = row if inside is None else inside | row
        if z < top:
            row = (lane == start + Y_LOW) | (lane == start + Y_HIGH)
        elif z == top:
            row = (lane >= start + Y_LOW) & (lane <= start + Y_HIGH)
        else:
            continue
        rim = row if rim is None else rim | row
    return inside, rim


def loop(count, body):
    def step(i, carry):
        body(i)
        return carry

    lax.fori_loop(0, count, step, 0)


def row_loop(start, count, body):
    loop(count, lambda i: body(pl.multiple_of(start + 8 * i, 8)))


def moved(value, matrix):
    high = value.astype(BF16)
    rest = value - high.astype(F32)
    mid = rest.astype(BF16)
    low = (rest - mid.astype(F32)).astype(BF16)

    def product(part):
        return jnp.dot(part, matrix, preferred_element_type=F32)

    return product(high) + (product(mid) + product(low))


def load_level(level, own, solid, low, high, buf):
    factor, count, row0 = FACTOR[level], CHUNKS[level], ROW0[level]
    n = OWN[level]

    def one(q, source):
        for j in range(8):
            buf[q, j % count, pl.ds(row0 + j // count, 8, stride=factor), :] = source(j)
        if low is not None:
            for c in range(count):
                rows = pl.ds(c, 2 * factor, stride=count) if count > 1 else pl.ds(0, 2 * factor)
                buf[q, c, pl.ds(row0 - 2 * factor, 2 * factor), :] = low[q, rows, :]
                buf[q, c, pl.ds(row0 + n, 2 * factor), :] = high[q, rows, :]

    loop(19, lambda q: one(q, lambda j: own[q, :, pl.ds(j * LANES, LANES)]))
    one(19, lambda j: solid[:, pl.ds(j * LANES, LANES)].astype(F32))


def store_level(level, buf, row0, out):
    factor, count = FACTOR[level], CHUNKS[level]

    def one(q):
        for j in range(8):
            out[q, :, pl.ds(j * LANES, LANES)] = buf[
                q, j % count, pl.ds(row0 + j // count, 8, stride=factor), :
            ]

    loop(19, one)


def collide_rows(level, source, solid, wide, dest, start, groups):
    masks = [interface_mask(level, c) for c in range(CHUNKS[level])]

    def body(row):
        for c in range(CHUNKS[level]):
            v = [source[q, c, pl.ds(row, 8), :] for q in range(19)]
            if wide is not None:
                v = [jnp.where(masks[c], wide[q, c, pl.ds(row, 8), :], v[q]) for q in range(19)]
            post = collided(v, solid[19, c, pl.ds(row, 8), :], level)
            for q in range(19):
                dest[q, c, pl.ds(row, 8), :] = post[q]

    row_loop(start, groups, body)


def pull_rows(level, post, dest, start, groups):
    def body(row):
        for c in range(CHUNKS[level]):
            v = pulled(post, level, row, c)
            for q in range(19):
                dest[q, c, pl.ds(row, 8), :] = v[q]

    row_loop(start, groups, body)


def load_zone(level, zone, zero_row, center, left, right):
    n = OWN[level]
    zone[...] = jnp.zeros(zone.shape, F32)
    for q in range(20):
        zone[q, pl.ds(zero_row - 1, n + 2), :] = center[pl.ds(q * 34, n + 2), :]
        zone[q, pl.ds(zero_row - 7, 8), :] += left[q]
        zone[q, pl.ds(zero_row + n - 1, 8), :] += right[q]


def convert_zone(level, zone, start, groups, rim, out):
    scale = parent_scale(level + 1)

    def body(i):
        row = pl.multiple_of(8 * i, 8)
        v = [zone[q, pl.ds(start + row, 8), :] for q in range(19)]
        v = relax(v, 1.0 - scale, scale)
        for q in range(19):
            out[q, pl.ds(row, 8), :] = v[q] if rim is None else jnp.where(rim, v[q], 0.0)

    loop(groups, body)


def widen(converted, matrix, child, skip, count, wide, spread, first):
    rows = converted.shape[1]
    value = moved(converted[...].reshape(19 * rows, LANES), matrix[...])
    for c in range(CHUNKS[child]):
        part = value[:, c * LANES : (c + 1) * LANES].reshape(19, rows, LANES)
        spread[...] = part
        for q in range(19):
            t = spread[q, pl.ds(skip, count), :]
            wide[q, c, pl.ds(first, count, stride=2), :] = t
            wide[q, c, pl.ds(first + 1, count, stride=2), :] = t


def start_kernel(own, solid, pack0, pack1, pack2, to_right, to_left, center, to_zone_right, to_zone_left):
    me = lax.axis_index("level")

    def halo(q, source):
        for j in range(8):
            to_left[q, pl.ds(j, 2, stride=8), :] = source(pl.ds(0, 2), j)
            to_right[q, pl.ds(j, 2, stride=8), :] = source(pl.ds(SLAB - 2, 2), j)

    loop(19, lambda q: halo(q, lambda rows, j: own[q, rows, pl.ds(j * LANES, LANES)]))
    halo(19, lambda rows, j: solid[rows, pl.ds(j * LANES, LANES)].astype(F32))

    for level, pack in enumerate((pack0, pack1, pack2)):

        def push(level=level, pack=pack):
            n, row0, count, rows = OWN[level], ROW0[level], CHUNKS[level], ROWS[level]

            def scoped(buf, post, packed):
                post[...] = jnp.zeros(post.shape, F32)
                buf[19] = jnp.zeros(buf.shape[1:], F32)
                load_level(level, own, solid, None, None, buf)
                collide_rows(level, buf, buf, None, post, row0, n // 8)
                pull_rows(level, post, buf, row0 - 8, n // 8 + 2)
                total = None
                for c in range(count):
                    part = buf[:, c, pl.ds(row0 - 8, n + 16), :].reshape(20 * (n + 16), LANES)
                    part = moved(part, pack[pl.ds(c * LANES, LANES), :])
                    total = part if total is None else total + part
                packed[...] = total.reshape(20, n + 16, LANES)
                for q in range(20):
                    center[pl.ds(q * 34, n + 2), :] = packed[q, pl.ds(7, n + 2), :]
                    to_zone_right[q] = packed[q, pl.ds(n + 1, 8), :]
                    to_zone_left[q] = packed[q, pl.ds(7, 8), :]

            pl.run_scoped(
                scoped,
                pltpu.VMEM((20, count, rows, LANES), F32),
                pltpu.VMEM((19, count, rows, LANES), F32),
                pltpu.VMEM((20, n + 16, LANES), F32),
            )

        pl.when(me == level)(push)


def pack_flows(post, start, out, first):
    lane = lanes()

    def body(i):
        row = pl.multiple_of(8 * i, 8)
        total = jnp.zeros((8, LANES), F32)
        for k, q in enumerate(Z_OUT):
            v = pltpu.roll(post[q, pl.ds(start + row, 8), :], (16 * k - zone_lane(2, 8, 1)) % LANES, 1)
            total = jnp.where((lane >= 16 * k) & (lane < 16 * k + 16), v, total)
        for group, y, base in ((Y_DOWN, 8, 80), (Y_UP, 23, 85)):
            for k, q in enumerate(group):
                lane0 = base + k
                v = pltpu.roll(post[q, pl.ds(start + row, 8), :], (lane0 - zone_lane(2, y, 0)) % LANES, 1)
                total = jnp.where((lane == lane0) | (lane == lane0 + 25), v, total)
        out[pl.ds(first + row, 8), :] = total

    loop(6, body)


def finest_role(own, solid, low, high, center, left, right, widen3, restrict3, compact, state, message):
    level, row0, n = 3, ROW0[3], OWN[3]

    def scoped(g, pa, pb, wide, zone, zpost, flat, spread):
        load_level(level, own, solid, low, high, g)
        load_zone(2, zone, 16, center, left, right)
        covered, rim = zone_masks(2, 0)
        mask = interface_mask(level, 0)

        def substep(v, row, dest):
            v = [jnp.where(mask, wide[q, 0, pl.ds(row, 8), :], v[q]) for q in range(19)]
            post = collided(v, g[19, 0, pl.ds(row, 8), :], level)
            for q in range(19):
                dest[q, 0, pl.ds(row, 8), :] = post[q]

        for cycle in range(4):
            if cycle > 0:

                def zone_collide(row):
                    v = [zone[q, pl.ds(row, 8), :] for q in range(19)]
                    post = collided(v, zone[19, pl.ds(row, 8), :], 2)
                    for q in range(19):
                        zpost[q, pl.ds(row, 8), :] = post[q]

                def zone_pull(row):
                    v = zone_pulled(zpost, 2, row)
                    for q in range(19):
                        zone[q, pl.ds(row, 8), :] = v[q]

                row_loop(8, 6, zone_collide)
                pack_flows(zpost, 8, message, 48 * (cycle - 1))
                row_loop(8, 6, zone_pull)
            convert_zone(2, zone, 8, 6, rim, flat)
            widen(flat, widen3, 3, 0, 48, wide, spread, PAD)
            first, groups = (PAD, 12) if cycle < 2 else (PAD + 8, 10)

            def step_one(row):
                substep([g[q, 0, pl.ds(row, 8), :] for q in range(19)], row, pa)

            def step_two(row):
                substep(pulled(pa, level, row, 0), row, pb)

            def step_out(row):
                v = pulled(pb, level, row, 0)
                for q in range(19):
                    g[q, 0, pl.ds(row, 8), :] = v[q]

            row_loop(first, groups, step_one)
            row_loop(first, groups, step_two)
            if cycle < 3:
                row_loop(first, groups, step_out)
                for q in range(19):
                    flat[q] = (
                        g[q, 0, pl.ds(PAD, 48, stride=2), :] + g[q, 0, pl.ds(PAD + 1, 48, stride=2), :]
                    )
                spread[...] = moved(flat[...].reshape(19 * 48, LANES), restrict3[...]).reshape(19, 48, LANES)
                scale = child_scale(3)

                def restrict(i):
                    row = pl.multiple_of(8 * i, 8)
                    v = relax([spread[q, pl.ds(row, 8), :] for q in range(19)], 1.0 - scale, scale)
                    for q in range(19):
                        old = zone[q, pl.ds(8 + row, 8), :]
                        zone[q, pl.ds(8 + row, 8), :] = jnp.where(covered, v[q], old)

                loop(6, restrict)
            else:
                row_loop(row0, n // 8, step_out)
                store_level(level, g, row0, state)
                for q in range(19):
                    flat[q, pl.ds(0, 32), :] = (
                        g[q, 0, pl.ds(row0, 32, stride=2), :] + g[q, 0, pl.ds(row0 + 1, 32, stride=2), :]
                    )
                flat[:, pl.ds(32, 8), :] = jnp.zeros((19, 8, LANES), F32)
                total = None
                for i in range(4):
                    part = jnp.concatenate(
                        [flat[q, pl.ds(8 * i, 8), :] for q in range(19)] + [jnp.zeros((8, LANES), F32)], axis=0
                    )
                    part = moved(part, compact[i])
                    total = part if total is None else total + part
                scale = child_scale(3)
                v = relax([total[8 * q : 8 * q + 8] for q in range(19)], 1.0 - scale, scale)
                for q in range(19):
                    message[pl.ds(144 + 8 * q, 8), :] = v[q]
                message[pl.ds(296, 8), :] = jnp.zeros((8, LANES), F32)

    rows = ROWS[3]
    pl.run_scoped(
        scoped,
        pltpu.VMEM((20, 1, rows, LANES), F32),
        pltpu.VMEM((19, 1, rows, LANES), F32),
        pltpu.VMEM((19, 1, rows, LANES), F32),
        pltpu.VMEM((19, 1, rows, LANES), F32),
        pltpu.VMEM((20, 64, LANES), F32),
        pltpu.VMEM((19, 64, LANES), F32),
        pltpu.VMEM((19, 48, LANES), F32),
        pltpu.VMEM((19, 48, LANES), F32),
    )


def restrict_pairs(level, g, first, count, skip, flat, matrix):
    flat[...] = jnp.zeros(flat.shape, F32)
    for q in range(19):
        for c in range(CHUNKS[level]):
            flat[q, c, pl.ds(skip, count), :] = (
                g[q, c, pl.ds(first, count, stride=2), :] + g[q, c, pl.ds(first + 1, count, stride=2), :]
            )
    rows = flat.shape[2]
    total = None
    for c in range(CHUNKS[level]):
        part = moved(flat[:, c].reshape(flat.shape[0] * rows, LANES), matrix[pl.ds(c * LANES, LANES), :])
        total = part if total is None else total + part
    return total.reshape(flat.shape[0], rows, LANES)


def second_role(own, solid, low, high, center, left, right, widen2, restrict2, keep_post, keep_wide, keep_zone):
    level, row0 = 2, ROW0[2]
    first = row0 - 8

    def scoped(g, wide, zone, zpost, conv, spread, flat):
        load_level(level, own, solid, low, high, g)
        load_zone(1, zone, 16, center, left, right)
        covered, rim = zone_masks(1, 0)
        keep_post[19] = g[19]
        convert_zone(1, zone, 8, 4, rim, conv)
        widen(conv, widen2, 2, 4, 24, wide, spread, first)
        collide_rows(level, g, g, wide, keep_post, first, 6)
        pull_rows(level, keep_post, g, first, 6)
        collide_rows(level, g, g, wide, keep_post, first, 6)
        pull_rows(level, keep_post, g, first, 6)
        spread[...] = restrict_pairs(level, g, first, 24, 4, flat, restrict2)
        scale = child_scale(2)

        def restrict(i):
            row = pl.multiple_of(8 * i, 8)
            v = relax([spread[q, pl.ds(row, 8), :] for q in range(19)], 1.0 - scale, scale)
            v = [jnp.where(covered, v[q], zone[q, pl.ds(8 + row, 8), :]) for q in range(19)]
            post = collided(v, zone[19, pl.ds(8 + row, 8), :], 1)
            for q in range(19):
                zpost[q, pl.ds(8 + row, 8), :] = post[q]

        loop(4, restrict)

        def zone_pull(row):
            v = zone_pulled(zpost, 1, row)
            for q in range(19):
                zone[q, pl.ds(row, 8), :] = v[q]

        row_loop(8, 4, zone_pull)
        convert_zone(1, zone, 8, 4, rim, conv)
        widen(conv, widen2, 2, 4, 24, keep_wide, spread, first)
        for q in range(19):
            keep_zone[q] = zone[q, pl.ds(16, 16), :]

    pl.run_scoped(
        scoped,
        pltpu.VMEM((20, 2, ROWS[2], LANES), F32),
        pltpu.VMEM((19, 2, ROWS[2], LANES), F32),
        pltpu.VMEM((20, 48, LANES), F32),
        pltpu.VMEM((19, 48, LANES), F32),
        pltpu.VMEM((19, 32, LANES), F32),
        pltpu.VMEM((19, 32, LANES), F32),
        pltpu.VMEM((19, 2, 32, LANES), F32),
    )


def first_role(own, solid, low, high, center, left, right, widen1, mean1, state, partial):
    level, row0, n = 1, ROW0[1], OWN[1]
    first = row0 - 8

    def scoped(g, post, wide, zone, conv, spread, flat):
        load_level(level, own, solid, low, high, g)
        load_zone(0, zone, 12, center, left, right)
        convert_zone(0, zone, 8, 2, None, conv)
        widen(conv, widen1, 1, 0, 16, wide, spread, first)
        collide_rows(level, g, g, wide, post, first, 4)
        pull_rows(level, post, g, first, 4)
        collide_rows(level, g, g, wide, post, first, 4)
        pull_rows(level, post, g, row0, n // 8)
        store_level(level, g, row0, state)
        total = None
        for c in range(CHUNKS[1]):
            part = moved(g[pl.ds(0, 19), c, pl.ds(row0, n), :].reshape(19 * n, LANES), mean1[pl.ds(c * LANES, LANES), :])
            total = part if total is None else total + part
        flat[...] = total.reshape(19, n, LANES)
        for q in range(19):
            partial[q] = flat[q, pl.ds(0, 8, stride=2), :] + flat[q, pl.ds(1, 8, stride=2), :]

    pl.run_scoped(
        scoped,
        pltpu.VMEM((20, 4, ROWS[1], LANES), F32),
        pltpu.VMEM((19, 4, ROWS[1], LANES), F32),
        pltpu.VMEM((19, 4, ROWS[1], LANES), F32),
        pltpu.VMEM((20, 32, LANES), F32),
        pltpu.VMEM((19, 16, LANES), F32),
        pltpu.VMEM((19, 16, LANES), F32),
        pltpu.VMEM((19, n, LANES), F32),
    )


def coarse_role(own, solid, low, high, state):
    level, row0 = 0, ROW0[0]

    def scoped(g, post):
        load_level(level, own, solid, low, high, g)
        collide_rows(level, g, g, None, post, row0 - 8, 3)
        pull_rows(level, post, g, row0, 1)
        store_level(level, g, row0, state)

    pl.run_scoped(
        scoped,
        pltpu.VMEM((20, 8, ROWS[0], LANES), F32),
        pltpu.VMEM((19, 8, ROWS[0], LANES), F32),
    )


def main_kernel(
    own, solid, low, high, center, left, right, widen1, widen2, widen3, restrict2, restrict3, compact, mean1,
    state, message, keep_post, keep_wide, keep_zone, partial,
):
    me = lax.axis_index("level")

    @pl.when(me == 3)
    def _():
        finest_role(own, solid, low, high, center, left, right, widen3, restrict3, compact, state, message)

    @pl.when(me == 2)
    def _():
        second_role(own, solid, low, high, center, left, right, widen2, restrict2, keep_post, keep_wide, keep_zone)

    @pl.when(me == 1)
    def _():
        first_role(own, solid, low, high, center, left, right, widen1, mean1, state, partial)

    @pl.when(me == 0)
    def _():
        coarse_role(own, solid, low, high, state)


def return_kernel(
    message, old_state, keep_post, keep_wide, keep_zone, partial, flows, spread2, restrict2, mean_zone,
    state, to_first, to_coarse,
):
    me = lax.axis_index("level")
    level, row0 = 2, ROW0[2]
    first = row0 - 8

    @pl.when(me == 2)
    def _():
        def scoped(g, post, override, back, flat, means, zone):
            total = moved(message[pl.ds(0, 144), :], flows[...])
            for k in range(len(FLOW_DIRECTIONS)):
                for c in range(2):
                    start = (2 * k + c) * LANES
                    override[k, c] = total[:, start : start + LANES]

            def overridden(c, row, cycle, v):
                lane = lanes() + c * LANES
                y, z = lane >> 3, lane & 7
                v = list(v)
                for k, q in enumerate(FLOW_DIRECTIONS):
                    mask = None
                    if q in Z_OUT:
                        mask = (z == 1) & (y >= Y_LOW) & (y <= Y_HIGH)
                    if q in Y_DOWN:
                        edge = (y == Y_LOW) & (z <= 1)
                        mask = edge if mask is None else mask | edge
                    if q in Y_UP:
                        edge = (y == Y_HIGH) & (z <= 1)
                        mask = edge if mask is None else mask | edge
                    v[q] = jnp.where(mask, override[k, c, pl.ds(48 * cycle + row - first, 8), :], v[q])
                return v

            masks = [interface_mask(level, c) for c in range(2)]

            def begin(row):
                for c in range(2):
                    v = overridden(c, row, 0, [keep_post[q, c, pl.ds(row, 8), :] for q in range(19)])
                    for q in range(19):
                        post[q, c, pl.ds(row, 8), :] = v[q]

            row_loop(first, 6, begin)
            for cycle in (1, 2):
                pull_rows(level, post, g, first, 6)

                def body(row, cycle=cycle):
                    for c in range(2):
                        v = [
                            jnp.where(masks[c], keep_wide[q, c, pl.ds(row, 8), :], g[q, c, pl.ds(row, 8), :])
                            for q in range(19)
                        ]
                        v = collided(v, keep_post[19, c, pl.ds(row, 8), :], level)
                        v = overridden(c, row, cycle, v)
                        for q in range(19):
                            post[q, c, pl.ds(row, 8), :] = v[q]

                row_loop(first, 6, body)
            pull_rows(level, post, g, row0, 4)
            total = moved(message[pl.ds(144, 160), :], spread2[...])
            for i in range(4):
                for c in range(2):
                    start = (2 * i + c) * LANES
                    back[i, c] = total[:, start : start + LANES].reshape(20, 8, LANES)
            for c in range(2):
                lane = lanes() + c * LANES
                y, z = lane >> 3, lane & 7
                covered = (y >= Y_LOW) & (y <= Y_HIGH) & (z <= 1)
                for i in range(4):
                    for q in range(19):
                        rows = pl.ds(row0 + 8 * i, 8)
                        g[q, c, rows, :] = jnp.where(covered, back[i, c, q], g[q, c, rows, :])
            store_level(level, g, row0, state)
            means[...] = restrict_pairs(level, g, row0, 16, 0, flat, restrict2)
            scale = child_scale(2)
            covered, _ = zone_masks(1, 0)
            near, _ = zone_masks(1, 1)
            for i in range(2):
                rows = pl.ds(8 * i, 8)
                v = relax([means[q, rows, :] for q in range(19)], 1.0 - scale, scale)
                for q in range(19):
                    value = jnp.where(covered, v[q], keep_zone[q, rows, :])
                    to_first[q, rows, :] = jnp.where(near, value, 0.0)
            zone[...] = moved(to_first[...].reshape(19 * 16, LANES), mean_zone[...]).reshape(19, 16, LANES)
            for q in range(19):
                to_coarse[q] = zone[q, pl.ds(0, 8, stride=2), :] + zone[q, pl.ds(1, 8, stride=2), :]

        pl.run_scoped(
            scoped,
            pltpu.VMEM((19, 2, ROWS[2], LANES), F32),
            pltpu.VMEM((19, 2, ROWS[2], LANES), F32),
            pltpu.VMEM((len(FLOW_DIRECTIONS), 2, 144, LANES), F32),
            pltpu.VMEM((4, 2, 20, 8, LANES), F32),
            pltpu.VMEM((19, 2, 16, LANES), F32),
            pltpu.VMEM((19, 16, LANES), F32),
            pltpu.VMEM((19, 16, LANES), F32),
        )

    @pl.when(me != 2)
    def _():
        state[...] = old_state[...]

    @pl.when(me == 1)
    def _():
        to_first[:, pl.ds(0, 8), :] = partial[...]


def finish_kernel(old_state, from_near, from_far, spread1, spread0, state):
    me = lax.axis_index("level")

    @pl.when(me >= 2)
    def _():
        state[...] = old_state[...]

    @pl.when(me == 1)
    def _():
        def scoped(wide):
            total = moved(from_near[...].reshape(19 * 16, LANES), spread1[...])
            for c in range(4):
                wide[:, c] = total[:, c * LANES : (c + 1) * LANES].reshape(19, 16, LANES)

            def one(q):
                for j in range(8):
                    c = j % 4
                    lane = lanes() + c * LANES
                    y, z = lane >> 4, lane & 15
                    near = (y >= Y_LOW - 1) & (y <= Y_HIGH + 1) & (z <= 4)
                    columns = pl.ds(j * LANES, LANES)
                    value = wide[q, c, pl.ds(j // 4, 8, stride=2), :]
                    state[q, :, columns] = jnp.where(near, value, old_state[q, :, columns])

            loop(19, one)

        pl.run_scoped(scoped, pltpu.VMEM((19, 4, 16, LANES), F32))

    @pl.when(me == 0)
    def _():
        def scoped(value):
            scale = child_scale(1)
            v = relax(
                [from_near[q, pl.ds(0, 8), :] + from_far[q] for q in range(19)], 1.0 - scale, scale
            )
            for q in range(19):
                value[q] = v[q]
            value[19] = jnp.zeros((8, LANES), F32)
            total = moved(value[...].reshape(160, LANES), spread0[...])
            for q in range(19):
                for j in range(8):
                    columns = pl.ds(j * LANES, LANES)
                    if j in (0, 1, 6, 7):
                        state[q, :, columns] = old_state[q, :, columns]
                    else:
                        covered = (lanes() & 31) < 8
                        part = total[8 * q : 8 * q + 8, j * LANES : (j + 1) * LANES]
                        state[q, :, columns] = jnp.where(covered, part, old_state[q, :, columns])

        pl.run_scoped(scoped, pltpu.VMEM((20, 8, LANES), F32))


def call(kernel, shapes, args):
    return pl.pallas_call(
        kernel,
        out_shape=[jax.ShapeDtypeStruct(s, F32) for s in shapes],
        in_specs=[pl.BlockSpec(memory_space=pltpu.VMEM)] * len(args),
        out_specs=[pl.BlockSpec(memory_space=pltpu.VMEM)] * len(shapes),
        compiler_params=pltpu.CompilerParams(vmem_limit_bytes=48 * 1024 * 1024),
    )(*args)


def weights(matrix):
    return jnp.asarray(matrix, BF16)


def shards(populations, solid):
    own, flags = populations[0], solid[0]
    if own.shape != (19, SLAB, NY * NZ):
        raise ValueError("unexpected slab")
    blocks = lax.axis_size("blocks")
    forward = [(i, (i + 1) % blocks) for i in range(blocks)]
    backward = [(i, (i - 1) % blocks) for i in range(blocks)]
    down = [(i, i + 1) for i in range(LEVELS - 1)]

    def diagonal(step):
        return [
            (level * blocks + b, (level + 1) * blocks + (b + step) % blocks)
            for level in range(LEVELS - 1)
            for b in range(blocks)
        ]

    both = ("level", "blocks")
    to_right, to_left, center, zone_right, zone_left = call(
        start_kernel,
        [(20, 16, LANES), (20, 16, LANES), (680, LANES), (20, 8, LANES), (20, 8, LANES)],
        [own, flags] + [weights(pack_matrix(level)) for level in range(3)],
    )
    center = lax.ppermute(center, "level", down)
    left = lax.ppermute(zone_right, both, diagonal(1))
    right = lax.ppermute(zone_left, both, diagonal(-1))
    low = lax.ppermute(to_right, "blocks", forward)
    high = lax.ppermute(to_left, "blocks", backward)

    mean1 = one_hot(
        [
            (level_lane(1, y, z), zone_lane(0, 8 + y // 2, z // 2))
            for y in range(NY)
            for z in range(16)
            if not (7 <= y <= 24 and z <= 4)
        ],
        4 * LANES,
        LANES,
        0.125,
    )
    mean_zone = one_hot(
        [
            (zone_lane(1, y, z), zone_lane(0, 8 + y // 2, z // 2))
            for y in range(7, 25)
            for z in range(5)
        ],
        LANES,
        LANES,
        0.125,
    )
    spread0 = one_hot(
        [(zone_lane(0, y, z), level_lane(0, y, z)) for y, z in ZONE_CELLS[0]], LANES, 8 * LANES
    )
    restrict2 = weights(restrict_matrix(2))
    state, message, keep_post, keep_wide, keep_zone, partial = call(
        main_kernel,
        [
            (19, SLAB, NY * NZ),
            (304, LANES),
            (20, 2, ROWS[2], LANES),
            (19, 2, ROWS[2], LANES),
            (19, 16, LANES),
            (19, 8, LANES),
        ],
        [own, flags, low, high, center, left, right]
        + [weights(interface_matrix(child)) for child in (1, 2, 3)]
        + [restrict2, weights(restrict_matrix(3)), weights(compact_matrix()), weights(mean1)],
    )
    message = lax.ppermute(message, "level", [(3, 2)])
    state, to_first, to_coarse = call(
        return_kernel,
        [(19, SLAB, NY * NZ), (19, 16, LANES), (19, 8, LANES)],
        [message, state, keep_post, keep_wide, keep_zone, partial]
        + [weights(flow_matrix()), weights(spread_matrix()), restrict2, weights(mean_zone)],
    )
    near = lax.ppermute(to_first, "level", [(2, 1), (1, 0)])
    far = lax.ppermute(to_coarse, "level", [(2, 0)])
    (state,) = call(
        finish_kernel,
        [(19, SLAB, NY * NZ)],
        [state, near, far, weights(spread_zone_matrix()), weights(spread0)],
    )
    return state[None]


def solution(mesh):
    in_specs = (P("level", None, "blocks", None), P("level", "blocks", None))
    out_specs = P("level", None, "blocks", None)
    return jax.shard_map(shards, mesh=mesh, in_specs=in_specs, out_specs=out_specs, check_vma=False)
```

time: 787 us -> 75.1 us (0.10); the launches traced: 774 us -> 74.4 us
  waiting for transfers between devices: 380 us -> 41.2 us
  starting transfers between devices: 187 us -> 17.5 us
  local copies, waits for them, and re-layouts: 132 us -> 10.5 us
  other arithmetic: 64.6 us -> 0 us
    ppermute x44 -> x8, waiting for transfers between devices: 380 us -> 41.2 us  [the longest x1 39.2 us: shards(): far = lax.ppermute(to_coarse, 'level', [(2, 0)])]
    ppermute x44 -> x8, starting transfers between devices: 187 us -> 17.5 us  [the longest x1 4.87 us: shards(): right = lax.ppermute(zone_left, both, diagonal(-1))]
    cond x52 -> x0, local copies, waits for them, and re-layouts: 59.9 us -> none  [the longest x14 28.5 us: level_run(): passed = lax.cond(my_level == level_id, advance, lambda: collided)]
    reduce_sum x7 -> x0, other arithmetic: 35 us -> none  [restrict_packet(): averaged = grid_view.sum(axis=(2, 4, 6)) / 8.0]
    concatenate x22 -> x0, other arithmetic: 22.9 us -> none  [the longest x15 21.2 us: padded(): block = jnp.concatenate([low, block, high], axis=dim)]
    slice x25 -> x0, local copies, waits for them, and re-layouts: 14.8 us -> none  [the longest x7 9.76 us: make_packet(): grid_view[:, :, ny_cells // 4:3 * ny_cells // 4, quarter - 1]]
    reshape x9 -> x0, local copies, waits for them, and re-layouts: 10.9 us -> none  [the longest x3 7.29 us: make_packet(): level_field.reshape(19, level_field.shape[1], ny_cells, parent_nz)]
    ppermute x18 -> x0, local copies, waits for them, and re-layouts: 10.7 us -> none  [the longest x9 8.15 us: padded(): lax.ppermute(lax.slice_in_dim(block, block.shape[dim] - width, None, axis...]
  transfers between devices with their start and end apart: 44 -> 8, of which waited for: 29 -> 3; matrix products, arithmetic and copies ran while one was open for 2% -> 0% of each run, Pallas kernels for 0% -> 0%
where the time goes in v1:
time: 75.1 us; the launch traced here: 74.4 us
  waiting for transfers between devices  41.2 us (55%)
  starting transfers between devices  17.5 us (23%)
  local copies, waits for them, and re-layouts  10.5 us (14%)
  Pallas kernels  5.03 us (7%)
    ppermute x1, waiting for transfers between devices, shards(): far = lax.ppermute(to_coarse, 'level', [(2, 0)])  39.2 us
    unnamed x34, local copies, waits for them, and re-layouts  10.5 us
    pallas_call x4, Pallas kernels, call(): pl.pallas_call(kernel, out_shape=[jax.ShapeDtypeStruct(s, F32) for s in s...  5.03 us
    ppermute x1, starting transfers between devices, shards(): right = lax.ppermute(zone_left, both, diagonal(-1))  4.87 us
    ppermute x1, starting transfers between devices, shards(): center = lax.ppermute(center, 'level', down)  4.65 us
    ppermute x1, starting transfers between devices, shards(): high = lax.ppermute(to_left, 'blocks', backward)  2.63 us
    ppermute x1, starting transfers between devices, shards(): left = lax.ppermute(zone_right, both, diagonal(1))  1.94 us
    ppermute x1, waiting for transfers between devices, shards(): right = lax.ppermute(zone_left, both, diagonal(-1))  1.86 us
  transfers between devices with their start and end apart: 8, of which 3 were waited for; matrix products, arithmetic and copies ran while one was open for 0% of the time, Pallas kernels for 0%

profile of v1, /device:TPU:0, one launch (start us, length us, event | category | flops | bytes accessed | tf_op | source)
XLA Modules:
  0.0 74.4 jit_solution(15747687614005364490)
XLA Ops:
  0.0 0.0 copy-start
  0.0 1.1 %copy-done = f32[1,19,8,1024]{3,2,1,0:T(8,128)S(1)} copy-done((f32[1,19,8,1024]{3,2,1,0:T(8,128)S(1)}, f32[1,19,8,1024]{3,2,1,0:T(8,128)}, u32[]{:S(2)}) %copy-start) | copy-done | bytes 622616
  1.1 0.0 copy-start.4
  1.1 0.9 %copy-done.4 = bf16[1024,128]{1,0:T(8,128)(2,1)S(1)} copy-done((bf16[1024,128]{1,0:T(8,128)(2,1)S(1)}, bf16[1024,128]{1,0:T(8,128)(2,1)}, u32[]{:S(2)}) %copy-start.4) | copy-done | bytes 262168
  2.0 0.0 copy-start.7
  2.0 0.8 %copy-done.7 = s32[1,8,1024]{2,1,0:T(8,128)S(1)} copy-done((s32[1,8,1024]{2,1,0:T(8,128)S(1)}, s32[1,8,1024]{2,1,0:T(8,128)}, u32[]{:S(2)}) %copy-start.7) | copy-done | bytes 32792
  2.8 0.9 %copy-done.11 = bf16[512,128]{1,0:T(8,128)(2,1)S(1)} copy-done((bf16[512,128]{1,0:T(8,128)(2,1)S(1)}, bf16[512,128]{1,0:T(8,128)(2,1)}, u32[]{:S(2)}) %copy-start.11) | copy-done | bytes 131096
  3.7 0.0 copy-start.13
  3.7 0.8 %copy-done.13 = bf16[256,128]{1,0:T(8,128)(2,1)S(1)} copy-done((bf16[256,128]{1,0:T(8,128)(2,1)S(1)}, bf16[256,128]{1,0:T(8,128)(2,1)}, u32[]{:S(2)}) %copy-start.13) | copy-done | bytes 65560
  4.5 0.0 copy-start.5
  4.5 0.0 copy-start.14
  4.5 2.6 %shard_map.163 = (f32[20,16,128]{2,1,0:T(8,128)S(1)}, f32[20,16,128]{2,1,0:T(8,128)S(1)}, f32[680,128]{1,0:T(8,128)S(1)}, f32[20,8,128]{2,1,0:T(8,128)S(1)}, f32[20,8,128]{2,1,0:T(8,128)S(1)}) custom-call(f32[19,8,1024]{2,1,0:T(8,128)S(1)} %bitcast.3, s32[8,1024]{1,0:T(8,128)S(1)} %bitcast.5, bf16[1024,128]{1,0:T(8,128)(2,1)S(1)} %copy-done.4, ...), custom_call_target="tpu_custom_call" | custom-call | tf_op jit(solution)/shard_map/pallas_call | solution.py:869
  7.1 0.0 copy-start.1
  7.1 4.6 %collective-permute-start.2 = (f32[680,128]{1,0:T(8,128)S(1)}, f32[680,128]{1,0:T(8,128)S(1)}, u32[]{:S(2)}, u32[]{:S(2)}) collective-permute-start(f32[680,128]{1,0:T(8,128)S(1)} %get-tuple-element.21), channel_id=1, source_target_pairs={{0,8},{8,16},{16,24},{1,9},{9,17},{17,25},{2,10},{10,18},{18,26},{... | collective-permute-start | bytes 1044488 | tf_op jit(solution)/shard_map/ppermute | solution.py:904
  11.8 0.1 collective-permute-start
  11.8 2.6 %collective-permute-start.1 = (f32[20,16,128]{2,1,0:T(8,128)S(1)}, f32[20,16,128]{2,1,0:T(8,128)S(1)}, u32[]{:S(2)}, u32[]{:S(2)}) collective-permute-start(f32[20,16,128]{2,1,0:T(8,128)S(1)} %get-tuple-element.20), channel_id=1, source_target_pairs={{0,7},{1,0},{2,1},{3,2},{4,3},{5,4},{6,5},{7,6},{8,15},{9,8},{10,9... | collective-permute-start | bytes 491528 | tf_op jit(solution)/shard_map/ppermute | solution.py:908
  14.5 1.9 %collective-permute-start.3 = (f32[20,8,128]{2,1,0:T(8,128)S(1)}, f32[20,8,128]{2,1,0:T(8,128)S(1)}, u32[]{:S(2)}, u32[]{:S(2)}) collective-permute-start(f32[20,8,128]{2,1,0:T(8,128)S(1)} %get-tuple-element.22), channel_id=1, source_target_pairs={{0,9},{1,10},{2,11},{3,12},{4,13},{5,14},{6,15},{7,8},{8,17},{9,18... | collective-permute-start | bytes 245768 | tf_op jit(solution)/shard_map/ppermute | solution.py:905
  16.4 4.9 %collective-permute-start.4 = (f32[20,8,128]{2,1,0:T(8,128)S(1)}, f32[20,8,128]{2,1,0:T(8,128)S(1)}, u32[]{:S(2)}, u32[]{:S(2)}) collective-permute-start(f32[20,8,128]{2,1,0:T(8,128)S(1)} %get-tuple-element.23), channel_id=1, source_target_pairs={{0,15},{1,8},{2,9},{3,10},{4,11},{5,12},{6,13},{7,14},{8,23},{9,16... | collective-permute-start | bytes 245768 | tf_op jit(solution)/shard_map/ppermute | solution.py:906
  21.3 0.2 collective-permute-done.3.left
  21.5 1.9 %collective-permute-done.4.right = f32[20,8,128]{2,1,0:T(8,128)S(1)} collective-permute-done((f32[20,8,128]{2,1,0:T(8,128)S(1)}, f32[20,8,128]{2,1,0:T(8,128)S(1)}, u32[]{:S(2)}, u32[]{:S(2)}) %collective-permute-start.4) | collective-permute-done | bytes 81952 | tf_op jit(solution)/shard_map/ppermute | solution.py:906
  23.3 0.0 collective-permute-done.low
  23.3 0.0 collective-permute-done.1.high
  23.3 0.0 collective-permute-done.2.center
  23.3 0.0 copy-start.2
  23.4 0.8 %copy-done.2 = bf16[256,128]{1,0:T(8,128)(2,1)S(1)} copy-done((bf16[256,128]{1,0:T(8,128)(2,1)S(1)}, bf16[256,128]{1,0:T(8,128)(2,1)}, u32[]{:S(2)}) %copy-start.2) | copy-done | bytes 65560
  24.2 0.0 copy-start.8
  24.2 0.9 %copy-done.8 = bf16[512,128]{1,0:T(8,128)(2,1)S(1)} copy-done((bf16[512,128]{1,0:T(8,128)(2,1)S(1)}, bf16[512,128]{1,0:T(8,128)(2,1)}, u32[]{:S(2)}) %copy-start.8) | copy-done | bytes 131096
  25.1 0.9 %copy-done.9 = bf16[4,128,128]{2,1,0:T(8,128)(2,1)S(1)} copy-done((bf16[4,128,128]{2,1,0:T(8,128)(2,1)S(1)}, bf16[4,128,128]{2,1,0:T(8,128)(2,1)}, u32[]{:S(2)}) %copy-start.9) | copy-done | bytes 131096
  26.0 0.9 %copy-done.10 = bf16[128,512]{1,0:T(8,128)(2,1)S(1)} copy-done((bf16[128,512]{1,0:T(8,128)(2,1)S(1)}, bf16[128,512]{1,0:T(8,128)(2,1)}, u32[]{:S(2)}) %copy-start.10) | copy-done | bytes 131096
  26.9 0.8 %copy-done.12 = bf16[128,256]{1,0:T(8,128)(2,1)S(1)} copy-done((bf16[128,256]{1,0:T(8,128)(2,1)S(1)}, bf16[128,256]{1,0:T(8,128)(2,1)}, u32[]{:S(2)}) %copy-start.12) | copy-done | bytes 65560
  27.7 0.8 %copy-done.15 = bf16[128,128]{1,0:T(8,128)(2,1)S(1)} copy-done((bf16[128,128]{1,0:T(8,128)(2,1)S(1)}, bf16[128,128]{1,0:T(8,128)(2,1)}, u32[]{:S(2)}) %copy-start.15) | copy-done | bytes 32792
  28.5 0.8 %copy-done.16 = bf16[128,128]{1,0:T(8,128)(2,1)S(1)} copy-done((bf16[128,128]{1,0:T(8,128)(2,1)S(1)}, bf16[128,128]{1,0:T(8,128)(2,1)}, u32[]{:S(2)}) %copy-start.16) | copy-done | bytes 32792
  29.3 1.2 %shard_map.164 = (f32[19,8,1024]{2,1,0:T(8,128)S(1)}, f32[304,128]{1,0:T(8,128)S(1)}, f32[20,2,64,128]{3,2,1,0:T(8,128)S(1)}, f32[19,2,64,128]{3,2,1,0:T(8,128)S...) custom-call(f32[19,8,1024]{2,1,0:T(8,128)S(1)} %bitcast.4, s32[8,1024]{1,0:T(8,128)S(1)} %bitcast.6, ...), custom_call_target="tpu_custom_call" | custom-call | tf_op jit(solution)/shard_map/pallas_call | solution.py:869
  30.5 0.7 collective-permute-start.5
  31.2 0.0 collective-permute-done.5.message
  31.2 0.0 copy-done.5
  31.2 0.0 copy-done.14
  31.2 0.0 copy-done.1
  31.2 0.0 copy-start.3
  31.2 0.0 copy-start.6
  31.3 0.1 shard_map.165
  31.3 1.4 %collective-permute-start.6 = (f32[19,16,128]{2,1,0:T(8,128)S(1)}, f32[19,16,128]{2,1,0:T(8,128)S(1)}, u32[]{:S(2)}, u32[]{:S(2)}) collective-permute-start(f32[19,16,128]{2,1,0:T(8,128)S(1)} %get-tuple-element.31), channel_id=1, source_target_pairs={{16,8},{8,0},{17,9},{9,1},{18,10},{10,2},{19,11},{11,3},{20,12},{1... | collective-permute-start | bytes 466952 | tf_op jit(solution)/shard_map/ppermute | solution.py:956
  32.8 1.3 %collective-permute-start.7 = (f32[19,8,128]{2,1,0:T(8,128)S(1)}, f32[19,8,128]{2,1,0:T(8,128)S(1)}, u32[]{:S(2)}, u32[]{:S(2)}) collective-permute-start(f32[19,8,128]{2,1,0:T(8,128)S(1)} %get-tuple-element.32), channel_id=1, source_target_pairs={{16,0},{17,1},{18,2},{19,3},{20,4},{21,5},{22,6},{23,7}} | collective-permute-start | bytes 233480 | tf_op jit(solution)/shard_map/ppermute | solution.py:957
  34.1 39.2 %collective-permute-done.7.from_far = f32[19,8,128]{2,1,0:T(8,128)S(1)} collective-permute-done((f32[19,8,128]{2,1,0:T(8,128)S(1)}, f32[19,8,128]{2,1,0:T(8,128)S(1)}, u32[]{:S(2)}, u32[]{:S(2)}) %collective-permute-start.7) | collective-permute-done | bytes 77856 | tf_op jit(solution)/shard_map/ppermute | solution.py:957
  73.3 0.0 collective-permute-done.6.from_near
  73.3 0.0 copy-done.3
  73.3 0.0 copy-done.6
  73.3 1.2 %shard_map.166 = f32[19,8,1024]{2,1,0:T(8,128)} custom-call(f32[19,8,1024]{2,1,0:T(8,128)S(1)} %get-tuple-element.30.old_state, f32[19,16,128]{2,1,0:T(8,128)S(1)} %collective-permute-done.6.from_near, f32[19,8,128]{2,1,0:T(8,128)S(1)} %collective-permute-done.7.from_far, bf16[128,512]{1,0:T(8,128)(2,1)S(1)} %copy-done.6, bf16[128,1024]{1,0:T(8,128)(2,1)S(1)} %copy-done.3), custom_call_target="tpu_custom_call" | custom-call | tf_op jit(solution)/shard_map/pallas_call | solution.py:869
  (6 shorter events, 0.0 us)
Async XLA Ops:
  0.0 1.1 %copy-start = (f32[1,19,8,1024]{3,2,1,0:T(8,128)S(1)}, f32[1,19,8,1024]{3,2,1,0:T(8,128)}, u32[]{:S(2)}) copy-start(f32[1,19,8,1024]{3,2,1,0:T(8,128)} %param.17) | copy-start | bytes 1867780
  1.1 0.9 %copy-start.4 = (bf16[1024,128]{1,0:T(8,128)(2,1)S(1)}, bf16[1024,128]{1,0:T(8,128)(2,1)}, u32[]{:S(2)}) copy-start(bf16[1024,128]{1,0:T(8,128)(2,1)} %constant.30.clone.pack0) | copy-start | bytes 786436
  2.0 0.8 %copy-start.7 = (s32[1,8,1024]{2,1,0:T(8,128)S(1)}, s32[1,8,1024]{2,1,0:T(8,128)}, u32[]{:S(2)}) copy-start(s32[1,8,1024]{2,1,0:T(8,128)} %param.18) | copy-start | bytes 98308
  2.8 0.9 %copy-start.11 = (bf16[512,128]{1,0:T(8,128)(2,1)S(1)}, bf16[512,128]{1,0:T(8,128)(2,1)}, u32[]{:S(2)}) copy-start(bf16[512,128]{1,0:T(8,128)(2,1)} %constant.31.clone.pack1) | copy-start | bytes 393220
  3.7 0.8 %copy-start.13 = (bf16[256,128]{1,0:T(8,128)(2,1)S(1)}, bf16[256,128]{1,0:T(8,128)(2,1)}, u32[]{:S(2)}) copy-start(bf16[256,128]{1,0:T(8,128)(2,1)} %constant.32.clone.pack2) | copy-start | bytes 196612
  4.5 26.7 %copy-start.5 = (bf16[128,1024]{1,0:T(8,128)(2,1)S(1)}, bf16[128,1024]{1,0:T(8,128)(2,1)}, u32[]{:S(2)}) copy-start(bf16[128,1024]{1,0:T(8,128)(2,1)} %constant.41.clone.spread2) | copy-start | bytes 786436
  4.5 26.7 %copy-start.14 = (bf16[128,128]{1,0:T(8,128)(2,1)S(1)}, bf16[128,128]{1,0:T(8,128)(2,1)}, u32[]{:S(2)}) copy-start(bf16[128,128]{1,0:T(8,128)(2,1)} %constant.42.clone.mean_zone) | copy-start | bytes 98308
  7.1 24.1 %copy-start.1 = (bf16[128,3328]{1,0:T(8,128)(2,1)S(1)}, bf16[128,3328]{1,0:T(8,128)(2,1)}, u32[]{:S(2)}) copy-start(bf16[128,3328]{1,0:T(8,128)(2,1)} %constant.40.clone.flows) | copy-start | bytes 2555908
  7.1 16.2 %collective-permute-start.2 = (f32[680,128]{1,0:T(8,128)S(1)}, f32[680,128]{1,0:T(8,128)S(1)}, u32[]{:S(2)}, u32[]{:S(2)}) collective-permute-start(f32[680,128]{1,0:T(8,128)S(1)} %get-tuple-element.21), channel_id=1, source_target_pairs={{0,8},{8,16},{16,24},{1,9},{9,17},{17,25},{2,10},{10,18},{18,26},{... | collective-permute-start | bytes 1044488 | tf_op jit(solution)/shard_map/ppermute | solution.py:904
  11.8 11.6 %collective-permute-start = (f32[20,16,128]{2,1,0:T(8,128)S(1)}, f32[20,16,128]{2,1,0:T(8,128)S(1)}, u32[]{:S(2)}, u32[]{:S(2)}) collective-permute-start(f32[20,16,128]{2,1,0:T(8,128)S(1)} %get-tuple-element.19), channel_id=1, source_target_pairs={{0,1},{1,2},{2,3},{3,4},{4,5},{5,6},{6,7},{7,0},{8,9},{9,10},{10,1... | collective-permute-start | bytes 491528 | tf_op jit(solution)/shard_map/ppermute | solution.py:907
  11.8 11.5 %collective-permute-start.1 = (f32[20,16,128]{2,1,0:T(8,128)S(1)}, f32[20,16,128]{2,1,0:T(8,128)S(1)}, u32[]{:S(2)}, u32[]{:S(2)}) collective-permute-start(f32[20,16,128]{2,1,0:T(8,128)S(1)} %get-tuple-element.20), channel_id=1, source_target_pairs={{0,7},{1,0},{2,1},{3,2},{4,3},{5,4},{6,5},{7,6},{8,15},{9,8},{10,9... | collective-permute-start | bytes 491528 | tf_op jit(solution)/shard_map/ppermute | solution.py:908
  14.5 7.0 %collective-permute-start.3 = (f32[20,8,128]{2,1,0:T(8,128)S(1)}, f32[20,8,128]{2,1,0:T(8,128)S(1)}, u32[]{:S(2)}, u32[]{:S(2)}) collective-permute-start(f32[20,8,128]{2,1,0:T(8,128)S(1)} %get-tuple-element.22), channel_id=1, source_target_pairs={{0,9},{1,10},{2,11},{3,12},{4,13},{5,14},{6,15},{7,8},{8,17},{9,18... | collective-permute-start | bytes 245768 | tf_op jit(solution)/shard_map/ppermute | solution.py:905
  16.4 6.9 %collective-permute-start.4 = (f32[20,8,128]{2,1,0:T(8,128)S(1)}, f32[20,8,128]{2,1,0:T(8,128)S(1)}, u32[]{:S(2)}, u32[]{:S(2)}) collective-permute-start(f32[20,8,128]{2,1,0:T(8,128)S(1)} %get-tuple-element.23), channel_id=1, source_target_pairs={{0,15},{1,8},{2,9},{3,10},{4,11},{5,12},{6,13},{7,14},{8,23},{9,16... | collective-permute-start | bytes 245768 | tf_op jit(solution)/shard_map/ppermute | solution.py:906
  23.3 0.8 %copy-start.2 = (bf16[256,128]{1,0:T(8,128)(2,1)S(1)}, bf16[256,128]{1,0:T(8,128)(2,1)}, u32[]{:S(2)}) copy-start(bf16[256,128]{1,0:T(8,128)(2,1)} %constant.33.clone.restrict2) | copy-start | bytes 196612
  24.2 0.9 %copy-start.8 = (bf16[512,128]{1,0:T(8,128)(2,1)S(1)}, bf16[512,128]{1,0:T(8,128)(2,1)}, u32[]{:S(2)}) copy-start(bf16[512,128]{1,0:T(8,128)(2,1)} %constant.39.clone.mean1) | copy-start | bytes 393220
  25.1 0.9 %copy-start.9 = (bf16[4,128,128]{2,1,0:T(8,128)(2,1)S(1)}, bf16[4,128,128]{2,1,0:T(8,128)(2,1)}, u32[]{:S(2)}) copy-start(bf16[4,128,128]{2,1,0:T(8,128)(2,1)} %constant.38.clone.compact) | copy-start | bytes 393220
  26.0 0.9 %copy-start.10 = (bf16[128,512]{1,0:T(8,128)(2,1)S(1)}, bf16[128,512]{1,0:T(8,128)(2,1)}, u32[]{:S(2)}) copy-start(bf16[128,512]{1,0:T(8,128)(2,1)} %constant.34.clone.widen1) | copy-start | bytes 393220
  26.9 0.8 %copy-start.12 = (bf16[128,256]{1,0:T(8,128)(2,1)S(1)}, bf16[128,256]{1,0:T(8,128)(2,1)}, u32[]{:S(2)}) copy-start(bf16[128,256]{1,0:T(8,128)(2,1)} %constant.35.clone.widen2) | copy-start | bytes 196612
  27.7 0.8 %copy-start.15 = (bf16[128,128]{1,0:T(8,128)(2,1)S(1)}, bf16[128,128]{1,0:T(8,128)(2,1)}, u32[]{:S(2)}) copy-start(bf16[128,128]{1,0:T(8,128)(2,1)} %constant.37.clone.restrict3) | copy-start | bytes 98308
  28.5 0.8 %copy-start.16 = (bf16[128,128]{1,0:T(8,128)(2,1)S(1)}, bf16[128,128]{1,0:T(8,128)(2,1)}, u32[]{:S(2)}) copy-start(bf16[128,128]{1,0:T(8,128)(2,1)} %constant.36.clone.widen3) | copy-start | bytes 98308
  30.5 0.7 collective-permute-start.5
  31.2 42.0 %copy-start.3 = (bf16[128,1024]{1,0:T(8,128)(2,1)S(1)}, bf16[128,1024]{1,0:T(8,128)(2,1)}, u32[]{:S(2)}) copy-start(bf16[128,1024]{1,0:T(8,128)(2,1)} %constant.44.clone.spread0) | copy-start | bytes 786436
  31.2 42.0 %copy-start.6 = (bf16[128,512]{1,0:T(8,128)(2,1)S(1)}, bf16[128,512]{1,0:T(8,128)(2,1)}, u32[]{:S(2)}) copy-start(bf16[128,512]{1,0:T(8,128)(2,1)} %constant.43.clone.spread1) | copy-start | bytes 393220
  31.3 41.9 %collective-permute-start.6 = (f32[19,16,128]{2,1,0:T(8,128)S(1)}, f32[19,16,128]{2,1,0:T(8,128)S(1)}, u32[]{:S(2)}, u32[]{:S(2)}) collective-permute-start(f32[19,16,128]{2,1,0:T(8,128)S(1)} %get-tuple-element.31), channel_id=1, source_target_pairs={{16,8},{8,0},{17,9},{9,1},{18,10},{10,2},{19,11},{11,3},{20,12},{1... | collective-permute-start | bytes 466952 | tf_op jit(solution)/shard_map/ppermute | solution.py:956
  32.8 40.5 %collective-permute-start.7 = (f32[19,8,128]{2,1,0:T(8,128)S(1)}, f32[19,8,128]{2,1,0:T(8,128)S(1)}, u32[]{:S(2)}, u32[]{:S(2)}) collective-permute-start(f32[19,8,128]{2,1,0:T(8,128)S(1)} %get-tuple-element.32), channel_id=1, source_target_pairs={{16,0},{17,1},{18,2},{19,3},{20,4},{21,5},{22,6},{23,7}} | collective-permute-start | bytes 233480 | tf_op jit(solution)/shard_map/ppermute | solution.py:957

commit v2 on v1

--- a/solution.py
+++ b/solution.py
@@ -1,6 +1,5 @@
 import jax
 import jax.numpy as jnp
-import numpy as np
 from jax import lax
 from jax.experimental import pallas as pl
 from jax.experimental.pallas import tpu as pltpu
@@ -70,57 +69,96 @@
     return y * DEPTH[level] + z
 
 
-def one_hot(pairs, inputs, outputs, weight=1.0):
-    m = np.zeros((inputs, outputs), np.float32)
-    for i, o in pairs:
-        m[i, o] = weight
-    return m
-
-
-def pack_matrix(level):
-    return one_hot(
-        [(level_lane(level, y, z), zone_lane(level, y, z)) for y, z in ZONE_CELLS[level]],
-        CHUNKS[level] * LANES,
-        LANES,
-    )
-
-
-def interface_matrix(child):
-    nz = DEPTH[child]
-    pairs = [
-        (zone_lane(child - 1, 8 + y // 2, z // 2), level_lane(child, y, z))
-        for y in range(NY)
-        for z in range(nz)
-        if y in (0, NY - 1) or z == nz - 1
-    ]
-    return one_hot(pairs, LANES, CHUNKS[child] * LANES)
-
-
-def restrict_matrix(child):
-    pairs = [
-        (level_lane(child, y, z), zone_lane(child - 1, 8 + y // 2, z // 2))
-        for y in range(NY)
-        for z in range(DEPTH[child])
-    ]
-    return one_hot(pairs, CHUNKS[child] * LANES, LANES, 0.125)
-
-
-def compact_matrix():
-    m = np.zeros((4, LANES, LANES), np.float32)
-    for i in range(4):
-        for y in range(NY):
-            for z in range(4):
-                m[i, level_lane(3, y, z), 32 * i + (y // 2) * 2 + z // 2] = 0.125
-    return m
-
-
-def spread_matrix():
-    m = np.zeros((LANES, 4, 2 * LANES), np.float32)
-    for i in range(4):
-        for y in range(16):
-            for z in range(2):
-                m[32 * i + y * 2 + z, i, level_lane(2, 8 + y, z)] = 1.0
-    return m.reshape(LANES, 4 * 2 * LANES)
+def made(columns, weight, holds):
+    row = lax.broadcasted_iota(jnp.int32, (LANES, columns), 0)
+    column = lax.broadcasted_iota(jnp.int32, (LANES, columns), 1)
+    matrix = jnp.where(holds(row, column), weight, 0.0).astype(BF16)
+    return jnp.concatenate([matrix, matrix], axis=0)
+
+
+def cell_of(level, lane):
+    return lane >> (DEPTH[level].bit_length() - 1), lane & (DEPTH[level] - 1)
+
+
+def pack_chunk(level, c):
+    ys, zs = zip(*ZONE_CELLS[level])
+
+    def holds(row, column):
+        y, z = cell_of(level, row + c * LANES)
+        inside = (y >= min(ys)) & (y <= max(ys)) & (z <= max(zs))
+        return inside & (column == zone_lane(level, y, z))
+
+    return made(LANES, 1.0, holds)
+
+
+def widen_matrix(child):
+    def holds(row, column):
+        y, z = cell_of(child, column)
+        edge = (y == 0) | (y == NY - 1) | (z == DEPTH[child] - 1)
+        return edge & (row == zone_lane(child - 1, 8 + (y >> 1), z >> 1))
+
+    return made(CHUNKS[child] * LANES, 1.0, holds)
+
+
+def restrict_chunk(child, c):
+    def holds(row, column):
+        y, z = cell_of(child, row + c * LANES)
+        return column == zone_lane(child - 1, 8 + (y >> 1), z >> 1)
+
+    return made(LANES, 0.125, holds)
+
+
+def compact_chunk(i):
+    def holds(row, column):
+        y, z = cell_of(3, row)
+        return column == 32 * i + (y >> 1) * 2 + (z >> 1)
+
+    return made(LANES, 0.125, holds)
+
+
+def spread_chunk(i):
+    def holds(row, column):
+        y, z = cell_of(2, column)
+        return (y >= Y_LOW) & (y <= Y_HIGH) & (z <= 1) & (row == 32 * i + (y - Y_LOW) * 2 + z)
+
+    return made(2 * LANES, 1.0, holds)
+
+
+def near_first(y, z):
+    return (y >= Y_LOW - 1) & (y <= Y_HIGH + 1) & (z <= 4)
+
+
+def mean_chunk(c):
+    def holds(row, column):
+        y, z = cell_of(1, row + c * LANES)
+        return jnp.logical_not(near_first(y, z)) & (column == zone_lane(0, 8 + (y >> 1), z >> 1))
+
+    return made(LANES, 0.125, holds)
+
+
+def mean_zone_matrix():
+    def holds(row, column):
+        z = sum((row >= 20 * k).astype(jnp.int32) for k in range(1, 6))
+        y = row - 20 * z + 6
+        return near_first(y, z) & (column == zone_lane(0, 8 + (y >> 1), z >> 1))
+
+    return made(LANES, 0.125, holds)
+
+
+def spread_zone_matrix():
+    def holds(row, column):
+        y, z = cell_of(1, column)
+        return near_first(y, z) & (row == zone_lane(1, y, z))
+
+    return made(4 * LANES, 1.0, holds)
+
+
+def spread_covered_matrix():
+    def holds(row, column):
+        y, z = cell_of(0, column + 2 * LANES)
+        return (z < 8) & (row == zone_lane(0, y, z))
+
+    return made(4 * LANES, 1.0, holds)
 
 
 Z_OUT = (5, 11, 14, 15, 18)
@@ -129,31 +167,31 @@
 FLOW_DIRECTIONS = tuple(sorted(set(Z_OUT + Y_DOWN + Y_UP)))
 
 
-def flow_cells(q):
-    cells = {}
+def flow_mask(q, y, z):
+    mask = None
     if q in Z_OUT:
-        for y in range(8, 24):
-            cells[(y, 1)] = 16 * Z_OUT.index(q) + y - 8
-    for group, y, first in ((Y_DOWN, 8, 80), (Y_UP, 23, 85)):
+        mask = (z == 1) & (y >= Y_LOW) & (y <= Y_HIGH)
+    for group, edge in ((Y_DOWN, Y_LOW), (Y_UP, Y_HIGH)):
         if q in group:
-            for z in range(2):
-                cells.setdefault((y, z), first + group.index(q) + 25 * z)
-    return cells
-
-
-def flow_matrix():
-    m = np.zeros((LANES, len(FLOW_DIRECTIONS), 2 * LANES), np.float32)
-    for k, q in enumerate(FLOW_DIRECTIONS):
-        for (y, z), lane in flow_cells(q).items():
-            m[lane, k, level_lane(2, y, z)] = 1.0
-    return m.reshape(LANES, -1)
-
-
-def spread_zone_matrix():
-    pairs = [
-        (zone_lane(1, y, z), level_lane(1, y, z)) for y in range(7, 25) for z in range(5)
-    ]
-    return one_hot(pairs, LANES, 4 * LANES)
+            cells = (y == edge) & (z <= 1)
+            mask = cells if mask is None else mask | cells
+    return mask
+
+
+def flow_chunk(q):
+    def holds(row, column):
+        y, z = cell_of(2, column)
+        source = None
+        if q in Y_DOWN:
+            source = 80 + Y_DOWN.index(q) + 25 * z
+        if q in Y_UP:
+            source = 85 + Y_UP.index(q) + 25 * z
+        if q in Z_OUT:
+            over = 16 * Z_OUT.index(q) + y - Y_LOW
+            source = over if source is None else jnp.where(z == 1, over, source)
+        return flow_mask(q, y, z) & (row == source)
+
+    return made(2 * LANES, 1.0, holds)
 
 
 def relaxation(level_id):
@@ -292,12 +330,14 @@
     return inside, rim
 
 
-def loop(count, body):
+def loop(count, body, unroll=None):
     def step(i, carry):
         body(i)
         return carry
 
-    lax.fori_loop(0, count, step, 0)
+    if unroll is None:
+        unroll = max(u for u in range(1, 7) if count % u == 0)
+    lax.fori_loop(0, count, step, 0, unroll=unroll)
 
 
 def row_loop(start, count, body):
@@ -306,14 +346,8 @@
 
 def moved(value, matrix):
     high = value.astype(BF16)
-    rest = value - high.astype(F32)
-    mid = rest.astype(BF16)
-    low = (rest - mid.astype(F32)).astype(BF16)
-
-    def product(part):
-        return jnp.dot(part, matrix, preferred_element_type=F32)
-
-    return product(high) + (product(mid) + product(low))
+    low = (value - high.astype(F32)).astype(BF16)
+    return jnp.dot(jnp.concatenate([high, low], axis=1), matrix, preferred_element_type=F32)
 
 
 def load_level(level, own, solid, low, high, buf):
@@ -394,7 +428,7 @@
 
 def widen(converted, matrix, child, skip, count, wide, spread, first):
     rows = converted.shape[1]
-    value = moved(converted[...].reshape(19 * rows, LANES), matrix[...])
+    value = moved(converted[...].reshape(19 * rows, LANES), matrix)
     for c in range(CHUNKS[child]):
         part = value[:, c * LANES : (c + 1) * LANES].reshape(19, rows, LANES)
         spread[...] = part
@@ -404,7 +438,7 @@
             wide[q, c, pl.ds(first + 1, count, stride=2), :] = t
 
 
-def start_kernel(own, solid, pack0, pack1, pack2, to_right, to_left, center, to_zone_right, to_zone_left):
+def start_kernel(own, solid, to_right, to_left, center, to_zone_right, to_zone_left):
     me = lax.axis_index("level")
 
     def halo(q, source):
@@ -415,9 +449,9 @@
     loop(19, lambda q: halo(q, lambda rows, j: own[q, rows, pl.ds(j * LANES, LANES)]))
     halo(19, lambda rows, j: solid[rows, pl.ds(j * LANES, LANES)].astype(F32))
 
-    for level, pack in enumerate((pack0, pack1, pack2)):
-
-        def push(level=level, pack=pack):
+    for level in range(3):
+
+        def push(level=level):
             n, row0, count, rows = OWN[level], ROW0[level], CHUNKS[level], ROWS[level]
 
             def scoped(buf, post, packed):
@@ -429,7 +463,7 @@
                 total = None
                 for c in range(count):
                     part = buf[:, c, pl.ds(row0 - 8, n + 16), :].reshape(20 * (n + 16), LANES)
-                    part = moved(part, pack[pl.ds(c * LANES, LANES), :])
+                    part = moved(part, pack_chunk(level, c))
                     total = part if total is None else total + part
                 packed[...] = total.reshape(20, n + 16, LANES)
                 for q in range(20):
@@ -466,10 +500,12 @@
     loop(6, body)
 
 
-def finest_role(own, solid, low, high, center, left, right, widen3, restrict3, compact, state, message):
+def finest_role(own, solid, low, high, center, left, right, state, message):
     level, row0, n = 3, ROW0[3], OWN[3]
 
-    def scoped(g, pa, pb, wide, zone, zpost, flat, spread):
+    def scoped(g, pa, pb, wide, zone, zpost, flat, spread, widen3, restrict3):
+        widen3[...] = widen_matrix(3)
+        restrict3[...] = restrict_chunk(3, 0)
         load_level(level, own, solid, low, high, g)
         load_zone(2, zone, 16, center, left, right)
         covered, rim = zone_masks(2, 0)
@@ -499,7 +535,7 @@
                 pack_flows(zpost, 8, message, 48 * (cycle - 1))
                 row_loop(8, 6, zone_pull)
             convert_zone(2, zone, 8, 6, rim, flat)
-            widen(flat, widen3, 3, 0, 48, wide, spread, PAD)
+            widen(flat, widen3[...], 3, 0, 48, wide, spread, PAD)
             first, groups = (PAD, 12) if cycle < 2 else (PAD + 8, 10)
 
             def step_one(row):
@@ -545,7 +581,7 @@
                     part = jnp.concatenate(
                         [flat[q, pl.ds(8 * i, 8), :] for q in range(19)] + [jnp.zeros((8, LANES), F32)], axis=0
                     )
-                    part = moved(part, compact[i])
+                    part = moved(part, compact_chunk(i))
                     total = part if total is None else total + part
                 scale = child_scale(3)
                 v = relax([total[8 * q : 8 * q + 8] for q in range(19)], 1.0 - scale, scale)
@@ -564,10 +600,12 @@
         pltpu.VMEM((19, 64, LANES), F32),
         pltpu.VMEM((19, 48, LANES), F32),
         pltpu.VMEM((19, 48, LANES), F32),
+        pltpu.VMEM((2 * LANES, LANES), BF16),
+        pltpu.VMEM((2 * LANES, LANES), BF16),
     )
 
 
-def restrict_pairs(level, g, first, count, skip, flat, matrix):
+def restrict_pairs(level, g, first, count, skip, flat):
     flat[...] = jnp.zeros(flat.shape, F32)
     for q in range(19):
         for c in range(CHUNKS[level]):
@@ -577,12 +615,12 @@
     rows = flat.shape[2]
     total = None
     for c in range(CHUNKS[level]):
-        part = moved(flat[:, c].reshape(flat.shape[0] * rows, LANES), matrix[pl.ds(c * LANES, LANES), :])
+        part = moved(flat[:, c].reshape(flat.shape[0] * rows, LANES), restrict_chunk(level, c))
         total = part if total is None else total + part
     return total.reshape(flat.shape[0], rows, LANES)
 
 
-def second_role(own, solid, low, high, center, left, right, widen2, restrict2, keep_post, keep_wide, keep_zone):
+def second_role(own, solid, low, high, center, left, right, keep_post, keep_wide, keep_zone):
     level, row0 = 2, ROW0[2]
     first = row0 - 8
 
@@ -592,12 +630,12 @@
         covered, rim = zone_masks(1, 0)
         keep_post[19] = g[19]
         convert_zone(1, zone, 8, 4, rim, conv)
-        widen(conv, widen2, 2, 4, 24, wide, spread, first)
+        widen(conv, widen_matrix(2), 2, 4, 24, wide, spread, first)
         collide_rows(level, g, g, wide, keep_post, first, 6)
         pull_rows(level, keep_post, g, first, 6)
         collide_rows(level, g, g, wide, keep_post, first, 6)
         pull_rows(level, keep_post, g, first, 6)
-        spread[...] = restrict_pairs(level, g, first, 24, 4, flat, restrict2)
+        spread[...] = restrict_pairs(level, g, first, 24, 4, flat)
         scale = child_scale(2)
 
         def restrict(i):
@@ -617,7 +655,7 @@
 
         row_loop(8, 4, zone_pull)
         convert_zone(1, zone, 8, 4, rim, conv)
-        widen(conv, widen2, 2, 4, 24, keep_wide, spread, first)
+        widen(conv, widen_matrix(2), 2, 4, 24, keep_wide, spread, first)
         for q in range(19):
             keep_zone[q] = zone[q, pl.ds(16, 16), :]
 
@@ -633,7 +671,7 @@
     )
 
 
-def first_role(own, solid, low, high, center, left, right, widen1, mean1, state, partial):
+def first_role(own, solid, low, high, center, left, right, state, partial):
     level, row0, n = 1, ROW0[1], OWN[1]
     first = row0 - 8
 
@@ -641,7 +679,7 @@
         load_level(level, own, solid, low, high, g)
         load_zone(0, zone, 12, center, left, right)
         convert_zone(0, zone, 8, 2, None, conv)
-        widen(conv, widen1, 1, 0, 16, wide, spread, first)
+        widen(conv, widen_matrix(1), 1, 0, 16, wide, spread, first)
         collide_rows(level, g, g, wide, post, first, 4)
         pull_rows(level, post, g, first, 4)
         collide_rows(level, g, g, wide, post, first, 4)
@@ -649,7 +687,7 @@
         store_level(level, g, row0, state)
         total = None
         for c in range(CHUNKS[1]):
-            part = moved(g[pl.ds(0, 19), c, pl.ds(row0, n), :].reshape(19 * n, LANES), mean1[pl.ds(c * LANES, LANES), :])
+            part = moved(g[pl.ds(0, 19), c, pl.ds(row0, n), :].reshape(19 * n, LANES), mean_chunk(c))
             total = part if total is None else total + part
         flat[...] = total.reshape(19, n, LANES)
         for q in range(19):
@@ -684,22 +722,23 @@
 
 
 def main_kernel(
-    own, solid, low, high, center, left, right, widen1, widen2, widen3, restrict2, restrict3, compact, mean1,
+    own, solid, low, high, center, left, right,
     state, message, keep_post, keep_wide, keep_zone, partial,
 ):
     me = lax.axis_index("level")
+    arrived = (own, solid, low, high, center, left, right)
 
     @pl.when(me == 3)
     def _():
-        finest_role(own, solid, low, high, center, left, right, widen3, restrict3, compact, state, message)
+        finest_role(*arrived, state, message)
 
     @pl.when(me == 2)
     def _():
-        second_role(own, solid, low, high, center, left, right, widen2, restrict2, keep_post, keep_wide, keep_zone)
+        second_role(*arrived, keep_post, keep_wide, keep_zone)
 
     @pl.when(me == 1)
     def _():
-        first_role(own, solid, low, high, center, left, right, widen1, mean1, state, partial)
+        first_role(*arrived, state, partial)
 
     @pl.when(me == 0)
     def _():
@@ -707,7 +746,7 @@
 
 
 def return_kernel(
-    message, old_state, keep_post, keep_wide, keep_zone, partial, flows, spread2, restrict2, mean_zone,
+    message, keep_post, keep_wide, keep_zone, partial,
     state, to_first, to_coarse,
 ):
     me = lax.axis_index("level")
@@ -717,26 +756,18 @@
     @pl.when(me == 2)
     def _():
         def scoped(g, post, override, back, flat, means, zone):
-            total = moved(message[pl.ds(0, 144), :], flows[...])
-            for k in range(len(FLOW_DIRECTIONS)):
+            flows = message[pl.ds(0, 144), :]
+            for k, q in enumerate(FLOW_DIRECTIONS):
+                total = moved(flows, flow_chunk(q))
                 for c in range(2):
-                    start = (2 * k + c) * LANES
-                    override[k, c] = total[:, start : start + LANES]
+                    override[k, c] = total[:, c * LANES : (c + 1) * LANES]
 
             def overridden(c, row, cycle, v):
                 lane = lanes() + c * LANES
                 y, z = lane >> 3, lane & 7
                 v = list(v)
                 for k, q in enumerate(FLOW_DIRECTIONS):
-                    mask = None
-                    if q in Z_OUT:
-                        mask = (z == 1) & (y >= Y_LOW) & (y <= Y_HIGH)
-                    if q in Y_DOWN:
-                        edge = (y == Y_LOW) & (z <= 1)
-                        mask = edge if mask is None else mask | edge
-                    if q in Y_UP:
-                        edge = (y == Y_HIGH) & (z <= 1)
-                        mask = edge if mask is None else mask | edge
+                    mask = flow_mask(q, y, z)
                     v[q] = jnp.where(mask, override[k, c, pl.ds(48 * cycle + row - first, 8), :], v[q])
                 return v
 
@@ -765,11 +796,11 @@
 
                 row_loop(first, 6, body)
             pull_rows(level, post, g, row0, 4)
-            total = moved(message[pl.ds(144, 160), :], spread2[...])
+            means_back = message[pl.ds(144, 160), :]
             for i in range(4):
+                total = moved(means_back, spread_chunk(i))
                 for c in range(2):
-                    start = (2 * i + c) * LANES
-                    back[i, c] = total[:, start : start + LANES].reshape(20, 8, LANES)
+                    back[i, c] = total[:, c * LANES : (c + 1) * LANES].reshape(20, 8, LANES)
             for c in range(2):
                 lane = lanes() + c * LANES
                 y, z = lane >> 3, lane & 7
@@ -779,7 +810,7 @@
                         rows = pl.ds(row0 + 8 * i, 8)
                         g[q, c, rows, :] = jnp.where(covered, back[i, c, q], g[q, c, rows, :])
             store_level(level, g, row0, state)
-            means[...] = restrict_pairs(level, g, row0, 16, 0, flat, restrict2)
+            means[...] = restrict_pairs(level, g, row0, 16, 0, flat)
             scale = child_scale(2)
             covered, _ = zone_masks(1, 0)
             near, _ = zone_masks(1, 1)
@@ -789,7 +820,7 @@
                 for q in range(19):
                     value = jnp.where(covered, v[q], keep_zone[q, rows, :])
                     to_first[q, rows, :] = jnp.where(near, value, 0.0)
-            zone[...] = moved(to_first[...].reshape(19 * 16, LANES), mean_zone[...]).reshape(19, 16, LANES)
+            zone[...] = moved(to_first[...].reshape(19 * 16, LANES), mean_zone_matrix()).reshape(19, 16, LANES)
             for q in range(19):
                 to_coarse[q] = zone[q, pl.ds(0, 8, stride=2), :] + zone[q, pl.ds(1, 8, stride=2), :]
 
@@ -804,26 +835,26 @@
             pltpu.VMEM((19, 16, LANES), F32),
         )
 
-    @pl.when(me != 2)
-    def _():
-        state[...] = old_state[...]
-
     @pl.when(me == 1)
     def _():
         to_first[:, pl.ds(0, 8), :] = partial[...]
 
 
-def finish_kernel(old_state, from_near, from_far, spread1, spread0, state):
+def finish_kernel(old_state, second_state, from_near, from_far, state):
     me = lax.axis_index("level")
 
-    @pl.when(me >= 2)
+    @pl.when(me == 3)
     def _():
         state[...] = old_state[...]
+
+    @pl.when(me == 2)
+    def _():
+        state[...] = second_state[...]
 
     @pl.when(me == 1)
     def _():
         def scoped(wide):
-            total = moved(from_near[...].reshape(19 * 16, LANES), spread1[...])
+            total = moved(from_near[...].reshape(19 * 16, LANES), spread_zone_matrix())
             for c in range(4):
                 wide[:, c] = total[:, c * LANES : (c + 1) * LANES].reshape(19, 16, LANES)
 
@@ -851,15 +882,15 @@
             for q in range(19):
                 value[q] = v[q]
             value[19] = jnp.zeros((8, LANES), F32)
-            total = moved(value[...].reshape(160, LANES), spread0[...])
+            total = moved(value[...].reshape(160, LANES), spread_covered_matrix())
             for q in range(19):
                 for j in range(8):
                     columns = pl.ds(j * LANES, LANES)
-                    if j in (0, 1, 6, 7):
+                    if not 2 <= j < 6:
                         state[q, :, columns] = old_state[q, :, columns]
                     else:
                         covered = (lanes() & 31) < 8
-                        part = total[8 * q : 8 * q + 8, j * LANES : (j + 1) * LANES]
+                        part = total[8 * q : 8 * q + 8, (j - 2) * LANES : (j - 1) * LANES]
                         state[q, :, columns] = jnp.where(covered, part, old_state[q, :, columns])
 
         pl.run_scoped(scoped, pltpu.VMEM((20, 8, LANES), F32))
@@ -871,12 +902,8 @@
         out_shape=[jax.ShapeDtypeStruct(s, F32) for s in shapes],
         in_specs=[pl.BlockSpec(memory_space=pltpu.VMEM)] * len(args),
         out_specs=[pl.BlockSpec(memory_space=pltpu.VMEM)] * len(shapes),
-        compiler_params=pltpu.CompilerParams(vmem_limit_bytes=48 * 1024 * 1024),
+        compiler_params=pltpu.CompilerParams(vmem_limit_bytes=24 * 1024 * 1024),
     )(*args)
-
-
-def weights(matrix):
-    return jnp.asarray(matrix, BF16)
 
 
 def shards(populations, solid):
@@ -899,7 +926,7 @@
     to_right, to_left, center, zone_right, zone_left = call(
         start_kernel,
         [(20, 16, LANES), (20, 16, LANES), (680, LANES), (20, 8, LANES), (20, 8, LANES)],
-        [own, flags] + [weights(pack_matrix(level)) for level in range(3)],
+        [own, flags],
     )
     center = lax.ppermute(center, "level", down)
     left = lax.ppermute(zone_right, both, diagonal(1))
@@ -907,31 +934,6 @@
     low = lax.ppermute(to_right, "blocks", forward)
     high = lax.ppermute(to_left, "blocks", backward)
 
-    mean1 = one_hot(
-        [
-            (level_lane(1, y, z), zone_lane(0, 8 + y // 2, z // 2))
-            for y in range(NY)
-            for z in range(16)
-            if not (7 <= y <= 24 and z <= 4)
-        ],
-        4 * LANES,
-        LANES,
-        0.125,
-    )
-    mean_zone = one_hot(
-        [
-            (zone_lane(1, y, z), zone_lane(0, 8 + y // 2, z // 2))
-            for y in range(7, 25)
-            for z in range(5)
-        ],
-        LANES,
-        LANES,
-        0.125,
-    )
-    spread0 = one_hot(
-        [(zone_lane(0, y, z), level_lane(0, y, z)) for y, z in ZONE_CELLS[0]], LANES, 8 * LANES
-    )
-    restrict2 = weights(restrict_matrix(2))
     state, message, keep_post, keep_wide, keep_zone, partial = call(
         main_kernel,
         [
@@ -942,23 +944,20 @@
             (19, 16, LANES),
             (19, 8, LANES),
         ],
-        [own, flags, low, high, center, left, right]
-        + [weights(interface_matrix(child)) for child in (1, 2, 3)]
-        + [restrict2, weights(restrict_matrix(3)), weights(compact_matrix()), weights(mean1)],
+        [own, flags, low, high, center, left, right],
     )
     message = lax.ppermute(message, "level", [(3, 2)])
-    state, to_first, to_coarse = call(
+    second_state, to_first, to_coarse = call(
         return_kernel,
         [(19, SLAB, NY * NZ), (19, 16, LANES), (19, 8, LANES)],
-        [message, state, keep_post, keep_wide, keep_zone, partial]
-        + [weights(flow_matrix()), weights(spread_matrix()), restrict2, weights(mean_zone)],
+        [message, keep_post, keep_wide, keep_zone, partial],
     )
     near = lax.ppermute(to_first, "level", [(2, 1), (1, 0)])
     far = lax.ppermute(to_coarse, "level", [(2, 0)])
     (state,) = call(
         finish_kernel,
         [(19, SLAB, NY * NZ)],
-        [state, near, far, weights(spread_zone_matrix()), weights(spread0)],
+        [state, second_state, near, far],
     )
     return state[None]
 

time: 75.1 us -> 48.3 us (0.64)
  waiting for transfers between devices: 41.2 us -> 24.2 us
  local copies, waits for them, and re-layouts: 10.5 us -> 1.83 us
  Pallas kernels: 5.03 us -> 3.69 us
    ppermute x1, waiting for transfers between devices: 39.2 us -> 22.2 us  [shards(): far = lax.ppermute(to_coarse, 'level', [(2, 0)])]
    unnamed x34 -> x4, local copies, waits for them, and re-layouts: 10.5 us -> 1.83 us
    pallas_call x4, Pallas kernels: 5.03 us -> 3.69 us  [call(): pl.pallas_call(kernel, out_shape=[jax.ShapeDtypeStruct(s, F32) for s in s...]
  transfers between devices with their start and end apart: 8 -> 8, of which waited for: 3 -> 2; matrix products, arithmetic and copies ran while one was open for 0% -> 0% of each run, Pallas kernels for 0% -> 0%
where the time goes in v2:
time: 48.3 us; the launch traced here: 48 us
  waiting for transfers between devices  24.2 us (50%)
  starting transfers between devices  18.1 us (37%)
  Pallas kernels  3.69 us (8%)
  local copies, waits for them, and re-layouts  1.83 us (4%)
    ppermute x1, waiting for transfers between devices, shards(): far = lax.ppermute(to_coarse, 'level', [(2, 0)])  22.2 us
    ppermute x1, starting transfers between devices, shards(): right = lax.ppermute(zone_left, both, diagonal(-1))  5.48 us
    ppermute x1, starting transfers between devices, shards(): center = lax.ppermute(center, 'level', down)  4.74 us
    pallas_call x4, Pallas kernels, call(): pl.pallas_call(kernel, out_shape=[jax.ShapeDtypeStruct(s, F32) for s in s...  3.69 us
    ppermute x1, starting transfers between devices, shards(): high = lax.ppermute(to_left, 'blocks', backward)  2.63 us
    ppermute x1, waiting for transfers between devices, shards(): right = lax.ppermute(zone_left, both, diagonal(-1))  2.03 us
    ppermute x1, starting transfers between devices, shards(): left = lax.ppermute(zone_right, both, diagonal(1))  1.96 us
    unnamed x4, local copies, waits for them, and re-layouts  1.83 us
  transfers between devices with their start and end apart: 8, of which 2 were waited for; matrix products, arithmetic and copies ran while one was open for 0% of the time, Pallas kernels for 0%

profile of v2, /device:TPU:0, one launch (start us, length us, event | category | flops | bytes accessed | tf_op | source)
XLA Modules:
  0.0 48.0 jit_solution(9221477778228865775)
XLA Ops:
  0.0 0.0 copy-start
  0.0 1.1 %copy-done = f32[1,19,8,1024]{3,2,1,0:T(8,128)S(1)} copy-done((f32[1,19,8,1024]{3,2,1,0:T(8,128)S(1)}, f32[1,19,8,1024]{3,2,1,0:T(8,128)}, u32[]{:S(2)}) %copy-start) | copy-done | bytes 622616
  1.1 0.0 copy-start.1
  1.1 0.8 %copy-done.1 = s32[1,8,1024]{2,1,0:T(8,128)S(1)} copy-done((s32[1,8,1024]{2,1,0:T(8,128)S(1)}, s32[1,8,1024]{2,1,0:T(8,128)}, u32[]{:S(2)}) %copy-start.1) | copy-done | bytes 32792
  1.8 1.5 %shard_map.28 = (f32[20,16,128]{2,1,0:T(8,128)S(1)}, f32[20,16,128]{2,1,0:T(8,128)S(1)}, f32[680,128]{1,0:T(8,128)S(1)}, f32[20,8,128]{2,1,0:T(8,128)S(1)}, f32[20,8,128]{2,1,0:T(8,128)S(1)}) custom-call(f32[19,8,1024]{2,1,0:T(8,128)S(1)} %bitcast.3, s32[8,1024]{1,0:T(8,128)S(1)} %bitcast.5), custom_call_target="tpu_custom_call" | custom-call | tf_op jit(solution)/shard_map/pallas_call | solution.py:900
  3.3 4.7 %collective-permute-start.2 = (f32[680,128]{1,0:T(8,128)S(1)}, f32[680,128]{1,0:T(8,128)S(1)}, u32[]{:S(2)}, u32[]{:S(2)}) collective-permute-start(f32[680,128]{1,0:T(8,128)S(1)} %get-tuple-element.21), channel_id=1, source_target_pairs={{0,8},{8,16},{16,24},{1,9},{9,17},{17,25},{2,10},{10,18},{18,26},{... | collective-permute-start | bytes 1044488 | tf_op jit(solution)/shard_map/ppermute | solution.py:931
  8.1 0.1 collective-permute-start
  8.1 2.6 %collective-permute-start.1 = (f32[20,16,128]{2,1,0:T(8,128)S(1)}, f32[20,16,128]{2,1,0:T(8,128)S(1)}, u32[]{:S(2)}, u32[]{:S(2)}) collective-permute-start(f32[20,16,128]{2,1,0:T(8,128)S(1)} %get-tuple-element.20), channel_id=1, source_target_pairs={{0,7},{1,0},{2,1},{3,2},{4,3},{5,4},{6,5},{7,6},{8,15},{9,8},{10,9... | collective-permute-start | bytes 491528 | tf_op jit(solution)/shard_map/ppermute | solution.py:935
  10.8 2.0 %collective-permute-start.3 = (f32[20,8,128]{2,1,0:T(8,128)S(1)}, f32[20,8,128]{2,1,0:T(8,128)S(1)}, u32[]{:S(2)}, u32[]{:S(2)}) collective-permute-start(f32[20,8,128]{2,1,0:T(8,128)S(1)} %get-tuple-element.22), channel_id=1, source_target_pairs={{0,9},{1,10},{2,11},{3,12},{4,13},{5,14},{6,15},{7,8},{8,17},{9,18... | collective-permute-start | bytes 245768 | tf_op jit(solution)/shard_map/ppermute | solution.py:932
  12.7 5.5 %collective-permute-start.4 = (f32[20,8,128]{2,1,0:T(8,128)S(1)}, f32[20,8,128]{2,1,0:T(8,128)S(1)}, u32[]{:S(2)}, u32[]{:S(2)}) collective-permute-start(f32[20,8,128]{2,1,0:T(8,128)S(1)} %get-tuple-element.23), channel_id=1, source_target_pairs={{0,15},{1,8},{2,9},{3,10},{4,11},{5,12},{6,13},{7,14},{8,23},{9,16... | collective-permute-start | bytes 245768 | tf_op jit(solution)/shard_map/ppermute | solution.py:933
  18.2 0.0 collective-permute-done.3.left
  18.2 2.0 %collective-permute-done.4.right = f32[20,8,128]{2,1,0:T(8,128)S(1)} collective-permute-done((f32[20,8,128]{2,1,0:T(8,128)S(1)}, f32[20,8,128]{2,1,0:T(8,128)S(1)}, u32[]{:S(2)}, u32[]{:S(2)}) %collective-permute-start.4) | collective-permute-done | bytes 81952 | tf_op jit(solution)/shard_map/ppermute | solution.py:933
  20.3 0.0 collective-permute-done.low
  20.3 0.0 collective-permute-done.1.high
  20.3 0.0 collective-permute-done.2.center
  20.3 1.1 %shard_map.29 = (f32[19,8,1024]{2,1,0:T(8,128)S(1)}, f32[304,128]{1,0:T(8,128)S(1)}, f32[20,2,64,128]{3,2,1,0:T(8,128)S(1)}, f32[19,2,64,128]{3,2,1,0:T(8,128)S(...) custom-call(f32[19,8,1024]{2,1,0:T(8,128)S(1)} %bitcast.4, s32[8,1024]{1,0:T(8,128)S(1)} %bitcast.6, ...), custom_call_target="tpu_custom_call" | custom-call | tf_op jit(solution)/shard_map/pallas_call | solution.py:900
  21.4 0.7 %collective-permute-start.5 = (f32[304,128]{1,0:T(8,128)S(1)}, f32[304,128]{1,0:T(8,128)S(1)}, u32[]{:S(2)}, u32[]{:S(2)}) collective-permute-start(f32[304,128]{1,0:T(8,128)S(1)} %get-tuple-element.25), channel_id=1, source_target_pairs={{24,16},{25,17},{26,18},{27,19},{28,20},{29,21},{30,22},{31,23}} | collective-permute-start | bytes 466952 | tf_op jit(solution)/shard_map/ppermute | solution.py:949
  22.1 0.0 collective-permute-done.5.message
  22.1 1.3 %collective-permute-start.6 = (f32[19,16,128]{2,1,0:T(8,128)S(1)}, f32[19,16,128]{2,1,0:T(8,128)S(1)}, u32[]{:S(2)}, u32[]{:S(2)}) collective-permute-start(f32[19,16,128]{2,1,0:T(8,128)S(1)} %get-tuple-element.31), channel_id=1, source_target_pairs={{16,8},{8,0},{17,9},{9,1},{18,10},{10,2},{19,11},{11,3},{20,12},{1... | collective-permute-start | bytes 466952 | tf_op jit(solution)/shard_map/ppermute | solution.py:955
  23.4 1.3 %collective-permute-start.7 = (f32[19,8,128]{2,1,0:T(8,128)S(1)}, f32[19,8,128]{2,1,0:T(8,128)S(1)}, u32[]{:S(2)}, u32[]{:S(2)}) collective-permute-start(f32[19,8,128]{2,1,0:T(8,128)S(1)} %get-tuple-element.32), channel_id=1, source_target_pairs={{16,0},{17,1},{18,2},{19,3},{20,4},{21,5},{22,6},{23,7}} | collective-permute-start | bytes 233480 | tf_op jit(solution)/shard_map/ppermute | solution.py:956
  24.7 22.2 %collective-permute-done.7.from_far = f32[19,8,128]{2,1,0:T(8,128)S(1)} collective-permute-done((f32[19,8,128]{2,1,0:T(8,128)S(1)}, f32[19,8,128]{2,1,0:T(8,128)S(1)}, u32[]{:S(2)}, u32[]{:S(2)}) %collective-permute-start.7) | collective-permute-done | bytes 77856 | tf_op jit(solution)/shard_map/ppermute | solution.py:956
  46.9 0.0 collective-permute-done.6.from_near
  46.9 1.1 %shard_map.31 = f32[19,8,1024]{2,1,0:T(8,128)} custom-call(f32[19,8,1024]{2,1,0:T(8,128)S(1)} %get-tuple-element.24.old_state, f32[19,8,1024]{2,1,0:T(8,128)S(1)} %get-tuple-element.30.second_state, f32[19,16,128]{2,1,0:T(8,128)S(1)} %collective-permute-done.6.from_near, f32[19,8,128]{2,1,0:T(8,128)S(1)} %collective-permute-done.7.from_far), custom_call_target="tpu_custom_call" | custom-call | tf_op jit(solution)/shard_map/pallas_call | solution.py:900
  (1 shorter events, 0.0 us)
Async XLA Ops:
  0.0 1.1 %copy-start = (f32[1,19,8,1024]{3,2,1,0:T(8,128)S(1)}, f32[1,19,8,1024]{3,2,1,0:T(8,128)}, u32[]{:S(2)}) copy-start(f32[1,19,8,1024]{3,2,1,0:T(8,128)} %param.2) | copy-start | bytes 1867780
  1.1 0.8 %copy-start.1 = (s32[1,8,1024]{2,1,0:T(8,128)S(1)}, s32[1,8,1024]{2,1,0:T(8,128)}, u32[]{:S(2)}) copy-start(s32[1,8,1024]{2,1,0:T(8,128)} %param.3) | copy-start | bytes 98308
  3.3 17.0 %collective-permute-start.2 = (f32[680,128]{1,0:T(8,128)S(1)}, f32[680,128]{1,0:T(8,128)S(1)}, u32[]{:S(2)}, u32[]{:S(2)}) collective-permute-start(f32[680,128]{1,0:T(8,128)S(1)} %get-tuple-element.21), channel_id=1, source_target_pairs={{0,8},{8,16},{16,24},{1,9},{9,17},{17,25},{2,10},{10,18},{18,26},{... | collective-permute-start | bytes 1044488 | tf_op jit(solution)/shard_map/ppermute | solution.py:931
  8.1 12.2 %collective-permute-start = (f32[20,16,128]{2,1,0:T(8,128)S(1)}, f32[20,16,128]{2,1,0:T(8,128)S(1)}, u32[]{:S(2)}, u32[]{:S(2)}) collective-permute-start(f32[20,16,128]{2,1,0:T(8,128)S(1)} %get-tuple-element.19), channel_id=1, source_target_pairs={{0,1},{1,2},{2,3},{3,4},{4,5},{5,6},{6,7},{7,0},{8,9},{9,10},{10,1... | collective-permute-start | bytes 491528 | tf_op jit(solution)/shard_map/ppermute | solution.py:934
  8.1 12.1 %collective-permute-start.1 = (f32[20,16,128]{2,1,0:T(8,128)S(1)}, f32[20,16,128]{2,1,0:T(8,128)S(1)}, u32[]{:S(2)}, u32[]{:S(2)}) collective-permute-start(f32[20,16,128]{2,1,0:T(8,128)S(1)} %get-tuple-element.20), channel_id=1, source_target_pairs={{0,7},{1,0},{2,1},{3,2},{4,3},{5,4},{6,5},{7,6},{8,15},{9,8},{10,9... | collective-permute-start | bytes 491528 | tf_op jit(solution)/shard_map/ppermute | solution.py:935
  10.8 7.5 %collective-permute-start.3 = (f32[20,8,128]{2,1,0:T(8,128)S(1)}, f32[20,8,128]{2,1,0:T(8,128)S(1)}, u32[]{:S(2)}, u32[]{:S(2)}) collective-permute-start(f32[20,8,128]{2,1,0:T(8,128)S(1)} %get-tuple-element.22), channel_id=1, source_target_pairs={{0,9},{1,10},{2,11},{3,12},{4,13},{5,14},{6,15},{7,8},{8,17},{9,18... | collective-permute-start | bytes 245768 | tf_op jit(solution)/shard_map/ppermute | solution.py:932
  12.7 7.5 %collective-permute-start.4 = (f32[20,8,128]{2,1,0:T(8,128)S(1)}, f32[20,8,128]{2,1,0:T(8,128)S(1)}, u32[]{:S(2)}, u32[]{:S(2)}) collective-permute-start(f32[20,8,128]{2,1,0:T(8,128)S(1)} %get-tuple-element.23), channel_id=1, source_target_pairs={{0,15},{1,8},{2,9},{3,10},{4,11},{5,12},{6,13},{7,14},{8,23},{9,16... | collective-permute-start | bytes 245768 | tf_op jit(solution)/shard_map/ppermute | solution.py:933
  21.4 0.7 %collective-permute-start.5 = (f32[304,128]{1,0:T(8,128)S(1)}, f32[304,128]{1,0:T(8,128)S(1)}, u32[]{:S(2)}, u32[]{:S(2)}) collective-permute-start(f32[304,128]{1,0:T(8,128)S(1)} %get-tuple-element.25), channel_id=1, source_target_pairs={{24,16},{25,17},{26,18},{27,19},{28,20},{29,21},{30,22},{31,23}} | collective-permute-start | bytes 466952 | tf_op jit(solution)/shard_map/ppermute | solution.py:949
  22.1 24.8 %collective-permute-start.6 = (f32[19,16,128]{2,1,0:T(8,128)S(1)}, f32[19,16,128]{2,1,0:T(8,128)S(1)}, u32[]{:S(2)}, u32[]{:S(2)}) collective-permute-start(f32[19,16,128]{2,1,0:T(8,128)S(1)} %get-tuple-element.31), channel_id=1, source_target_pairs={{16,8},{8,0},{17,9},{9,1},{18,10},{10,2},{19,11},{11,3},{20,12},{1... | collective-permute-start | bytes 466952 | tf_op jit(solution)/shard_map/ppermute | solution.py:955
  23.4 23.5 %collective-permute-start.7 = (f32[19,8,128]{2,1,0:T(8,128)S(1)}, f32[19,8,128]{2,1,0:T(8,128)S(1)}, u32[]{:S(2)}, u32[]{:S(2)}) collective-permute-start(f32[19,8,128]{2,1,0:T(8,128)S(1)} %get-tuple-element.32), channel_id=1, source_target_pairs={{16,0},{17,1},{18,2},{19,3},{20,4},{21,5},{22,6},{23,7}} | collective-permute-start | bytes 233480 | tf_op jit(solution)/shard_map/ppermute | solution.py:956

commit v3 on v2

--- a/solution.py
+++ b/solution.py
@@ -136,13 +136,95 @@
     return made(LANES, 0.125, holds)
 
 
-def mean_zone_matrix():
-    def holds(row, column):
-        z = sum((row >= 20 * k).astype(jnp.int32) for k in range(1, 6))
-        y = row - 20 * z + 6
-        return near_first(y, z) & (column == zone_lane(0, 8 + (y >> 1), z >> 1))
+def zone_cell(level, lane):
+    pitch, first = ZONE_PITCH[level], 6 if level == 1 else 4
+    z = sum((lane >= pitch * k).astype(jnp.int32) for k in range(1, 7))
+    return lane - pitch * z + first, z
+
+
+def covered_first(y, z):
+    return (y >= Y_LOW) & (y <= Y_HIGH) & (z <= 3)
+
+
+def mean_lane(y, z):
+    return y - 11 + 10 * z
+
+
+def mean_ring_matrix():
+    def holds(row, column):
+        y, z = zone_cell(1, row)
+        ring = near_first(y, z) & jnp.logical_not(covered_first(y, z))
+        return ring & (column == mean_lane(8 + (y >> 1), z >> 1))
 
     return made(LANES, 0.125, holds)
+
+
+def late_chunk(half, c):
+    def holds(row, column):
+        y, z = cell_of(2, row + c * LANES)
+        return column == 64 * half + (z >> 1) * 16 + (y >> 1)
+
+    return made(LANES, 0.125, holds)
+
+
+def late_back_chunk(half):
+    def holds(row, column):
+        y, z = cell_of(1, column + LANES)
+        return covered_first(y, z) & (row == 64 * half + z * 16 + y - Y_LOW)
+
+    return made(2 * LANES, 1.0, holds)
+
+
+def deep_late(cell):
+    return (cell >= 4) & (cell < 12)
+
+
+def late_mean_matrix(half, deep):
+    def holds(row, column):
+        cell = row - 64 * half
+        inside = (cell >= 0) & (cell < 64)
+        inside = inside & (deep_late(cell) if deep else jnp.logical_not(deep_late(cell)))
+        return inside & (column == mean_lane(12 + ((cell & 15) >> 1), cell >> 5))
+
+    return made(LANES, 0.125, holds)
+
+
+def deep_matrix(odd):
+    def holds(row, column):
+        i, y = row >> 5, (row & 31) >> 1
+        return ((i & 1) == odd) & (column == 64 * (i >> 1) + 4 + (y >> 1))
+
+    return made(LANES, 0.125, holds)
+
+
+def mean_back_matrix():
+    def holds(row, column):
+        z = (row >= 10).astype(jnp.int32) + (row >= 20).astype(jnp.int32)
+        return (row < 30) & (column == zone_lane(0, row - 10 * z + 11, z))
+
+    return made(LANES, 1.0, holds)
+
+
+def packed_planes(source, out, width):
+    lane = lanes()
+    per = LANES // width
+    for plane in range(-(-19 // per)):
+        total = jnp.zeros((8, LANES), F32)
+        for k in range(per):
+            q = per * plane + k
+            if q < 19:
+                part = source[q] if k == 0 else pltpu.roll(source[q], width * k, 1)
+                total = jnp.where((lane >= width * k) & (lane < width * (k + 1)), part, total)
+        out[pl.ds(8 * plane, 8), :] = total
+
+
+def late_means(late, deep, value, scratch):
+    for half in range(2):
+        scratch[...] = moved(late[...], late_mean_matrix(half, deep)).reshape(20, 8, LANES)
+        for q in range(19):
+            value[q, pl.ds(4 * half, 4), :] = (
+                scratch[q, pl.ds(0, 4, stride=2), :] + scratch[q, pl.ds(1, 4, stride=2), :]
+            )
 
 
 def spread_zone_matrix():
@@ -431,7 +513,7 @@
     value = moved(converted[...].reshape(19 * rows, LANES), matrix)
     for c in range(CHUNKS[child]):
         part = value[:, c * LANES : (c + 1) * LANES].reshape(19, rows, LANES)
-        spread[...] = part
+        spread[pl.ds(0, 19)] = part
         for q in range(19):
             t = spread[q, pl.ds(skip, count), :]
             wide[q, c, pl.ds(first, count, stride=2), :] = t
@@ -500,109 +582,161 @@
     loop(6, body)
 
 
-def finest_role(own, solid, low, high, center, left, right, state, message):
-    level, row0, n = 3, ROW0[3], OWN[3]
-
-    def scoped(g, pa, pb, wide, zone, zpost, flat, spread, widen3, restrict3):
+def finest_cycle(g, pa, pb, wide, first, groups):
+    mask = interface_mask(3, 0)
+
+    def substep(v, row, dest):
+        v = [jnp.where(mask, wide[q, 0, pl.ds(row, 8), :], v[q]) for q in range(19)]
+        post = collided(v, g[19, 0, pl.ds(row, 8), :], 3)
+        for q in range(19):
+            dest[q, 0, pl.ds(row, 8), :] = post[q]
+
+    row_loop(first, groups, lambda row: substep([g[q, 0, pl.ds(row, 8), :] for q in range(19)], row, pa))
+    row_loop(first, groups, lambda row: substep(pulled(pa, 3, row, 0), row, pb))
+
+
+def finest_role(own, solid, low, high, center, left, right, g, zpost, flows):
+    def scoped(pa, pb, wide, zone, flat, spread, widen3, restrict3):
         widen3[...] = widen_matrix(3)
         restrict3[...] = restrict_chunk(3, 0)
-        load_level(level, own, solid, low, high, g)
+        load_level(3, own, solid, low, high, g)
         load_zone(2, zone, 16, center, left, right)
         covered, rim = zone_masks(2, 0)
-        mask = interface_mask(level, 0)
-
-        def substep(v, row, dest):
-            v = [jnp.where(mask, wide[q, 0, pl.ds(row, 8), :], v[q]) for q in range(19)]
-            post = collided(v, g[19, 0, pl.ds(row, 8), :], level)
-            for q in range(19):
-                dest[q, 0, pl.ds(row, 8), :] = post[q]
-
-        for cycle in range(4):
-            if cycle > 0:
-
-                def zone_collide(row):
-                    v = [zone[q, pl.ds(row, 8), :] for q in range(19)]
-                    post = collided(v, zone[19, pl.ds(row, 8), :], 2)
-                    for q in range(19):
-                        zpost[q, pl.ds(row, 8), :] = post[q]
-
-                def zone_pull(row):
-                    v = zone_pulled(zpost, 2, row)
-                    for q in range(19):
-                        zone[q, pl.ds(row, 8), :] = v[q]
-
-                row_loop(8, 6, zone_collide)
-                pack_flows(zpost, 8, message, 48 * (cycle - 1))
-                row_loop(8, 6, zone_pull)
+        scale = child_scale(3)
+
+        def restrict(i):
+            row = pl.multiple_of(8 * i, 8)
+            v = relax([spread[q, pl.ds(row, 8), :] for q in range(19)], 1.0 - scale, scale)
+            v = [jnp.where(covered, v[q], zone[q, pl.ds(8 + row, 8), :]) for q in range(19)]
+            post = collided(v, zone[19, pl.ds(8 + row, 8), :], 2)
+            for q in range(19):
+                zpost[q, pl.ds(8 + row, 8), :] = post[q]
+
+        def zone_pull(row):
+            v = zone_pulled(zpost, 2, row)
+            for q in range(19):
+                zone[q, pl.ds(row, 8), :] = v[q]
+
+        def interface():
             convert_zone(2, zone, 8, 6, rim, flat)
             widen(flat, widen3[...], 3, 0, 48, wide, spread, PAD)
+
+        interface()
+        for cycle in range(3):
             first, groups = (PAD, 12) if cycle < 2 else (PAD + 8, 10)
 
-            def step_one(row):
-                substep([g[q, 0, pl.ds(row, 8), :] for q in range(19)], row, pa)
-
-            def step_two(row):
-                substep(pulled(pa, level, row, 0), row, pb)
-
             def step_out(row):
-                v = pulled(pb, level, row, 0)
+                v = pulled(pb, 3, row, 0)
                 for q in range(19):
                     g[q, 0, pl.ds(row, 8), :] = v[q]
 
-            row_loop(first, groups, step_one)
-            row_loop(first, groups, step_two)
-            if cycle < 3:
-                row_loop(first, groups, step_out)
-                for q in range(19):
-                    flat[q] = (
-                        g[q, 0, pl.ds(PAD, 48, stride=2), :] + g[q, 0, pl.ds(PAD + 1, 48, stride=2), :]
-                    )
-                spread[...] = moved(flat[...].reshape(19 * 48, LANES), restrict3[...]).reshape(19, 48, LANES)
-                scale = child_scale(3)
-
-                def restrict(i):
-                    row = pl.multiple_of(8 * i, 8)
-                    v = relax([spread[q, pl.ds(row, 8), :] for q in range(19)], 1.0 - scale, scale)
-                    for q in range(19):
-                        old = zone[q, pl.ds(8 + row, 8), :]
-                        zone[q, pl.ds(8 + row, 8), :] = jnp.where(covered, v[q], old)
-
-                loop(6, restrict)
-            else:
-                row_loop(row0, n // 8, step_out)
-                store_level(level, g, row0, state)
-                for q in range(19):
-                    flat[q, pl.ds(0, 32), :] = (
-                        g[q, 0, pl.ds(row0, 32, stride=2), :] + g[q, 0, pl.ds(row0 + 1, 32, stride=2), :]
-                    )
-                flat[:, pl.ds(32, 8), :] = jnp.zeros((19, 8, LANES), F32)
-                total = None
-                for i in range(4):
-                    part = jnp.concatenate(
-                        [flat[q, pl.ds(8 * i, 8), :] for q in range(19)] + [jnp.zeros((8, LANES), F32)], axis=0
-                    )
-                    part = moved(part, compact_chunk(i))
-                    total = part if total is None else total + part
-                scale = child_scale(3)
-                v = relax([total[8 * q : 8 * q + 8] for q in range(19)], 1.0 - scale, scale)
-                for q in range(19):
-                    message[pl.ds(144 + 8 * q, 8), :] = v[q]
-                message[pl.ds(296, 8), :] = jnp.zeros((8, LANES), F32)
+            finest_cycle(g, pa, pb, wide, first, groups)
+            row_loop(first, groups, step_out)
+            for q in range(19):
+                flat[q] = g[q, 0, pl.ds(PAD, 48, stride=2), :] + g[q, 0, pl.ds(PAD + 1, 48, stride=2), :]
+            spread[...] = moved(flat[...].reshape(19 * 48, LANES), restrict3[...]).reshape(19, 48, LANES)
+            loop(6, restrict)
+            pack_flows(zpost, 8, flows, 48 * cycle)
+            if cycle < 2:
+                row_loop(8, 6, zone_pull)
+                interface()
 
     rows = ROWS[3]
     pl.run_scoped(
         scoped,
-        pltpu.VMEM((20, 1, rows, LANES), F32),
         pltpu.VMEM((19, 1, rows, LANES), F32),
         pltpu.VMEM((19, 1, rows, LANES), F32),
         pltpu.VMEM((19, 1, rows, LANES), F32),
         pltpu.VMEM((20, 64, LANES), F32),
-        pltpu.VMEM((19, 64, LANES), F32),
         pltpu.VMEM((19, 48, LANES), F32),
         pltpu.VMEM((19, 48, LANES), F32),
         pltpu.VMEM((2 * LANES, LANES), BF16),
         pltpu.VMEM((2 * LANES, LANES), BF16),
     )
+
+
+def last_cycle_kernel(g, zpost, state, means, far_first, far_coarse):
+    row0, n = ROW0[3], OWN[3]
+
+    @pl.when(lax.axis_index("level") == 3)
+    def _():
+        def scoped(pa, pb, wide, zone, flat, spread, out, pairs, value, scratch):
+            _, rim = zone_masks(2, 0)
+
+            def zone_pull(row):
+                v = zone_pulled(zpost, 2, row)
+                for q in range(19):
+                    zone[q, pl.ds(row, 8), :] = v[q]
+
+            row_loop(8, 6, zone_pull)
+            convert_zone(2, zone, 8, 6, rim, flat)
+            widen(flat, widen_matrix(3), 3, 0, 48, wide, spread, PAD)
+            finest_cycle(g, pa, pb, wide, PAD + 8, 10)
+
+            def step_out(row):
+                v = pulled(pb, 3, row, 0)
+                for q in range(19):
+                    out[q, 0, pl.ds(row - row0, 8), :] = v[q]
+
+            row_loop(row0, n // 8, step_out)
+            for q in range(19):
+                flat[q, pl.ds(0, 32), :] = (
+                    out[q, 0, pl.ds(0, 32, stride=2), :] + out[q, 0, pl.ds(1, 32, stride=2), :]
+                )
+            total = None
+            for i in range(4):
+                part = jnp.concatenate(
+                    [flat[q, pl.ds(8 * i, 8), :] for q in range(19)] + [jnp.zeros((8, LANES), F32)], axis=0
+                )
+                part = moved(part, compact_chunk(i))
+                total = part if total is None else total + part
+            scale = child_scale(3)
+            v = relax([total[8 * q : 8 * q + 8] for q in range(19)], 1.0 - scale, scale)
+            for q in range(19):
+                means[pl.ds(8 * q, 8), :] = v[q]
+            means[pl.ds(152, 8), :] = jnp.zeros((8, LANES), F32)
+            pairs[...] = jnp.zeros(pairs.shape, F32)
+            for q in range(19):
+                pairs[pl.ds(4 * q, 4), :] = (
+                    means[pl.ds(8 * q, 4, stride=2), :] + means[pl.ds(8 * q + 1, 4, stride=2), :]
+                )
+            for odd in range(2):
+                scratch[pl.ds(0, 80), :] = moved(pairs[...], deep_matrix(odd))
+                for q in range(19):
+                    value[pl.ds(8 * q + 4 * odd, 4), :] = scratch[pl.ds(4 * q, 4), :]
+            scale = child_scale(2)
+            v = relax([value[pl.ds(8 * q, 8), :] for q in range(19)], 1.0 - scale, scale)
+            deep = deep_late(lanes() & 63)
+            for q in range(19):
+                value[pl.ds(8 * q, 8), :] = jnp.where(deep, v[q], 0.0)
+            value[pl.ds(152, 8), :] = jnp.zeros((8, LANES), F32)
+            lane = lanes()
+            for plane in range(3):
+                total = jnp.zeros((8, LANES), F32)
+                for k in range(8):
+                    q = 8 * plane + k
+                    if q < 19:
+                        part = pltpu.roll(value[pl.ds(8 * q, 8), :], (8 * k - 4) % LANES, 1)
+                        total = jnp.where(((lane & 63) >> 3) == k, part, total)
+                far_first[pl.ds(8 * plane, 8), :] = total
+            late_means(value, True, flat.at[:, pl.ds(0, 8)], spread.at[pl.ds(0, 20), pl.ds(0, 8)])
+            packed_planes([flat[q, pl.ds(0, 8), :] for q in range(19)], far_coarse, 32)
+            store_level(3, out, 0, state)
+
+        rows = ROWS[3]
+        pl.run_scoped(
+            scoped,
+            pltpu.VMEM((19, 1, rows, LANES), F32),
+            pltpu.VMEM((19, 1, rows, LANES), F32),
+            pltpu.VMEM((19, 1, rows, LANES), F32),
+            pltpu.VMEM((19, 64, LANES), F32),
+            pltpu.VMEM((19, 48, LANES), F32),
+            pltpu.VMEM((20, 48, LANES), F32),
+            pltpu.VMEM((19, 1, n, LANES), F32),
+            pltpu.VMEM((80, LANES), F32),
+            pltpu.VMEM((160, LANES), F32),
+            pltpu.VMEM((80, LANES), F32),
+        )
 
 
 def restrict_pairs(level, g, first, count, skip, flat):
@@ -620,7 +754,7 @@
     return total.reshape(flat.shape[0], rows, LANES)
 
 
-def second_role(own, solid, low, high, center, left, right, keep_post, keep_wide, keep_zone):
+def second_role(own, solid, low, high, center, left, right, keep_post, keep_wide, early, ring):
     level, row0 = 2, ROW0[2]
     first = row0 - 8
 
@@ -656,8 +790,15 @@
         row_loop(8, 4, zone_pull)
         convert_zone(1, zone, 8, 4, rim, conv)
         widen(conv, widen_matrix(2), 2, 4, 24, keep_wide, spread, first)
+        near, _ = zone_masks(1, 1)
         for q in range(19):
-            keep_zone[q] = zone[q, pl.ds(16, 16), :]
+            for i in range(2):
+                rows = pl.ds(8 * i, 8)
+                early[q, rows, :] = jnp.where(near, zone[q, pl.ds(16 + 8 * i, 8), :], 0.0)
+        mean = moved(early[...].reshape(19 * 16, LANES), mean_ring_matrix())
+        spread[:, pl.ds(0, 16), :] = mean.reshape(19, 16, LANES)
+        for q in range(19):
+            ring[q] = spread[q, pl.ds(0, 8, stride=2), :] + spread[q, pl.ds(1, 8, stride=2), :]
 
     pl.run_scoped(
         scoped,
@@ -671,7 +812,7 @@
     )
 
 
-def first_role(own, solid, low, high, center, left, right, state, partial):
+def first_role(own, solid, low, high, center, left, right, state, early):
     level, row0, n = 1, ROW0[1], OWN[1]
     first = row0 - 8
 
@@ -691,7 +832,7 @@
             total = part if total is None else total + part
         flat[...] = total.reshape(19, n, LANES)
         for q in range(19):
-            partial[q] = flat[q, pl.ds(0, 8, stride=2), :] + flat[q, pl.ds(1, 8, stride=2), :]
+            early[q, pl.ds(0, 8), :] = flat[q, pl.ds(0, 8, stride=2), :] + flat[q, pl.ds(1, 8, stride=2), :]
 
     pl.run_scoped(
         scoped,
@@ -723,52 +864,46 @@
 
 def main_kernel(
     own, solid, low, high, center, left, right,
-    state, message, keep_post, keep_wide, keep_zone, partial,
+    state, fine, fine_post, flows, keep_post, keep_wide, early, ring,
 ):
     me = lax.axis_index("level")
     arrived = (own, solid, low, high, center, left, right)
 
     @pl.when(me == 3)
     def _():
-        finest_role(*arrived, state, message)
+        finest_role(*arrived, fine, fine_post, flows)
 
     @pl.when(me == 2)
     def _():
-        second_role(*arrived, keep_post, keep_wide, keep_zone)
+        second_role(*arrived, keep_post, keep_wide, early, ring)
 
     @pl.when(me == 1)
     def _():
-        first_role(*arrived, state, partial)
+        first_role(*arrived, state, early)
 
     @pl.when(me == 0)
     def _():
         coarse_role(own, solid, low, high, state)
 
 
-def return_kernel(
-    message, keep_post, keep_wide, keep_zone, partial,
-    state, to_first, to_coarse,
-):
-    me = lax.axis_index("level")
+def flow_kernel(flows, keep_post, keep_wide, ring, result, late, late_mean):
     level, row0 = 2, ROW0[2]
     first = row0 - 8
 
-    @pl.when(me == 2)
+    @pl.when(lax.axis_index("level") == 2)
     def _():
-        def scoped(g, post, override, back, flat, means, zone):
-            flows = message[pl.ds(0, 144), :]
+        def scoped(g, post, override, flat, value, scratch):
             for k, q in enumerate(FLOW_DIRECTIONS):
-                total = moved(flows, flow_chunk(q))
+                total = moved(flows[...], flow_chunk(q))
                 for c in range(2):
                     override[k, c] = total[:, c * LANES : (c + 1) * LANES]
 
             def overridden(c, row, cycle, v):
-                lane = lanes() + c * LANES
-                y, z = lane >> 3, lane & 7
+                y, z = cell_of(2, lanes() + c * LANES)
                 v = list(v)
                 for k, q in enumerate(FLOW_DIRECTIONS):
-                    mask = flow_mask(q, y, z)
-                    v[q] = jnp.where(mask, override[k, c, pl.ds(48 * cycle + row - first, 8), :], v[q])
+                    value = override[k, c, pl.ds(48 * cycle + row - first, 8), :]
+                    v[q] = jnp.where(flow_mask(q, y, z), value, v[q])
                 return v
 
             masks = [interface_mask(level, c) for c in range(2)]
@@ -795,93 +930,130 @@
                             post[q, c, pl.ds(row, 8), :] = v[q]
 
                 row_loop(first, 6, body)
-            pull_rows(level, post, g, row0, 4)
-            means_back = message[pl.ds(144, 160), :]
-            for i in range(4):
-                total = moved(means_back, spread_chunk(i))
+
+            def last(row):
                 for c in range(2):
-                    back[i, c] = total[:, c * LANES : (c + 1) * LANES].reshape(20, 8, LANES)
-            for c in range(2):
-                lane = lanes() + c * LANES
-                y, z = lane >> 3, lane & 7
-                covered = (y >= Y_LOW) & (y <= Y_HIGH) & (z <= 1)
-                for i in range(4):
+                    v = pulled(post, level, row, c)
                     for q in range(19):
-                        rows = pl.ds(row0 + 8 * i, 8)
-                        g[q, c, rows, :] = jnp.where(covered, back[i, c, q], g[q, c, rows, :])
-            store_level(level, g, row0, state)
-            means[...] = restrict_pairs(level, g, row0, 16, 0, flat)
+                        result[q, c, pl.ds(row - row0, 8), :] = v[q]
+
+            row_loop(row0, 4, last)
+            for q in range(19):
+                for c in range(2):
+                    flat[c, q] = result[q, c, pl.ds(0, 16, stride=2), :] + result[q, c, pl.ds(1, 16, stride=2), :]
+            flat[:, 19] = jnp.zeros((2, 16, LANES), F32)
+            total = None
+            for half in range(2):
+                for c in range(2):
+                    part = moved(flat[c, :, pl.ds(8 * half, 8), :].reshape(160, LANES), late_chunk(half, c))
+                    total = part if total is None else total + part
             scale = child_scale(2)
-            covered, _ = zone_masks(1, 0)
-            near, _ = zone_masks(1, 1)
-            for i in range(2):
-                rows = pl.ds(8 * i, 8)
-                v = relax([means[q, rows, :] for q in range(19)], 1.0 - scale, scale)
-                for q in range(19):
-                    value = jnp.where(covered, v[q], keep_zone[q, rows, :])
-                    to_first[q, rows, :] = jnp.where(near, value, 0.0)
-            zone[...] = moved(to_first[...].reshape(19 * 16, LANES), mean_zone_matrix()).reshape(19, 16, LANES)
-            for q in range(19):
-                to_coarse[q] = zone[q, pl.ds(0, 8, stride=2), :] + zone[q, pl.ds(1, 8, stride=2), :]
+            v = relax([total[8 * q : 8 * q + 8] for q in range(19)], 1.0 - scale, scale)
+            for q in range(19):
+                late[pl.ds(8 * q, 8), :] = v[q]
+            late[pl.ds(152, 8), :] = jnp.zeros((8, LANES), F32)
+            late_means(late, False, value, scratch)
+            packed_planes([value[q] + ring[q] for q in range(19)], late_mean, 32)
 
         pl.run_scoped(
             scoped,
             pltpu.VMEM((19, 2, ROWS[2], LANES), F32),
             pltpu.VMEM((19, 2, ROWS[2], LANES), F32),
             pltpu.VMEM((len(FLOW_DIRECTIONS), 2, 144, LANES), F32),
-            pltpu.VMEM((4, 2, 20, 8, LANES), F32),
-            pltpu.VMEM((19, 2, 16, LANES), F32),
-            pltpu.VMEM((19, 16, LANES), F32),
-            pltpu.VMEM((19, 16, LANES), F32),
+            pltpu.VMEM((2, 20, 16, LANES), F32),
+            pltpu.VMEM((19, 8, LANES), F32),
+            pltpu.VMEM((20, 8, LANES), F32),
+        )
+
+
+def finish_kernel(old_state, result, third_state, early, near, far, far_coarse, state):
+    me = lax.axis_index("level")
+
+    @pl.when(me == 3)
+    def _():
+        state[...] = third_state[...]
+
+    @pl.when(me == 2)
+    def _():
+        def scoped(g, back):
+            for i in range(4):
+                total = moved(near[...], spread_chunk(i))
+                for c in range(2):
+                    back[i, c] = total[:, c * LANES : (c + 1) * LANES].reshape(20, 8, LANES)
+            for c in range(2):
+                y, z = cell_of(2, lanes() + c * LANES)
+                covered = (y >= Y_LOW) & (y <= Y_HIGH) & (z <= 1)
+
+                def insert(q, c=c, covered=covered):
+                    for i in range(4):
+                        rows = pl.ds(8 * i, 8)
+                        g[q, c, rows, :] = jnp.where(covered, back[i, c, q], result[q, c, rows, :])
+
+                loop(19, insert, 1)
+            store_level(2, g, 0, state)
+
+        pl.run_scoped(
+            scoped, pltpu.VMEM((19, 2, OWN[2], LANES), F32), pltpu.VMEM((4, 2, 20, 8, LANES), F32)
         )
 
     @pl.when(me == 1)
     def _():
-        to_first[:, pl.ds(0, 8), :] = partial[...]
-
-
-def finish_kernel(old_state, second_state, from_near, from_far, state):
-    me = lax.axis_index("level")
-
-    @pl.when(me == 3)
-    def _():
-        state[...] = old_state[...]
-
-    @pl.when(me == 2)
-    def _():
-        state[...] = second_state[...]
-
-    @pl.when(me == 1)
-    def _():
-        def scoped(wide):
-            total = moved(from_near[...].reshape(19 * 16, LANES), spread_zone_matrix())
+        def scoped(wide, inner, value):
+            lane = lanes()
+            deep = deep_late(lane & 63)
+            for q in range(19):
+                part = pltpu.roll(far[pl.ds(8 * (q // 8), 8), :], (4 - 8 * (q % 8)) % LANES, 1)
+                value[pl.ds(8 * q, 8), :] = jnp.where(deep, part, near[pl.ds(8 * q, 8), :])
+            value[pl.ds(152, 8), :] = jnp.zeros((8, LANES), F32)
+            total = moved(early[...].reshape(19 * 16, LANES), spread_zone_matrix())
             for c in range(4):
                 wide[:, c] = total[:, c * LANES : (c + 1) * LANES].reshape(19, 16, LANES)
+            for half in range(2):
+                total = moved(value[...], late_back_chunk(half))
+                for c in range(2):
+                    part = total[:, c * LANES : (c + 1) * LANES].reshape(20, 8, LANES)
+                    inner[c, :, pl.ds(8 * half, 8), :] = part
 
             def one(q):
                 for j in range(8):
                     c = j % 4
-                    lane = lanes() + c * LANES
-                    y, z = lane >> 4, lane & 15
-                    near = (y >= Y_LOW - 1) & (y <= Y_HIGH + 1) & (z <= 4)
+                    y, z = cell_of(1, lanes() + c * LANES)
                     columns = pl.ds(j * LANES, LANES)
-                    value = wide[q, c, pl.ds(j // 4, 8, stride=2), :]
-                    state[q, :, columns] = jnp.where(near, value, old_state[q, :, columns])
+                    rows = pl.ds(j // 4, 8, stride=2)
+                    value = jnp.where(near_first(y, z), wide[q, c, rows, :], old_state[q, :, columns])
+                    if c in (1, 2):
+                        value = jnp.where(covered_first(y, z), inner[c - 1, q, rows, :], value)
+                    state[q, :, columns] = value
 
             loop(19, one)
 
-        pl.run_scoped(scoped, pltpu.VMEM((19, 4, 16, LANES), F32))
+        pl.run_scoped(
+            scoped,
+            pltpu.VMEM((19, 4, 16, LANES), F32),
+            pltpu.VMEM((2, 20, 16, LANES), F32),
+            pltpu.VMEM((160, LANES), F32),
+        )
 
     @pl.when(me == 0)
     def _():
         def scoped(value):
+            lane = lanes()
+            for q in range(19):
+                rows = pl.ds(8 * (q // 4), 8)
+                part = far[rows, :] + far_coarse[rows, :]
+                if q % 4:
+                    part = pltpu.roll(part, LANES - 32 * (q % 4), 1)
+                value[q] = jnp.where(lane < 32, part, 0.0)
+            value[19] = jnp.zeros((8, LANES), F32)
+            total = moved(value[...].reshape(160, LANES), mean_back_matrix())
             scale = child_scale(1)
             v = relax(
-                [from_near[q, pl.ds(0, 8), :] + from_far[q] for q in range(19)], 1.0 - scale, scale
+                [early[q, pl.ds(0, 8), :] + total[8 * q : 8 * q + 8] for q in range(19)],
+                1.0 - scale,
+                scale,
             )
             for q in range(19):
                 value[q] = v[q]
-            value[19] = jnp.zeros((8, LANES), F32)
             total = moved(value[...].reshape(160, LANES), spread_covered_matrix())
             for q in range(19):
                 for j in range(8):
@@ -889,19 +1061,22 @@
                     if not 2 <= j < 6:
                         state[q, :, columns] = old_state[q, :, columns]
                     else:
-                        covered = (lanes() & 31) < 8
+                        covered = (lane & 31) < 8
                         part = total[8 * q : 8 * q + 8, (j - 2) * LANES : (j - 1) * LANES]
                         state[q, :, columns] = jnp.where(covered, part, old_state[q, :, columns])
 
         pl.run_scoped(scoped, pltpu.VMEM((20, 8, LANES), F32))
 
 
-def call(kernel, shapes, args):
+def call(kernel, shapes, args, micros):
     return pl.pallas_call(
         kernel,
         out_shape=[jax.ShapeDtypeStruct(s, F32) for s in shapes],
         in_specs=[pl.BlockSpec(memory_space=pltpu.VMEM)] * len(args),
         out_specs=[pl.BlockSpec(memory_space=pltpu.VMEM)] * len(shapes),
+        cost_estimate=pl.CostEstimate(
+            flops=int(micros * 1e9), bytes_accessed=int(micros * 3.6e6), transcendentals=0
+        ),
         compiler_params=pltpu.CompilerParams(vmem_limit_bytes=24 * 1024 * 1024),
     )(*args)
 
@@ -927,6 +1102,7 @@
         start_kernel,
         [(20, 16, LANES), (20, 16, LANES), (680, LANES), (20, 8, LANES), (20, 8, LANES)],
         [own, flags],
+        1.5,
     )
     center = lax.ppermute(center, "level", down)
     left = lax.ppermute(zone_right, both, diagonal(1))
@@ -934,30 +1110,39 @@
     low = lax.ppermute(to_right, "blocks", forward)
     high = lax.ppermute(to_left, "blocks", backward)
 
-    state, message, keep_post, keep_wide, keep_zone, partial = call(
+    full = (19, SLAB, NY * NZ)
+    state, fine, fine_post, flows, keep_post, keep_wide, early, ring = call(
         main_kernel,
         [
-            (19, SLAB, NY * NZ),
-            (304, LANES),
+            full,
+            (20, 1, ROWS[3], LANES),
+            (19, 64, LANES),
+            (144, LANES),
             (20, 2, ROWS[2], LANES),
             (19, 2, ROWS[2], LANES),
             (19, 16, LANES),
             (19, 8, LANES),
         ],
         [own, flags, low, high, center, left, right],
+        8.0,
     )
-    message = lax.ppermute(message, "level", [(3, 2)])
-    second_state, to_first, to_coarse = call(
-        return_kernel,
-        [(19, SLAB, NY * NZ), (19, 16, LANES), (19, 8, LANES)],
-        [message, keep_post, keep_wide, keep_zone, partial],
+    flows = lax.ppermute(flows, "level", [(3, 2)])
+    early = lax.ppermute(early, "level", [(2, 1), (1, 0)])
+    third_state, means, far_first, far_coarse = call(
+        last_cycle_kernel, [full, (160, LANES), (40, LANES), (40, LANES)], [fine, fine_post], 4.0
     )
-    near = lax.ppermute(to_first, "level", [(2, 1), (1, 0)])
-    far = lax.ppermute(to_coarse, "level", [(2, 0)])
+    far_coarse = lax.ppermute(far_coarse, "level", [(3, 0)])
+    result, late, late_mean = call(
+        flow_kernel,
+        [(19, 2, OWN[2], LANES), (160, LANES), (40, LANES)],
+        [flows, keep_post, keep_wide, ring],
+        2.5,
+    )
+    me = lax.axis_index("level")
+    far = lax.ppermute(jnp.where(me == 3, far_first, late_mean), "level", [(3, 1), (2, 0)])
+    near = lax.ppermute(jnp.where(me == 3, means, late), "level", [(3, 2), (2, 1)])
     (state,) = call(
-        finish_kernel,
-        [(19, SLAB, NY * NZ)],
-        [state, second_state, near, far],
+        finish_kernel, [full], [state, result, third_state, early, near, far, far_coarse], 1.0
     )
     return state[None]
 

time: 48.3 us -> 42.5 us (0.88)
  waiting for transfers between devices: 24.2 us -> 16.2 us
  starting transfers between devices: 18.1 us -> 20.1 us
    ppermute x3 -> x5, waiting for transfers between devices: 22.2 us -> 14.1 us  [the longest x1 9.43 us: shards(): far_coarse = lax.ppermute(far_coarse, 'level', [(3, 0)])]
    ppermute x3 -> x5, starting transfers between devices: 3.25 us -> 5.21 us  [the longest x1 1.29 us: shards(): far_coarse = lax.ppermute(far_coarse, 'level', [(3, 0)])]
    pallas_call x4 -> x5, Pallas kernels: 3.69 us -> 3.93 us  [call(): pl.pallas_call(kernel, out_shape=[jax.ShapeDtypeStruct(s, F32) for s in s...]
    unnamed x4 -> x8, local copies, waits for them, and re-layouts: 1.83 us -> 1.84 us
  transfers between devices with their start and end apart: 8 -> 10, of which waited for: 2 -> 3; matrix products, arithmetic and copies ran while one was open for 0% -> 0% of each run, Pallas kernels for 0% -> 0%
where the time goes in v3:
time: 42.5 us; the launch traced here: 42.2 us
  starting transfers between devices  20.1 us (47%)
  waiting for transfers between devices  16.2 us (38%)
  Pallas kernels  3.93 us (9%)
  local copies, waits for them, and re-layouts  1.84 us (4%)
    ppermute x1, waiting for transfers between devices, shards(): far_coarse = lax.ppermute(far_coarse, 'level', [(3, 0)])  9.43 us
    ppermute x1, starting transfers between devices, shards(): right = lax.ppermute(zone_left, both, diagonal(-1))  5.49 us
    ppermute x1, starting transfers between devices, shards(): center = lax.ppermute(center, 'level', down)  4.74 us
    ppermute x1, waiting for transfers between devices, shards(): lax.ppermute(jnp.where(me == 3, far_first, late_mean), 'level', [(3, 1),...  4.69 us
    pallas_call x5, Pallas kernels, call(): pl.pallas_call(kernel, out_shape=[jax.ShapeDtypeStruct(s, F32) for s in s...  3.93 us
    ppermute x1, starting transfers between devices, shards(): high = lax.ppermute(to_left, 'blocks', backward)  2.63 us
    ppermute x1, waiting for transfers between devices, shards(): right = lax.ppermute(zone_left, both, diagonal(-1))  2.02 us
    ppermute x1, starting transfers between devices, shards(): left = lax.ppermute(zone_right, both, diagonal(1))  1.95 us
  transfers between devices with their start and end apart: 10, of which 3 were waited for; matrix products, arithmetic and copies ran while one was open for 0% of the time, Pallas kernels for 0%

profile of v3, /device:TPU:0, one launch (start us, length us, event | category | flops | bytes accessed | tf_op | source)
XLA Modules:
  0.0 42.2 jit_solution(16168382040751310227)
XLA Ops:
  0.0 0.0 copy-start
  0.0 1.1 %copy-done = f32[1,19,8,1024]{3,2,1,0:T(8,128)S(1)} copy-done((f32[1,19,8,1024]{3,2,1,0:T(8,128)S(1)}, f32[1,19,8,1024]{3,2,1,0:T(8,128)}, u32[]{:S(2)}) %copy-start) | copy-done | bytes 622616
  1.1 0.0 copy-start.2
  1.1 0.8 %copy-done.2 = s32[1,8,1024]{2,1,0:T(8,128)S(1)} copy-done((s32[1,8,1024]{2,1,0:T(8,128)S(1)}, s32[1,8,1024]{2,1,0:T(8,128)}, u32[]{:S(2)}) %copy-start.2) | copy-done | bytes 32792
  1.8 0.0 copy-start.1
  1.8 0.0 copy-start.3
  1.8 1.5 %shard_map.28 = (f32[20,16,128]{2,1,0:T(8,128)S(1)}, f32[20,16,128]{2,1,0:T(8,128)S(1)}, f32[680,128]{1,0:T(8,128)S(1)}, f32[20,8,128]{2,1,0:T(8,128)S(1)}, f32[20,8,128]{2,1,0:T(8,128)S(1)}) custom-call(f32[19,8,1024]{2,1,0:T(8,128)S(1)} %bitcast.3, s32[8,1024]{1,0:T(8,128)S(1)} %bitcast.5), custom_call_target="tpu_custom_call" | custom-call | flops 1500000000 | bytes 5400000 | tf_op jit(solution)/shard_map/pallas_call | solution.py:1072
  3.3 4.7 %collective-permute-start.2 = (f32[680,128]{1,0:T(8,128)S(1)}, f32[680,128]{1,0:T(8,128)S(1)}, u32[]{:S(2)}, u32[]{:S(2)}) collective-permute-start(f32[680,128]{1,0:T(8,128)S(1)} %get-tuple-element.27), channel_id=1, source_target_pairs={{0,8},{8,16},{16,24},{1,9},{9,17},{17,25},{2,10},{10,18},{18,26},{... | collective-permute-start | bytes 1044488 | tf_op jit(solution)/shard_map/ppermute | solution.py:1107
  8.1 0.1 collective-permute-start
  8.1 2.6 %collective-permute-start.1 = (f32[20,16,128]{2,1,0:T(8,128)S(1)}, f32[20,16,128]{2,1,0:T(8,128)S(1)}, u32[]{:S(2)}, u32[]{:S(2)}) collective-permute-start(f32[20,16,128]{2,1,0:T(8,128)S(1)} %get-tuple-element.26), channel_id=1, source_target_pairs={{0,7},{1,0},{2,1},{3,2},{4,3},{5,4},{6,5},{7,6},{8,15},{9,8},{10,9... | collective-permute-start | bytes 491528 | tf_op jit(solution)/shard_map/ppermute | solution.py:1111
  10.8 2.0 %collective-permute-start.3 = (f32[20,8,128]{2,1,0:T(8,128)S(1)}, f32[20,8,128]{2,1,0:T(8,128)S(1)}, u32[]{:S(2)}, u32[]{:S(2)}) collective-permute-start(f32[20,8,128]{2,1,0:T(8,128)S(1)} %get-tuple-element.28), channel_id=1, source_target_pairs={{0,9},{1,10},{2,11},{3,12},{4,13},{5,14},{6,15},{7,8},{8,17},{9,18... | collective-permute-start | bytes 245768 | tf_op jit(solution)/shard_map/ppermute | solution.py:1108
  12.7 5.5 %collective-permute-start.4 = (f32[20,8,128]{2,1,0:T(8,128)S(1)}, f32[20,8,128]{2,1,0:T(8,128)S(1)}, u32[]{:S(2)}, u32[]{:S(2)}) collective-permute-start(f32[20,8,128]{2,1,0:T(8,128)S(1)} %get-tuple-element.29), channel_id=1, source_target_pairs={{0,15},{1,8},{2,9},{3,10},{4,11},{5,12},{6,13},{7,14},{8,23},{9,16... | collective-permute-start | bytes 245768 | tf_op jit(solution)/shard_map/ppermute | solution.py:1109
  18.2 0.0 collective-permute-done.3.left
  18.2 2.0 %collective-permute-done.4.right = f32[20,8,128]{2,1,0:T(8,128)S(1)} collective-permute-done((f32[20,8,128]{2,1,0:T(8,128)S(1)}, f32[20,8,128]{2,1,0:T(8,128)S(1)}, u32[]{:S(2)}, u32[]{:S(2)}) %collective-permute-start.4) | collective-permute-done | bytes 81952 | tf_op jit(solution)/shard_map/ppermute | solution.py:1109
  20.3 0.0 collective-permute-done.low
  20.3 0.0 collective-permute-done.1.high
  20.3 0.0 collective-permute-done.2.center
  20.3 0.0 copy-done.1
  20.3 0.0 copy-done.3
  20.3 1.2 %shard_map.29 = (f32[19,8,1024]{2,1,0:T(8,128)S(1)}, f32[20,1,112,128]{3,2,1,0:T(8,128)S(1)}, f32[19,64,128]{2,1,0:T(8,128)S(1)}, f32[144,128]{1,0:T(8,128)S(1)}...) custom-call(f32[19,8,1024]{2,1,0:T(8,128)S(1)} %bitcast.4, ...), custom_call_target="tpu_custom_call" | custom-call | flops 8000000000 | bytes 28800000 | tf_op jit(solution)/shard_map/pallas_call | solution.py:1072
  21.5 0.7 %collective-permute-start.5 = (f32[144,128]{1,0:T(8,128)S(1)}, f32[144,128]{1,0:T(8,128)S(1)}, u32[]{:S(2)}, u32[]{:S(2)}) collective-permute-start(f32[144,128]{1,0:T(8,128)S(1)} %get-tuple-element.31), channel_id=1, source_target_pairs={{24,16},{25,17},{26,18},{27,19},{28,20},{29,21},{30,22},{31,23}} | collective-permute-start | bytes 221192 | tf_op jit(solution)/shard_map/ppermute | solution.py:1129
  22.2 1.3 %collective-permute-start.9 = (f32[40,128]{1,0:T(8,128)S(1)}, f32[40,128]{1,0:T(8,128)S(1)}, u32[]{:S(2)}, u32[]{:S(2)}) collective-permute-start(f32[40,128]{1,0:T(8,128)S(1)} %get-tuple-element.44), channel_id=1, source_target_pairs={{24,0},{25,1},{26,2},{27,3},{28,4},{29,5},{30,6},{31,7}} | collective-permute-start | bytes 61448 | tf_op jit(solution)/shard_map/ppermute | solution.py:1134
  23.5 1.3 %collective-permute-start.6 = (f32[19,16,128]{2,1,0:T(8,128)S(1)}, f32[19,16,128]{2,1,0:T(8,128)S(1)}, u32[]{:S(2)}, u32[]{:S(2)}) collective-permute-start(f32[19,16,128]{2,1,0:T(8,128)S(1)} %get-tuple-element.39), channel_id=1, source_target_pairs={{16,8},{8,0},{17,9},{9,1},{18,10},{10,2},{19,11},{11,3},{20,12},{1... | collective-permute-start | bytes 466952 | tf_op jit(solution)/shard_map/ppermute | solution.py:1130
  24.8 0.0 collective-permute-done.5.flows
  24.8 0.7 %collective-permute-start.7 = (f32[160,128]{1,0:T(8,128)S(1)}, f32[160,128]{1,0:T(8,128)S(1)}, u32[]{:S(2)}, u32[]{:S(2)}) collective-permute-start(f32[160,128]{1,0:T(8,128)S(1)} %broadcast_select_fusion), channel_id=1, source_target_pairs={{24,16},{16,8},{25,17},{17,9},{26,18},{18,10},{27,19},{19,11},{28,... | collective-permute-start | bytes 245768 | tf_op jit(solution)/shard_map/ppermute | solution.py:1143
  25.5 1.3 %collective-permute-start.8 = (f32[40,128]{1,0:T(8,128)S(1)}, f32[40,128]{1,0:T(8,128)S(1)}, u32[]{:S(2)}, u32[]{:S(2)}) collective-permute-start(f32[40,128]{1,0:T(8,128)S(1)} %broadcast_select_fusion.1), channel_id=1, source_target_pairs={{24,8},{16,0},{25,9},{17,1},{26,10},{18,2},{27,11},{19,3},{28,12},... | collective-permute-start | bytes 61448 | tf_op jit(solution)/shard_map/ppermute | solution.py:1142
  26.8 9.4 %collective-permute-done.9.far_coarse = f32[40,128]{1,0:T(8,128)S(1)} collective-permute-done((f32[40,128]{1,0:T(8,128)S(1)}, f32[40,128]{1,0:T(8,128)S(1)}, u32[]{:S(2)}, u32[]{:S(2)}) %collective-permute-start.9) | collective-permute-done | bytes 20512 | tf_op jit(solution)/shard_map/ppermute | solution.py:1134
  36.2 4.7 %collective-permute-done.8.far = f32[40,128]{1,0:T(8,128)S(1)} collective-permute-done((f32[40,128]{1,0:T(8,128)S(1)}, f32[40,128]{1,0:T(8,128)S(1)}, u32[]{:S(2)}, u32[]{:S(2)}) %collective-permute-start.8) | collective-permute-done | bytes 20512 | tf_op jit(solution)/shard_map/ppermute | solution.py:1142
  40.9 0.0 collective-permute-done.7.near
  40.9 0.0 collective-permute-done.6.early
  40.9 1.3 %shard_map.32 = f32[19,8,1024]{2,1,0:T(8,128)} custom-call(f32[19,8,1024]{2,1,0:T(8,128)S(1)} %get-tuple-element.30.old_state, f32[19,2,32,128]{3,2,1,0:T(8,128)S(1)} %get-tuple-element.35.result, f32[19,8,1024]{2,1,0:T(8,128)S(1)} %get-tuple-element.38.third_state, f32[19,16,128]{2,1,0:T(8,128)S(1)} %collective-permute-done.6.early, ...), custom_call_target="tpu_custom_call" | custom-call | flops 1000000000 | bytes 3600000 | tf_op jit(solution)/shard_map/pallas_call | solution.py:1072
  (4 shorter events, 0.1 us)
Async XLA Ops:
  0.0 1.1 %copy-start = (f32[1,19,8,1024]{3,2,1,0:T(8,128)S(1)}, f32[1,19,8,1024]{3,2,1,0:T(8,128)}, u32[]{:S(2)}) copy-start(f32[1,19,8,1024]{3,2,1,0:T(8,128)} %param.2) | copy-start | bytes 1867780
  1.1 0.8 %copy-start.2 = (s32[1,8,1024]{2,1,0:T(8,128)S(1)}, s32[1,8,1024]{2,1,0:T(8,128)}, u32[]{:S(2)}) copy-start(s32[1,8,1024]{2,1,0:T(8,128)} %param.3) | copy-start | bytes 98308
  1.8 18.4 %copy-start.1 = (f32[1,19,8,1024]{3,2,1,0:T(8,128)S(1)}, f32[1,19,8,1024]{3,2,1,0:T(8,128)}, u32[]{:S(2)}) copy-start(f32[1,19,8,1024]{3,2,1,0:T(8,128)} %param.2) | copy-start | bytes 1867780
  1.8 18.4 %copy-start.3 = (s32[1,8,1024]{2,1,0:T(8,128)S(1)}, s32[1,8,1024]{2,1,0:T(8,128)}, u32[]{:S(2)}) copy-start(s32[1,8,1024]{2,1,0:T(8,128)} %param.3) | copy-start | bytes 98308
  3.3 16.9 %collective-permute-start.2 = (f32[680,128]{1,0:T(8,128)S(1)}, f32[680,128]{1,0:T(8,128)S(1)}, u32[]{:S(2)}, u32[]{:S(2)}) collective-permute-start(f32[680,128]{1,0:T(8,128)S(1)} %get-tuple-element.27), channel_id=1, source_target_pairs={{0,8},{8,16},{16,24},{1,9},{9,17},{17,25},{2,10},{10,18},{18,26},{... | collective-permute-start | bytes 1044488 | tf_op jit(solution)/shard_map/ppermute | solution.py:1107
  8.1 12.2 %collective-permute-start = (f32[20,16,128]{2,1,0:T(8,128)S(1)}, f32[20,16,128]{2,1,0:T(8,128)S(1)}, u32[]{:S(2)}, u32[]{:S(2)}) collective-permute-start(f32[20,16,128]{2,1,0:T(8,128)S(1)} %get-tuple-element.25), channel_id=1, source_target_pairs={{0,1},{1,2},{2,3},{3,4},{4,5},{5,6},{6,7},{7,0},{8,9},{9,10},{10,1... | collective-permute-start | bytes 491528 | tf_op jit(solution)/shard_map/ppermute | solution.py:1110
  8.1 12.1 %collective-permute-start.1 = (f32[20,16,128]{2,1,0:T(8,128)S(1)}, f32[20,16,128]{2,1,0:T(8,128)S(1)}, u32[]{:S(2)}, u32[]{:S(2)}) collective-permute-start(f32[20,16,128]{2,1,0:T(8,128)S(1)} %get-tuple-element.26), channel_id=1, source_target_pairs={{0,7},{1,0},{2,1},{3,2},{4,3},{5,4},{6,5},{7,6},{8,15},{9,8},{10,9... | collective-permute-start | bytes 491528 | tf_op jit(solution)/shard_map/ppermute | solution.py:1111
  10.8 7.5 %collective-permute-start.3 = (f32[20,8,128]{2,1,0:T(8,128)S(1)}, f32[20,8,128]{2,1,0:T(8,128)S(1)}, u32[]{:S(2)}, u32[]{:S(2)}) collective-permute-start(f32[20,8,128]{2,1,0:T(8,128)S(1)} %get-tuple-element.28), channel_id=1, source_target_pairs={{0,9},{1,10},{2,11},{3,12},{4,13},{5,14},{6,15},{7,8},{8,17},{9,18... | collective-permute-start | bytes 245768 | tf_op jit(solution)/shard_map/ppermute | solution.py:1108
  12.7 7.5 %collective-permute-start.4 = (f32[20,8,128]{2,1,0:T(8,128)S(1)}, f32[20,8,128]{2,1,0:T(8,128)S(1)}, u32[]{:S(2)}, u32[]{:S(2)}) collective-permute-start(f32[20,8,128]{2,1,0:T(8,128)S(1)} %get-tuple-element.29), channel_id=1, source_target_pairs={{0,15},{1,8},{2,9},{3,10},{4,11},{5,12},{6,13},{7,14},{8,23},{9,16... | collective-permute-start | bytes 245768 | tf_op jit(solution)/shard_map/ppermute | solution.py:1109
  21.5 3.3 %collective-permute-start.5 = (f32[144,128]{1,0:T(8,128)S(1)}, f32[144,128]{1,0:T(8,128)S(1)}, u32[]{:S(2)}, u32[]{:S(2)}) collective-permute-start(f32[144,128]{1,0:T(8,128)S(1)} %get-tuple-element.31), channel_id=1, source_target_pairs={{24,16},{25,17},{26,18},{27,19},{28,20},{29,21},{30,22},{31,23}} | collective-permute-start | bytes 221192 | tf_op jit(solution)/shard_map/ppermute | solution.py:1129
  22.2 14.1 %collective-permute-start.9 = (f32[40,128]{1,0:T(8,128)S(1)}, f32[40,128]{1,0:T(8,128)S(1)}, u32[]{:S(2)}, u32[]{:S(2)}) collective-permute-start(f32[40,128]{1,0:T(8,128)S(1)} %get-tuple-element.44), channel_id=1, source_target_pairs={{24,0},{25,1},{26,2},{27,3},{28,4},{29,5},{30,6},{31,7}} | collective-permute-start | bytes 61448 | tf_op jit(solution)/shard_map/ppermute | solution.py:1134
  23.5 17.5 %collective-permute-start.6 = (f32[19,16,128]{2,1,0:T(8,128)S(1)}, f32[19,16,128]{2,1,0:T(8,128)S(1)}, u32[]{:S(2)}, u32[]{:S(2)}) collective-permute-start(f32[19,16,128]{2,1,0:T(8,128)S(1)} %get-tuple-element.39), channel_id=1, source_target_pairs={{16,8},{8,0},{17,9},{9,1},{18,10},{10,2},{19,11},{11,3},{20,12},{1... | collective-permute-start | bytes 466952 | tf_op jit(solution)/shard_map/ppermute | solution.py:1130
  24.8 16.1 %collective-permute-start.7 = (f32[160,128]{1,0:T(8,128)S(1)}, f32[160,128]{1,0:T(8,128)S(1)}, u32[]{:S(2)}, u32[]{:S(2)}) collective-permute-start(f32[160,128]{1,0:T(8,128)S(1)} %broadcast_select_fusion), channel_id=1, source_target_pairs={{24,16},{16,8},{25,17},{17,9},{26,18},{18,10},{27,19},{19,11},{28,... | collective-permute-start | bytes 245768 | tf_op jit(solution)/shard_map/ppermute | solution.py:1143
  25.5 15.4 %collective-permute-start.8 = (f32[40,128]{1,0:T(8,128)S(1)}, f32[40,128]{1,0:T(8,128)S(1)}, u32[]{:S(2)}, u32[]{:S(2)}) collective-permute-start(f32[40,128]{1,0:T(8,128)S(1)} %broadcast_select_fusion.1), channel_id=1, source_target_pairs={{24,8},{16,0},{25,9},{17,1},{26,10},{18,2},{27,11},{19,3},{28,12},... | collective-permute-start | bytes 61448 | tf_op jit(solution)/shard_map/ppermute | solution.py:1142

commit v4 on v3

--- a/solution.py
+++ b/solution.py
@@ -57,11 +57,6 @@
     return z * 25 + y - 4
 
 
-ZONE_CELLS = (
-    [(y, z) for y in range(8, 24) for z in range(8)],
-    [(y, z) for y in range(6, 26) for z in range(6)],
-    [(y, z) for y in range(5, 27) for z in range(5)],
-)
 ZONE_PITCH = (None, 20, 25)
 
 
@@ -80,15 +75,63 @@
     return lane >> (DEPTH[level].bit_length() - 1), lane & (DEPTH[level] - 1)
 
 
+def message_cell(level, y, z):
+    if level == 0:
+        side = (z < 7) & ((y == 8) | (y == 23))
+        top = (z == 7) & (y >= 8) & (y <= 23)
+        return jnp.where(z == 7, y - 8, 16 + 2 * z + (y == 23).astype(jnp.int32)), side | top
+    if level == 1:
+        outer = ((y >= 6) & (y <= 8)) | ((y >= 23) & (y <= 25))
+        side = (z < 3) & outer
+        top = (z >= 3) & (z <= 5) & (y >= 6) & (y <= 25)
+        return jnp.where(z >= 3, (z - 3) * 20 + y - 6, 60 + z * 6 + jnp.where(y < 9, y - 6, y - 20)), side | top
+    outer = ((y >= 5) & (y <= 8)) | ((y >= 23) & (y <= 26))
+    side = (z == 0) & outer
+    top = (z >= 1) & (z <= 4) & (y >= 5) & (y <= 26)
+    return jnp.where(z >= 1, (z - 1) * 22 + y - 5, 88 + jnp.where(y < 9, y - 5, y - 19)), side | top
+
+
 def pack_chunk(level, c):
-    ys, zs = zip(*ZONE_CELLS[level])
-
     def holds(row, column):
         y, z = cell_of(level, row + c * LANES)
-        inside = (y >= min(ys)) & (y <= max(ys)) & (z <= max(zs))
+        lane, sent = message_cell(level, y, z)
+        return sent & (column == lane)
+
+    return made(LANES, 1.0, holds)
+
+
+def flag_chunk(level, c):
+    def holds(row, column):
+        y, z = cell_of(level, row + c * LANES)
+        if level == 0:
+            inside = (y >= 8) & (y <= 23) & (z <= 7)
+        elif level == 1:
+            inside = (y >= 6) & (y <= 25) & (z <= 5)
+        else:
+            inside = (y >= 5) & (y <= 26) & (z <= 4)
         return inside & (column == zone_lane(level, y, z))
 
     return made(LANES, 1.0, holds)
+
+
+def fold_chunk(level, c):
+    def holds(row, column):
+        y, z = cell_of(level, row + c * LANES)
+        lane, sent = message_cell(level, y, z)
+        return sent & ((column & (LANES - 1)) == 96 + (lane & 31)) & ((column >> 7) == (lane >> 5))
+
+    return made(3 * LANES, 1.0, holds)
+
+
+def unpack_matrix(level, k):
+    def holds(row, column):
+        y, z = zone_cell(level, column & (LANES - 1))
+        lane, sent = message_cell(level, y, z)
+        folded = (row == 96 + (lane & 31)) & ((lane >> 5) == k)
+        own = row == lane
+        return sent & (((column < LANES) & own) | ((column >= LANES) & folded))
+
+    return made(2 * LANES, 1.0, holds)
 
 
 def widen_matrix(child):
@@ -137,6 +180,8 @@
 
 
 def zone_cell(level, lane):
+    if level == 0:
+        return 8 + (lane >> 3), lane & 7
     pitch, first = ZONE_PITCH[level], 6 if level == 1 else 4
     z = sum((lane >= pitch * k).astype(jnp.int32) for k in range(1, 7))
     return lane - pitch * z + first, z
@@ -432,7 +477,7 @@
     return jnp.dot(jnp.concatenate([high, low], axis=1), matrix, preferred_element_type=F32)
 
 
-def load_level(level, own, solid, low, high, buf):
+def load_level(level, own, low, high, buf):
     factor, count, row0 = FACTOR[level], CHUNKS[level], ROW0[level]
     n = OWN[level]
 
@@ -445,8 +490,7 @@
                 buf[q, c, pl.ds(row0 - 2 * factor, 2 * factor), :] = low[q, rows, :]
                 buf[q, c, pl.ds(row0 + n, 2 * factor), :] = high[q, rows, :]
 
-    loop(19, lambda q: one(q, lambda j: own[q, :, pl.ds(j * LANES, LANES)]))
-    one(19, lambda j: solid[:, pl.ds(j * LANES, LANES)].astype(F32))
+    loop(20, lambda q: one(q, lambda j: own[q, :, pl.ds(j * LANES, LANES)]))
 
 
 def store_level(level, buf, row0, out):
@@ -486,13 +530,31 @@
     row_loop(start, groups, body)
 
 
-def load_zone(level, zone, zero_row, center, left, right):
+PLANES = 15
+CENTER_ROWS = (PLANES + 1) * (OWN[2] + 2)
+
+
+def load_zone(level, zone, zero_row, center, left, right, start, rows):
     n = OWN[level]
-    zone[...] = jnp.zeros(zone.shape, F32)
-    for q in range(20):
-        zone[q, pl.ds(zero_row - 1, n + 2), :] = center[pl.ds(q * 34, n + 2), :]
-        zone[q, pl.ds(zero_row - 7, 8), :] += left[q]
-        zone[q, pl.ds(zero_row + n - 1, 8), :] += right[q]
+
+    def scoped(planes):
+        planes[...] = jnp.zeros(planes.shape, F32)
+        for p in range(PLANES + 1):
+            planes[p, pl.ds(zero_row - 1, n + 2), :] = center[pl.ds(p * (OWN[2] + 2), n + 2), :]
+            planes[p, pl.ds(zero_row - 7, 8), :] += left[p]
+            planes[p, pl.ds(zero_row + n - 1, 8), :] += right[p]
+        folded = None
+        for k in range(3):
+            part = jnp.concatenate([planes[3 * j + k, pl.ds(start, rows), :] for j in range(5)], axis=0)
+            total = moved(part, unpack_matrix(level, k))
+            for j in range(5):
+                zone[3 * j + k, pl.ds(start, rows), :] = total[rows * j : rows * (j + 1), :LANES]
+            folded = total[:, LANES:] if folded is None else folded + total[:, LANES:]
+        for j in range(4):
+            zone[PLANES + j, pl.ds(start, rows), :] = folded[rows * j : rows * (j + 1)]
+        zone[19, pl.ds(start, rows), :] = planes[PLANES, pl.ds(start, rows), :]
+
+    pl.run_scoped(scoped, pltpu.VMEM((PLANES + 1, *zone.shape[1:]), F32))
 
 
 def convert_zone(level, zone, start, groups, rim, out):
@@ -513,14 +575,15 @@
     value = moved(converted[...].reshape(19 * rows, LANES), matrix)
     for c in range(CHUNKS[child]):
         part = value[:, c * LANES : (c + 1) * LANES].reshape(19, rows, LANES)
-        spread[pl.ds(0, 19)] = part
+        if count < rows:
+            spread[pl.ds(0, 19)] = part
         for q in range(19):
-            t = spread[q, pl.ds(skip, count), :]
+            t = part[q] if count == rows else spread[q, pl.ds(skip, count), :]
             wide[q, c, pl.ds(first, count, stride=2), :] = t
             wide[q, c, pl.ds(first + 1, count, stride=2), :] = t
 
 
-def start_kernel(own, solid, to_right, to_left, center, to_zone_right, to_zone_left):
+def start_kernel(own, to_right, to_left, center, to_zone_right, to_zone_left):
     me = lax.axis_index("level")
 
     def halo(q, source):
@@ -528,58 +591,76 @@
             to_left[q, pl.ds(j, 2, stride=8), :] = source(pl.ds(0, 2), j)
             to_right[q, pl.ds(j, 2, stride=8), :] = source(pl.ds(SLAB - 2, 2), j)
 
-    loop(19, lambda q: halo(q, lambda rows, j: own[q, rows, pl.ds(j * LANES, LANES)]))
-    halo(19, lambda rows, j: solid[rows, pl.ds(j * LANES, LANES)].astype(F32))
+    loop(20, lambda q: halo(q, lambda rows, j: own[q, rows, pl.ds(j * LANES, LANES)]))
 
     for level in range(3):
 
         def push(level=level):
             n, row0, count, rows = OWN[level], ROW0[level], CHUNKS[level], ROWS[level]
+            span = max(n + 16, 32)
 
             def scoped(buf, post, packed):
                 post[...] = jnp.zeros(post.shape, F32)
                 buf[19] = jnp.zeros(buf.shape[1:], F32)
-                load_level(level, own, solid, None, None, buf)
+                load_level(level, own, None, None, buf)
                 collide_rows(level, buf, buf, None, post, row0, n // 8)
                 pull_rows(level, post, buf, row0 - 8, n // 8 + 2)
-                total = None
+                def spanned(first, many, c):
+                    return buf[pl.ds(first, many), c, pl.ds(row0 - 8, span), :].reshape(many * span, LANES)
+
+                main = folded = flags = None
                 for c in range(count):
-                    part = buf[:, c, pl.ds(row0 - 8, n + 16), :].reshape(20 * (n + 16), LANES)
-                    part = moved(part, pack_chunk(level, c))
-                    total = part if total is None else total + part
-                packed[...] = total.reshape(20, n + 16, LANES)
-                for q in range(20):
-                    center[pl.ds(q * 34, n + 2), :] = packed[q, pl.ds(7, n + 2), :]
-                    to_zone_right[q] = packed[q, pl.ds(n + 1, 8), :]
-                    to_zone_left[q] = packed[q, pl.ds(7, 8), :]
+                    part = moved(spanned(0, PLANES, c), pack_chunk(level, c))
+                    main = part if main is None else main + part
+                    part = moved(spanned(PLANES, 4, c), fold_chunk(level, c))
+                    folded = part if folded is None else folded + part
+                    part = moved(spanned(19, 1, c), flag_chunk(level, c))
+                    flags = part if flags is None else flags + part
+                for p in range(PLANES):
+                    j, k = divmod(p, 3)
+                    part = main[span * p : span * (p + 1)]
+                    if j < 4:
+                        part = part + folded[span * j : span * (j + 1), LANES * k : LANES * (k + 1)]
+                    packed[p] = part
+                packed[PLANES] = flags
+                for p in range(PLANES + 1):
+                    center[pl.ds(p * (OWN[2] + 2), n + 2), :] = packed[p, pl.ds(7, n + 2), :]
+                    to_zone_right[p] = packed[p, pl.ds(n + 1, 8), :]
+                    to_zone_left[p] = packed[p, pl.ds(7, 8), :]
 
             pl.run_scoped(
                 scoped,
                 pltpu.VMEM((20, count, rows, LANES), F32),
                 pltpu.VMEM((19, count, rows, LANES), F32),
-                pltpu.VMEM((20, n + 16, LANES), F32),
+                pltpu.VMEM((PLANES + 1, span, LANES), F32),
             )
 
         pl.when(me == level)(push)
 
 
-def pack_flows(post, start, out, first):
+def pack_flows(post, out, row):
     lane = lanes()
-
-    def body(i):
-        row = pl.multiple_of(8 * i, 8)
-        total = jnp.zeros((8, LANES), F32)
-        for k, q in enumerate(Z_OUT):
-            v = pltpu.roll(post[q, pl.ds(start + row, 8), :], (16 * k - zone_lane(2, 8, 1)) % LANES, 1)
-            total = jnp.where((lane >= 16 * k) & (lane < 16 * k + 16), v, total)
-        for group, y, base in ((Y_DOWN, 8, 80), (Y_UP, 23, 85)):
-            for k, q in enumerate(group):
-                lane0 = base + k
-                v = pltpu.roll(post[q, pl.ds(start + row, 8), :], (lane0 - zone_lane(2, y, 0)) % LANES, 1)
-                total = jnp.where((lane == lane0) | (lane == lane0 + 25), v, total)
-        out[pl.ds(first + row, 8), :] = total
-
-    loop(6, body)
+    total = jnp.zeros((8, LANES), F32)
+    for k, q in enumerate(Z_OUT):
+        v = pltpu.roll(post[q], (16 * k - zone_lane(2, 8, 1)) % LANES, 1)
+        total = jnp.where((lane >= 16 * k) & (lane < 16 * k + 16), v, total)
+    for group, y, base in ((Y_DOWN, 8, 80), (Y_UP, 23, 85)):
+        for k, q in enumerate(group):
+            lane0 = base + k
+            v = pltpu.roll(post[q], (lane0 - zone_lane(2, y, 0)) % LANES, 1)
+            total = jnp.where((lane == lane0) | (lane == lane0 + 25), v, total)
+    out[pl.ds(pl.multiple_of(row, 8), 8), :] = total
+
+
+def pull_and_convert(zpost, zone, row, rim, converted):
+    scale = parent_scale(3)
+    v = zone_pulled(zpost, 2, row)
+    if zone is not None:
+        for q in range(19):
+            zone[q, pl.ds(row, 8), :] = v[q]
+    v = relax(v, 1.0 - scale, scale)
+    for q in range(19):
+        converted[q, pl.ds(pl.multiple_of(row - 8, 8), 8), :] = jnp.where(rim, v[q], 0.0)
 
 
 def finest_cycle(g, pa, pb, wide, first, groups):
@@ -595,12 +676,12 @@
     row_loop(first, groups, lambda row: substep(pulled(pa, 3, row, 0), row, pb))
 
 
-def finest_role(own, solid, low, high, center, left, right, g, zpost, flows):
+def finest_role(own, low, high, center, left, right, g, zpost, flows):
     def scoped(pa, pb, wide, zone, flat, spread, widen3, restrict3):
         widen3[...] = widen_matrix(3)
         restrict3[...] = restrict_chunk(3, 0)
-        load_level(3, own, solid, low, high, g)
-        load_zone(2, zone, 16, center, left, right)
+        load_level(3, own, low, high, g)
+        load_zone(2, zone, 16, center, left, right, 8, 48)
         covered, rim = zone_masks(2, 0)
         scale = child_scale(3)
 
@@ -611,16 +692,12 @@
             post = collided(v, zone[19, pl.ds(8 + row, 8), :], 2)
             for q in range(19):
                 zpost[q, pl.ds(8 + row, 8), :] = post[q]
-
-        def zone_pull(row):
-            v = zone_pulled(zpost, 2, row)
-            for q in range(19):
-                zone[q, pl.ds(row, 8), :] = v[q]
+            return post
 
         def interface():
-            convert_zone(2, zone, 8, 6, rim, flat)
             widen(flat, widen3[...], 3, 0, 48, wide, spread, PAD)
 
+        convert_zone(2, zone, 8, 6, rim, flat)
         interface()
         for cycle in range(3):
             first, groups = (PAD, 12) if cycle < 2 else (PAD + 8, 10)
@@ -635,10 +712,9 @@
             for q in range(19):
                 flat[q] = g[q, 0, pl.ds(PAD, 48, stride=2), :] + g[q, 0, pl.ds(PAD + 1, 48, stride=2), :]
             spread[...] = moved(flat[...].reshape(19 * 48, LANES), restrict3[...]).reshape(19, 48, LANES)
-            loop(6, restrict)
-            pack_flows(zpost, 8, flows, 48 * cycle)
+            loop(6, lambda i: pack_flows(restrict(i), flows, 48 * cycle + 8 * i))
             if cycle < 2:
-                row_loop(8, 6, zone_pull)
+                row_loop(8, 6, lambda row: pull_and_convert(zpost, zone, row, rim, flat))
                 interface()
 
     rows = ROWS[3]
@@ -660,16 +736,10 @@
 
     @pl.when(lax.axis_index("level") == 3)
     def _():
-        def scoped(pa, pb, wide, zone, flat, spread, out, pairs, value, scratch):
+        def scoped(pa, pb, wide, flat, spread, out, pairs, value, scratch):
             _, rim = zone_masks(2, 0)
 
-            def zone_pull(row):
-                v = zone_pulled(zpost, 2, row)
-                for q in range(19):
-                    zone[q, pl.ds(row, 8), :] = v[q]
-
-            row_loop(8, 6, zone_pull)
-            convert_zone(2, zone, 8, 6, rim, flat)
+            row_loop(8, 6, lambda row: pull_and_convert(zpost, None, row, rim, flat))
             widen(flat, widen_matrix(3), 3, 0, 48, wide, spread, PAD)
             finest_cycle(g, pa, pb, wide, PAD + 8, 10)
 
@@ -729,7 +799,6 @@
             pltpu.VMEM((19, 1, rows, LANES), F32),
             pltpu.VMEM((19, 1, rows, LANES), F32),
             pltpu.VMEM((19, 1, rows, LANES), F32),
-            pltpu.VMEM((19, 64, LANES), F32),
             pltpu.VMEM((19, 48, LANES), F32),
             pltpu.VMEM((20, 48, LANES), F32),
             pltpu.VMEM((19, 1, n, LANES), F32),
@@ -754,13 +823,13 @@
     return total.reshape(flat.shape[0], rows, LANES)
 
 
-def second_role(own, solid, low, high, center, left, right, keep_post, keep_wide, early, ring):
+def second_role(own, low, high, center, left, right, keep_post, keep_wide, early, ring):
     level, row0 = 2, ROW0[2]
     first = row0 - 8
 
     def scoped(g, wide, zone, zpost, conv, spread, flat):
-        load_level(level, own, solid, low, high, g)
-        load_zone(1, zone, 16, center, left, right)
+        load_level(level, own, low, high, g)
+        load_zone(1, zone, 16, center, left, right, 8, 32)
         covered, rim = zone_masks(1, 0)
         keep_post[19] = g[19]
         convert_zone(1, zone, 8, 4, rim, conv)
@@ -812,14 +881,15 @@
     )
 
 
-def first_role(own, solid, low, high, center, left, right, state, early):
+def first_role(own, low, high, center, left, right, state, early):
     level, row0, n = 1, ROW0[1], OWN[1]
     first = row0 - 8
 
     def scoped(g, post, wide, zone, conv, spread, flat):
-        load_level(level, own, solid, low, high, g)
-        load_zone(0, zone, 12, center, left, right)
-        convert_zone(0, zone, 8, 2, None, conv)
+        load_level(level, own, low, high, g)
+        load_zone(0, zone, 12, center, left, right, 8, 16)
+        y, z = zone_cell(0, lanes())
+        convert_zone(0, zone, 8, 2, (z == 7) | (y == Y_LOW) | (y == Y_HIGH), conv)
         widen(conv, widen_matrix(1), 1, 0, 16, wide, spread, first)
         collide_rows(level, g, g, wide, post, first, 4)
         pull_rows(level, post, g, first, 4)
@@ -846,11 +916,11 @@
     )
 
 
-def coarse_role(own, solid, low, high, state):
+def coarse_role(own, low, high, state):
     level, row0 = 0, ROW0[0]
 
     def scoped(g, post):
-        load_level(level, own, solid, low, high, g)
+        load_level(level, own, low, high, g)
         collide_rows(level, g, g, None, post, row0 - 8, 3)
         pull_rows(level, post, g, row0, 1)
         store_level(level, g, row0, state)
@@ -863,11 +933,11 @@
 
 
 def main_kernel(
-    own, solid, low, high, center, left, right,
+    own, low, high, center, left, right,
     state, fine, fine_post, flows, keep_post, keep_wide, early, ring,
 ):
     me = lax.axis_index("level")
-    arrived = (own, solid, low, high, center, left, right)
+    arrived = (own, low, high, center, left, right)
 
     @pl.when(me == 3)
     def _():
@@ -883,7 +953,7 @@
 
     @pl.when(me == 0)
     def _():
-        coarse_role(own, solid, low, high, state)
+        coarse_role(own, low, high, state)
 
 
 def flow_kernel(flows, keep_post, keep_wide, ring, result, late, late_mean):
@@ -966,7 +1036,7 @@
         )
 
 
-def finish_kernel(old_state, result, third_state, early, near, far, far_coarse, state):
+def finish_kernel(old_state, result, third_state, means, early, late, far, far_coarse, state):
     me = lax.axis_index("level")
 
     @pl.when(me == 3)
@@ -977,7 +1047,7 @@
     def _():
         def scoped(g, back):
             for i in range(4):
-                total = moved(near[...], spread_chunk(i))
+                total = moved(means[...], spread_chunk(i))
                 for c in range(2):
                     back[i, c] = total[:, c * LANES : (c + 1) * LANES].reshape(20, 8, LANES)
             for c in range(2):
@@ -1003,7 +1073,7 @@
             deep = deep_late(lane & 63)
             for q in range(19):
                 part = pltpu.roll(far[pl.ds(8 * (q // 8), 8), :], (4 - 8 * (q % 8)) % LANES, 1)
-                value[pl.ds(8 * q, 8), :] = jnp.where(deep, part, near[pl.ds(8 * q, 8), :])
+                value[pl.ds(8 * q, 8), :] = jnp.where(deep, part, late[pl.ds(8 * q, 8), :])
             value[pl.ds(152, 8), :] = jnp.zeros((8, LANES), F32)
             total = moved(early[...].reshape(19 * 16, LANES), spread_zone_matrix())
             for c in range(4):
@@ -1082,9 +1152,9 @@
 
 
 def shards(populations, solid):
-    own, flags = populations[0], solid[0]
-    if own.shape != (19, SLAB, NY * NZ):
+    if populations.shape[1:] != (19, SLAB, NY * NZ):
         raise ValueError("unexpected slab")
+    own = jnp.concatenate([populations[0], solid.astype(F32)], axis=0)
     blocks = lax.axis_size("blocks")
     forward = [(i, (i + 1) % blocks) for i in range(blocks)]
     backward = [(i, (i - 1) % blocks) for i in range(blocks)]
@@ -1100,8 +1170,8 @@
     both = ("level", "blocks")
     to_right, to_left, center, zone_right, zone_left = call(
         start_kernel,
-        [(20, 16, LANES), (20, 16, LANES), (680, LANES), (20, 8, LANES), (20, 8, LANES)],
-        [own, flags],
+        [(20, 16, LANES), (20, 16, LANES), (CENTER_ROWS, LANES), (PLANES + 1, 8, LANES), (PLANES + 1, 8, LANES)],
+        [own],
         1.5,
     )
     center = lax.ppermute(center, "level", down)
@@ -1123,7 +1193,7 @@
             (19, 16, LANES),
             (19, 8, LANES),
         ],
-        [own, flags, low, high, center, left, right],
+        [own, low, high, center, left, right],
         8.0,
     )
     flows = lax.ppermute(flows, "level", [(3, 2)])
@@ -1132,6 +1202,7 @@
         last_cycle_kernel, [full, (160, LANES), (40, LANES), (40, LANES)], [fine, fine_post], 4.0
     )
     far_coarse = lax.ppermute(far_coarse, "level", [(3, 0)])
+    means = lax.ppermute(means, "level", [(3, 2)])
     result, late, late_mean = call(
         flow_kernel,
         [(19, 2, OWN[2], LANES), (160, LANES), (40, LANES)],
@@ -1140,9 +1211,9 @@
     )
     me = lax.axis_index("level")
     far = lax.ppermute(jnp.where(me == 3, far_first, late_mean), "level", [(3, 1), (2, 0)])
-    near = lax.ppermute(jnp.where(me == 3, means, late), "level", [(3, 2), (2, 1)])
+    late = lax.ppermute(late, "level", [(2, 1)])
     (state,) = call(
-        finish_kernel, [full], [state, result, third_state, early, near, far, far_coarse], 1.0
+        finish_kernel, [full], [state, result, third_state, means, early, late, far, far_coarse], 1.0
     )
     return state[None]
 

time: 42.5 us -> 40.6 us (0.955)
  waiting for transfers between devices: 16.2 us -> 13.6 us
  other arithmetic: 0.02 us -> 1.89 us
  local copies, waits for them, and re-layouts: 1.84 us -> 0 us
    unnamed x8 -> x0, local copies, waits for them, and re-layouts: 1.84 us -> none
    ppermute x1, waiting for transfers between devices: 4.69 us -> 2.91 us  [shards(): lax.ppermute(jnp.where(me == 3, far_first, late_mean), 'level', [(3, 1),...]
    concatenate x0 -> x1, other arithmetic: none -> 1.12 us  [shards(): own = jnp.concatenate([populations[0], solid.astype(F32)], axis=0)]
    convert_element_type x0 -> x1, other arithmetic: none -> 0.76 us  [shards(): own = jnp.concatenate([populations[0], solid.astype(F32)], axis=0)]
    ppermute x1 -> x2, starting transfers between devices: 0.67 us -> 1.33 us  [the longest x1 0.67 us: shards(): means = lax.ppermute(means, 'level', [(3, 2)])]
    ppermute x1, waiting for transfers between devices: 9.43 us -> 8.8 us  [shards(): far_coarse = lax.ppermute(far_coarse, 'level', [(3, 0)])]
  transfers between devices with their start and end apart: 10 -> 11, of which waited for: 3 -> 3; matrix products, arithmetic and copies ran while one was open for 0% -> 0% of each run, Pallas kernels for 0% -> 0%
where the time goes in v4:
time: 40.6 us; the launch traced here: 40.2 us
  starting transfers between devices  20.5 us (50%)
  waiting for transfers between devices  13.6 us (33%)
  Pallas kernels  4.05 us (10%)
  other arithmetic  1.89 us (5%)
    ppermute x1, waiting for transfers between devices, shards(): far_coarse = lax.ppermute(far_coarse, 'level', [(3, 0)])  8.8 us
    ppermute x1, starting transfers between devices, shards(): right = lax.ppermute(zone_left, both, diagonal(-1))  5.44 us
    ppermute x1, starting transfers between devices, shards(): center = lax.ppermute(center, 'level', down)  4.61 us
    pallas_call x5, Pallas kernels, call(): pl.pallas_call(kernel, out_shape=[jax.ShapeDtypeStruct(s, F32) for s in s...  4.05 us
    ppermute x1, waiting for transfers between devices, shards(): lax.ppermute(jnp.where(me == 3, far_first, late_mean), 'level', [(3, 1),...  2.91 us
    ppermute x1, starting transfers between devices, shards(): high = lax.ppermute(to_left, 'blocks', backward)  2.63 us
    ppermute x1, starting transfers between devices, shards(): left = lax.ppermute(zone_right, both, diagonal(1))  1.92 us
    ppermute x1, waiting for transfers between devices, shards(): right = lax.ppermute(zone_left, both, diagonal(-1))  1.87 us
  transfers between devices with their start and end apart: 11, of which 3 were waited for; matrix products, arithmetic and copies ran while one was open for 0% of the time, Pallas kernels for 0%

profile of v4, /device:TPU:0, one launch (start us, length us, event | category | flops | bytes accessed | tf_op | source)
XLA Modules:
  0.0 40.2 jit_solution(4412753324974595694)
XLA Ops:
  0.0 0.8 %convert_element_type.3 = f32[1,8,1024]{2,1,0:T(8,128)S(1)} convert(s32[1,8,1024]{2,1,0:T(8,128)} %param.3) | non-fusion elementwise | flops 8192 | bytes 65536 | tf_op jit(solution)/shard_map/convert_element_type | solution.py:1157
  0.8 1.1 %pad_maximum_fusion.own = f32[20,8,1024]{2,1,0:T(8,128)S(1)} fusion(f32[1,8,1024]{2,1,0:T(8,128)S(1)} %convert_element_type.3, f32[19,8,1024]{2,1,0:T(8,128)} %bitcast.2), kind=kLoop, calls=%fused_computation | loop fusion | flops 163840 | bytes 1310720 | tf_op jit(solution)/shard_map/concatenate | solution.py:1157
  1.9 1.6 %shard_map.28 = (f32[20,16,128]{2,1,0:T(8,128)S(1)}, f32[20,16,128]{2,1,0:T(8,128)S(1)}, f32[544,128]{1,0:T(8,128)S(1)}, f32[16,8,128]{2,1,0:T(8,128)S(1)}, f32[16,8,128]{2,1,0:T(8,128)S(1)}) custom-call(f32[20,8,1024]{2,1,0:T(8,128)S(1)} %pad_maximum_fusion.own), custom_call_target="tpu_custom_call" | custom-call | flops 1500000000 | bytes 5400000 | tf_op jit(solution)/shard_map/pallas_call | solution.py:1142
  3.5 4.6 %collective-permute-start.2 = (f32[544,128]{1,0:T(8,128)S(1)}, f32[544,128]{1,0:T(8,128)S(1)}, u32[]{:S(2)}, u32[]{:S(2)}) collective-permute-start(f32[544,128]{1,0:T(8,128)S(1)} %get-tuple-element.27), channel_id=1, source_target_pairs={{0,8},{8,16},{16,24},{1,9},{9,17},{17,25},{2,10},{10,18},{18,26},{... | collective-permute-start | bytes 835592 | tf_op jit(solution)/shard_map/ppermute | solution.py:1177
  8.1 0.1 collective-permute-start
  8.2 2.6 %collective-permute-start.1 = (f32[20,16,128]{2,1,0:T(8,128)S(1)}, f32[20,16,128]{2,1,0:T(8,128)S(1)}, u32[]{:S(2)}, u32[]{:S(2)}) collective-permute-start(f32[20,16,128]{2,1,0:T(8,128)S(1)} %get-tuple-element.26), channel_id=1, source_target_pairs={{0,7},{1,0},{2,1},{3,2},{4,3},{5,4},{6,5},{7,6},{8,15},{9,8},{10,9... | collective-permute-start | bytes 491528 | tf_op jit(solution)/shard_map/ppermute | solution.py:1181
  10.8 1.9 %collective-permute-start.3 = (f32[16,8,128]{2,1,0:T(8,128)S(1)}, f32[16,8,128]{2,1,0:T(8,128)S(1)}, u32[]{:S(2)}, u32[]{:S(2)}) collective-permute-start(f32[16,8,128]{2,1,0:T(8,128)S(1)} %get-tuple-element.28), channel_id=1, source_target_pairs={{0,9},{1,10},{2,11},{3,12},{4,13},{5,14},{6,15},{7,8},{8,17},{9,18... | collective-permute-start | bytes 196616 | tf_op jit(solution)/shard_map/ppermute | solution.py:1178
  12.8 5.4 %collective-permute-start.4 = (f32[16,8,128]{2,1,0:T(8,128)S(1)}, f32[16,8,128]{2,1,0:T(8,128)S(1)}, u32[]{:S(2)}, u32[]{:S(2)}) collective-permute-start(f32[16,8,128]{2,1,0:T(8,128)S(1)} %get-tuple-element.29), channel_id=1, source_target_pairs={{0,15},{1,8},{2,9},{3,10},{4,11},{5,12},{6,13},{7,14},{8,23},{9,16... | collective-permute-start | bytes 196616 | tf_op jit(solution)/shard_map/ppermute | solution.py:1179
  18.2 0.0 collective-permute-done.3.left
  18.2 1.9 %collective-permute-done.4.right = f32[16,8,128]{2,1,0:T(8,128)S(1)} collective-permute-done((f32[16,8,128]{2,1,0:T(8,128)S(1)}, f32[16,8,128]{2,1,0:T(8,128)S(1)}, u32[]{:S(2)}, u32[]{:S(2)}) %collective-permute-start.4) | collective-permute-done | bytes 65568 | tf_op jit(solution)/shard_map/ppermute | solution.py:1179
  20.1 0.0 collective-permute-done.low
  20.1 0.0 collective-permute-done.1.high
  20.1 0.0 collective-permute-done.2.center
  20.1 1.1 %shard_map.29 = (f32[19,8,1024]{2,1,0:T(8,128)S(1)}, f32[20,1,112,128]{3,2,1,0:T(8,128)S(1)}, f32[19,64,128]{2,1,0:T(8,128)S(1)}, f32[144,128]{1,0:T(8,128)S(1)}...) custom-call(f32[20,8,1024]{2,1,0:T(8,128)S(1)} %pad_maximum_fusion.o, ...), custom_call_target="tpu_custom_call" | custom-call | flops 8000000000 | bytes 28800000 | tf_op jit(solution)/shard_map/pallas_call | solution.py:1142
  21.2 0.7 %collective-permute-start.5 = (f32[144,128]{1,0:T(8,128)S(1)}, f32[144,128]{1,0:T(8,128)S(1)}, u32[]{:S(2)}, u32[]{:S(2)}) collective-permute-start(f32[144,128]{1,0:T(8,128)S(1)} %get-tuple-element.31), channel_id=1, source_target_pairs={{24,16},{25,17},{26,18},{27,19},{28,20},{29,21},{30,22},{31,23}} | collective-permute-start | bytes 221192 | tf_op jit(solution)/shard_map/ppermute | solution.py:1199
  21.9 0.7 %collective-permute-start.6 = (f32[160,128]{1,0:T(8,128)S(1)}, f32[160,128]{1,0:T(8,128)S(1)}, u32[]{:S(2)}, u32[]{:S(2)}) collective-permute-start(f32[160,128]{1,0:T(8,128)S(1)} %get-tuple-element.39), channel_id=1, source_target_pairs={{24,16},{25,17},{26,18},{27,19},{28,20},{29,21},{30,22},{31,23}} | collective-permute-start | bytes 245768 | tf_op jit(solution)/shard_map/ppermute | solution.py:1205
  22.6 1.3 %collective-permute-start.10 = (f32[40,128]{1,0:T(8,128)S(1)}, f32[40,128]{1,0:T(8,128)S(1)}, u32[]{:S(2)}, u32[]{:S(2)}) collective-permute-start(f32[40,128]{1,0:T(8,128)S(1)} %get-tuple-element.44), channel_id=1, source_target_pairs={{24,0},{25,1},{26,2},{27,3},{28,4},{29,5},{30,6},{31,7}} | collective-permute-start | bytes 61448 | tf_op jit(solution)/shard_map/ppermute | solution.py:1204
  23.9 1.3 %collective-permute-start.7 = (f32[19,16,128]{2,1,0:T(8,128)S(1)}, f32[19,16,128]{2,1,0:T(8,128)S(1)}, u32[]{:S(2)}, u32[]{:S(2)}) collective-permute-start(f32[19,16,128]{2,1,0:T(8,128)S(1)} %get-tuple-element.40), channel_id=1, source_target_pairs={{16,8},{8,0},{17,9},{9,1},{18,10},{10,2},{19,11},{11,3},{20,12},{1... | collective-permute-start | bytes 466952 | tf_op jit(solution)/shard_map/ppermute | solution.py:1200
  25.2 0.0 collective-permute-done.5.flows
  25.2 0.7 %collective-permute-start.8 = (f32[160,128]{1,0:T(8,128)S(1)}, f32[160,128]{1,0:T(8,128)S(1)}, u32[]{:S(2)}, u32[]{:S(2)}) collective-permute-start(f32[160,128]{1,0:T(8,128)S(1)} %get-tuple-element.41), channel_id=1, source_target_pairs={{16,8},{17,9},{18,10},{19,11},{20,12},{21,13},{22,14},{23,15}} | collective-permute-start | bytes 245768 | tf_op jit(solution)/shard_map/ppermute | solution.py:1214
  25.9 1.3 %collective-permute-start.9 = (f32[40,128]{1,0:T(8,128)S(1)}, f32[40,128]{1,0:T(8,128)S(1)}, u32[]{:S(2)}, u32[]{:S(2)}) collective-permute-start(f32[40,128]{1,0:T(8,128)S(1)} %broadcast_select_fusion), channel_id=1, source_target_pairs={{24,8},{16,0},{25,9},{17,1},{26,10},{18,2},{27,11},{19,3},{28,12},... | collective-permute-start | bytes 61448 | tf_op jit(solution)/shard_map/ppermute | solution.py:1213
  27.2 8.8 %collective-permute-done.10.far_coarse = f32[40,128]{1,0:T(8,128)S(1)} collective-permute-done((f32[40,128]{1,0:T(8,128)S(1)}, f32[40,128]{1,0:T(8,128)S(1)}, u32[]{:S(2)}, u32[]{:S(2)}) %collective-permute-start.10) | collective-permute-done | bytes 20512 | tf_op jit(solution)/shard_map/ppermute | solution.py:1204
  36.0 0.0 collective-permute-done.6.means
  36.0 2.9 %collective-permute-done.9.far = f32[40,128]{1,0:T(8,128)S(1)} collective-permute-done((f32[40,128]{1,0:T(8,128)S(1)}, f32[40,128]{1,0:T(8,128)S(1)}, u32[]{:S(2)}, u32[]{:S(2)}) %collective-permute-start.9) | collective-permute-done | bytes 20512 | tf_op jit(solution)/shard_map/ppermute | solution.py:1213
  39.0 0.0 collective-permute-done.8.late
  39.0 0.0 collective-permute-done.7.early
  39.0 1.3 %shard_map.32 = f32[19,8,1024]{2,1,0:T(8,128)} custom-call(f32[19,8,1024]{2,1,0:T(8,128)S(1)} %get-tuple-element.30.old_state, f32[19,2,32,128]{3,2,1,0:T(8,128)S(1)} %get-tuple-element.35.result, f32[19,8,1024]{2,1,0:T(8,128)S(1)} %get-tuple-element.38.third_state, f32[160,128]{1,0:T(8,128)S(1)} %collective-permute-done.6.means, ...), custom_call_target="tpu_custom_call" | custom-call | flops 1000000000 | bytes 3600000 | tf_op jit(solution)/shard_map/pallas_call | solution.py:1142
  (3 shorter events, 0.0 us)
Async XLA Ops:
  3.5 16.6 %collective-permute-start.2 = (f32[544,128]{1,0:T(8,128)S(1)}, f32[544,128]{1,0:T(8,128)S(1)}, u32[]{:S(2)}, u32[]{:S(2)}) collective-permute-start(f32[544,128]{1,0:T(8,128)S(1)} %get-tuple-element.27), channel_id=1, source_target_pairs={{0,8},{8,16},{16,24},{1,9},{9,17},{17,25},{2,10},{10,18},{18,26},{... | collective-permute-start | bytes 835592 | tf_op jit(solution)/shard_map/ppermute | solution.py:1177
  8.1 12.0 %collective-permute-start = (f32[20,16,128]{2,1,0:T(8,128)S(1)}, f32[20,16,128]{2,1,0:T(8,128)S(1)}, u32[]{:S(2)}, u32[]{:S(2)}) collective-permute-start(f32[20,16,128]{2,1,0:T(8,128)S(1)} %get-tuple-element.25), channel_id=1, source_target_pairs={{0,1},{1,2},{2,3},{3,4},{4,5},{5,6},{6,7},{7,0},{8,9},{9,10},{10,1... | collective-permute-start | bytes 491528 | tf_op jit(solution)/shard_map/ppermute | solution.py:1180
  8.2 11.9 %collective-permute-start.1 = (f32[20,16,128]{2,1,0:T(8,128)S(1)}, f32[20,16,128]{2,1,0:T(8,128)S(1)}, u32[]{:S(2)}, u32[]{:S(2)}) collective-permute-start(f32[20,16,128]{2,1,0:T(8,128)S(1)} %get-tuple-element.26), channel_id=1, source_target_pairs={{0,7},{1,0},{2,1},{3,2},{4,3},{5,4},{6,5},{7,6},{8,15},{9,8},{10,9... | collective-permute-start | bytes 491528 | tf_op jit(solution)/shard_map/ppermute | solution.py:1181
  10.8 7.4 %collective-permute-start.3 = (f32[16,8,128]{2,1,0:T(8,128)S(1)}, f32[16,8,128]{2,1,0:T(8,128)S(1)}, u32[]{:S(2)}, u32[]{:S(2)}) collective-permute-start(f32[16,8,128]{2,1,0:T(8,128)S(1)} %get-tuple-element.28), channel_id=1, source_target_pairs={{0,9},{1,10},{2,11},{3,12},{4,13},{5,14},{6,15},{7,8},{8,17},{9,18... | collective-permute-start | bytes 196616 | tf_op jit(solution)/shard_map/ppermute | solution.py:1178
  12.8 7.3 %collective-permute-start.4 = (f32[16,8,128]{2,1,0:T(8,128)S(1)}, f32[16,8,128]{2,1,0:T(8,128)S(1)}, u32[]{:S(2)}, u32[]{:S(2)}) collective-permute-start(f32[16,8,128]{2,1,0:T(8,128)S(1)} %get-tuple-element.29), channel_id=1, source_target_pairs={{0,15},{1,8},{2,9},{3,10},{4,11},{5,12},{6,13},{7,14},{8,23},{9,16... | collective-permute-start | bytes 196616 | tf_op jit(solution)/shard_map/ppermute | solution.py:1179
  21.2 4.0 %collective-permute-start.5 = (f32[144,128]{1,0:T(8,128)S(1)}, f32[144,128]{1,0:T(8,128)S(1)}, u32[]{:S(2)}, u32[]{:S(2)}) collective-permute-start(f32[144,128]{1,0:T(8,128)S(1)} %get-tuple-element.31), channel_id=1, source_target_pairs={{24,16},{25,17},{26,18},{27,19},{28,20},{29,21},{30,22},{31,23}} | collective-permute-start | bytes 221192 | tf_op jit(solution)/shard_map/ppermute | solution.py:1199
  21.9 14.1 %collective-permute-start.6 = (f32[160,128]{1,0:T(8,128)S(1)}, f32[160,128]{1,0:T(8,128)S(1)}, u32[]{:S(2)}, u32[]{:S(2)}) collective-permute-start(f32[160,128]{1,0:T(8,128)S(1)} %get-tuple-element.39), channel_id=1, source_target_pairs={{24,16},{25,17},{26,18},{27,19},{28,20},{29,21},{30,22},{31,23}} | collective-permute-start | bytes 245768 | tf_op jit(solution)/shard_map/ppermute | solution.py:1205
  22.6 13.4 %collective-permute-start.10 = (f32[40,128]{1,0:T(8,128)S(1)}, f32[40,128]{1,0:T(8,128)S(1)}, u32[]{:S(2)}, u32[]{:S(2)}) collective-permute-start(f32[40,128]{1,0:T(8,128)S(1)} %get-tuple-element.44), channel_id=1, source_target_pairs={{24,0},{25,1},{26,2},{27,3},{28,4},{29,5},{30,6},{31,7}} | collective-permute-start | bytes 61448 | tf_op jit(solution)/shard_map/ppermute | solution.py:1204
  23.9 15.1 %collective-permute-start.7 = (f32[19,16,128]{2,1,0:T(8,128)S(1)}, f32[19,16,128]{2,1,0:T(8,128)S(1)}, u32[]{:S(2)}, u32[]{:S(2)}) collective-permute-start(f32[19,16,128]{2,1,0:T(8,128)S(1)} %get-tuple-element.40), channel_id=1, source_target_pairs={{16,8},{8,0},{17,9},{9,1},{18,10},{10,2},{19,11},{11,3},{20,12},{1... | collective-permute-start | bytes 466952 | tf_op jit(solution)/shard_map/ppermute | solution.py:1200
  25.2 13.7 %collective-permute-start.8 = (f32[160,128]{1,0:T(8,128)S(1)}, f32[160,128]{1,0:T(8,128)S(1)}, u32[]{:S(2)}, u32[]{:S(2)}) collective-permute-start(f32[160,128]{1,0:T(8,128)S(1)} %get-tuple-element.41), channel_id=1, source_target_pairs={{16,8},{17,9},{18,10},{19,11},{20,12},{21,13},{22,14},{23,15}} | collective-permute-start | bytes 245768 | tf_op jit(solution)/shard_map/ppermute | solution.py:1214
  25.9 13.0 %collective-permute-start.9 = (f32[40,128]{1,0:T(8,128)S(1)}, f32[40,128]{1,0:T(8,128)S(1)}, u32[]{:S(2)}, u32[]{:S(2)}) collective-permute-start(f32[40,128]{1,0:T(8,128)S(1)} %broadcast_select_fusion), channel_id=1, source_target_pairs={{24,8},{16,0},{25,9},{17,1},{26,10},{18,2},{27,11},{19,3},{28,12},... | collective-permute-start | bytes 61448 | tf_op jit(solution)/shard_map/ppermute | solution.py:1213

commit v5 on v4

--- a/solution.py
+++ b/solution.py
@@ -305,9 +305,14 @@
     return mask
 
 
-def flow_chunk(q):
-    def holds(row, column):
-        y, z = cell_of(2, column)
+FLOW_CHUNKS = tuple(
+    (q, c) for q in FLOW_DIRECTIONS for c in range(2) if q in Z_OUT or q in (Y_DOWN, Y_UP)[c]
+)
+
+
+def flow_chunk(q, c):
+    def holds(row, column):
+        y, z = cell_of(2, column + c * LANES)
         source = None
         if q in Y_DOWN:
             source = 80 + Y_DOWN.index(q) + 25 * z
@@ -318,7 +323,7 @@
             source = over if source is None else jnp.where(z == 1, over, source)
         return flow_mask(q, y, z) & (row == source)
 
-    return made(2 * LANES, 1.0, holds)
+    return made(LANES, 1.0, holds)
 
 
 def relaxation(level_id):
@@ -389,35 +394,42 @@
     return mask
 
 
-def pulled(post, level, row, c):
+def pulled(post, level, row, chunks, interface_next=False):
     lane = lanes()
     nz, count = DEPTH[level], CHUNKS[level]
-    out = []
+    out = [[] for _ in chunks]
     for q in range(19):
         cx, cy, cz = VELOCITY[q]
         shift = cy * nz + cz
-        value = post[q, c, pl.ds(row - cx, 8), :]
-        if shift != 0:
-            value = pltpu.roll(value, shift % LANES, 1)
+        rolled = {}
+
+        def moved_chunk(c):
+            if c not in rolled:
+                value = post[q, c, pl.ds(row - cx, 8), :]
+                rolled[c] = pltpu.roll(value, shift % LANES, 1) if shift != 0 else value
+            return rolled[c]
+
+        for place, c in enumerate(chunks):
+            value = moved_chunk(c)
             outside = None
             if cy == 1:
                 if c > 0:
-                    other = pltpu.roll(post[q, c - 1, pl.ds(row - cx, 8), :], shift, 1)
-                    value = jnp.where(lane < shift, other, value)
+                    value = jnp.where(lane < shift, moved_chunk(c - 1), value)
                 else:
                     outside = lane < nz
             if cy == -1:
                 if c < count - 1:
-                    other = pltpu.roll(post[q, c + 1, pl.ds(row - cx, 8), :], shift % LANES, 1)
-                    value = jnp.where(lane >= LANES + shift, other, value)
+                    value = jnp.where(lane >= LANES + shift, moved_chunk(c + 1), value)
                 else:
                     outside = lane >= LANES - nz
             if cz != 0:
                 edge = (lane & (nz - 1)) == (0 if cz == 1 else nz - 1)
                 outside = edge if outside is None else outside | edge
+            if interface_next:
+                outside = (lane & (nz - 1)) == 0 if cz == 1 else None
             if outside is not None:
                 value = jnp.where(outside, post[OPPOSITE[q], c, pl.ds(row, 8), :], value)
-        out.append(value)
+            out[place].append(value)
     return out
 
 
@@ -522,10 +534,12 @@
 
 def pull_rows(level, post, dest, start, groups):
     def body(row):
-        for c in range(CHUNKS[level]):
-            v = pulled(post, level, row, c)
-            for q in range(19):
-                dest[q, c, pl.ds(row, 8), :] = v[q]
+        step = min(2, CHUNKS[level])
+        for first in range(0, CHUNKS[level], step):
+            chunks = range(first, first + step)
+            for c, v in zip(chunks, pulled(post, level, row, chunks)):
+                for q in range(19):
+                    dest[q, c, pl.ds(row, 8), :] = v[q]
 
     row_loop(start, groups, body)
 
@@ -649,18 +663,46 @@
             lane0 = base + k
             v = pltpu.roll(post[q], (lane0 - zone_lane(2, y, 0)) % LANES, 1)
             total = jnp.where((lane == lane0) | (lane == lane0 + 25), v, total)
-    out[pl.ds(pl.multiple_of(row, 8), 8), :] = total
-
-
-def pull_and_convert(zpost, zone, row, rim, converted):
+    out[pl.ds(row, 8), :] = total
+
+
+def interface_values(zpost, zone, rim, matrix, wide):
     scale = parent_scale(3)
-    v = zone_pulled(zpost, 2, row)
-    if zone is not None:
+    for i in range(3):
+        halves = []
+        for half in range(2):
+            rows = pl.ds(8 + 16 * i + 8 * half, 8)
+            if zpost is None:
+                v = [zone[q, rows, :] for q in range(19)]
+            else:
+                v = zone_pulled(zpost, 2, 8 + 16 * i + 8 * half)
+                if zone is not None:
+                    for q in range(19):
+                        zone[q, rows, :] = v[q]
+            v = relax(v, 1.0 - scale, scale)
+            halves.append([jnp.where(rim, v[q], 0.0) for q in range(19)])
+        part = jnp.concatenate([halves[half][q] for q in range(19) for half in range(2)], axis=0)
+        total = moved(part, matrix[...])
         for q in range(19):
-            zone[q, pl.ds(row, 8), :] = v[q]
-    v = relax(v, 1.0 - scale, scale)
-    for q in range(19):
-        converted[q, pl.ds(pl.multiple_of(row - 8, 8), 8), :] = jnp.where(rim, v[q], 0.0)
+            t = total[16 * q : 16 * q + 16]
+            wide[q, 0, pl.ds(PAD + 32 * i, 16, stride=2), :] = t
+            wide[q, 0, pl.ds(PAD + 32 * i + 1, 16, stride=2), :] = t
+
+
+def restrict_and_collide(g, zone, covered, matrix, zpost, flows, first):
+    scale = child_scale(3)
+    for i in range(3):
+        even, odd = pl.ds(PAD + 32 * i, 16, stride=2), pl.ds(PAD + 32 * i + 1, 16, stride=2)
+        part = jnp.concatenate([g[q, 0, even, :] + g[q, 0, odd, :] for q in range(19)], axis=0)
+        total = moved(part, matrix[...])
+        for half in range(2):
+            rows = pl.ds(8 + 16 * i + 8 * half, 8)
+            v = relax([total[16 * q + 8 * half : 16 * q + 8 * half + 8] for q in range(19)], 1.0 - scale, scale)
+            v = [jnp.where(covered, v[q], zone[q, rows, :]) for q in range(19)]
+            post = collided(v, zone[19, rows, :], 2)
+            for q in range(19):
+                zpost[q, rows, :] = post[q]
+            pack_flows(post, flows, first + 16 * i + 8 * half)
 
 
 def finest_cycle(g, pa, pb, wide, first, groups):
@@ -673,49 +715,30 @@
             dest[q, 0, pl.ds(row, 8), :] = post[q]
 
     row_loop(first, groups, lambda row: substep([g[q, 0, pl.ds(row, 8), :] for q in range(19)], row, pa))
-    row_loop(first, groups, lambda row: substep(pulled(pa, 3, row, 0), row, pb))
+    row_loop(first, groups, lambda row: substep(pulled(pa, 3, row, [0], True)[0], row, pb))
 
 
 def finest_role(own, low, high, center, left, right, g, zpost, flows):
-    def scoped(pa, pb, wide, zone, flat, spread, widen3, restrict3):
+    def scoped(pa, pb, wide, zone, widen3, restrict3):
         widen3[...] = widen_matrix(3)
         restrict3[...] = restrict_chunk(3, 0)
         load_level(3, own, low, high, g)
         load_zone(2, zone, 16, center, left, right, 8, 48)
         covered, rim = zone_masks(2, 0)
-        scale = child_scale(3)
-
-        def restrict(i):
-            row = pl.multiple_of(8 * i, 8)
-            v = relax([spread[q, pl.ds(row, 8), :] for q in range(19)], 1.0 - scale, scale)
-            v = [jnp.where(covered, v[q], zone[q, pl.ds(8 + row, 8), :]) for q in range(19)]
-            post = collided(v, zone[19, pl.ds(8 + row, 8), :], 2)
-            for q in range(19):
-                zpost[q, pl.ds(8 + row, 8), :] = post[q]
-            return post
-
-        def interface():
-            widen(flat, widen3[...], 3, 0, 48, wide, spread, PAD)
-
-        convert_zone(2, zone, 8, 6, rim, flat)
-        interface()
+        interface_values(None, zone, rim, widen3, wide)
         for cycle in range(3):
             first, groups = (PAD, 12) if cycle < 2 else (PAD + 8, 10)
 
             def step_out(row):
-                v = pulled(pb, 3, row, 0)
+                v = pulled(pb, 3, row, [0])[0]
                 for q in range(19):
                     g[q, 0, pl.ds(row, 8), :] = v[q]
 
             finest_cycle(g, pa, pb, wide, first, groups)
             row_loop(first, groups, step_out)
-            for q in range(19):
-                flat[q] = g[q, 0, pl.ds(PAD, 48, stride=2), :] + g[q, 0, pl.ds(PAD + 1, 48, stride=2), :]
-            spread[...] = moved(flat[...].reshape(19 * 48, LANES), restrict3[...]).reshape(19, 48, LANES)
-            loop(6, lambda i: pack_flows(restrict(i), flows, 48 * cycle + 8 * i))
+            restrict_and_collide(g, zone, covered, restrict3, zpost, flows, 48 * cycle)
             if cycle < 2:
-                row_loop(8, 6, lambda row: pull_and_convert(zpost, zone, row, rim, flat))
-                interface()
+                interface_values(zpost, zone, rim, widen3, wide)
 
     rows = ROWS[3]
     pl.run_scoped(
@@ -724,27 +747,30 @@
         pltpu.VMEM((19, 1, rows, LANES), F32),
         pltpu.VMEM((19, 1, rows, LANES), F32),
         pltpu.VMEM((20, 64, LANES), F32),
-        pltpu.VMEM((19, 48, LANES), F32),
-        pltpu.VMEM((19, 48, LANES), F32),
         pltpu.VMEM((2 * LANES, LANES), BF16),
         pltpu.VMEM((2 * LANES, LANES), BF16),
     )
 
 
-def last_cycle_kernel(g, zpost, state, means, far_first, far_coarse):
+def last_cycle_kernel(g, zpost, state, means, far_first, far_coarse, matrices):
     row0, n = ROW0[3], OWN[3]
 
+    @pl.when(lax.axis_index("level") == 2)
+    def _():
+        for k, (q, c) in enumerate(FLOW_CHUNKS):
+            matrices[:, pl.ds(k * LANES, LANES)] = flow_chunk(q, c)
+
     @pl.when(lax.axis_index("level") == 3)
     def _():
-        def scoped(pa, pb, wide, flat, spread, out, pairs, value, scratch):
+        def scoped(pa, pb, wide, flat, spread, out, pairs, value, scratch, widen3):
             _, rim = zone_masks(2, 0)
 
-            row_loop(8, 6, lambda row: pull_and_convert(zpost, None, row, rim, flat))
-            widen(flat, widen_matrix(3), 3, 0, 48, wide, spread, PAD)
+            widen3[...] = widen_matrix(3)
+            interface_values(zpost, None, rim, widen3, wide)
             finest_cycle(g, pa, pb, wide, PAD + 8, 10)
 
             def step_out(row):
-                v = pulled(pb, 3, row, 0)
+                v = pulled(pb, 3, row, [0])[0]
                 for q in range(19):
                     out[q, 0, pl.ds(row - row0, 8), :] = v[q]
 
@@ -805,6 +831,7 @@
             pltpu.VMEM((80, LANES), F32),
             pltpu.VMEM((160, LANES), F32),
             pltpu.VMEM((80, LANES), F32),
+            pltpu.VMEM((2 * LANES, LANES), BF16),
         )
 
 
@@ -956,24 +983,27 @@
         coarse_role(own, low, high, state)
 
 
-def flow_kernel(flows, keep_post, keep_wide, ring, result, late, late_mean):
+def flow_kernel(flows, keep_post, keep_wide, ring, matrices, result, late, late_mean):
     level, row0 = 2, ROW0[2]
     first = row0 - 8
 
     @pl.when(lax.axis_index("level") == 2)
     def _():
         def scoped(g, post, override, flat, value, scratch):
-            for k, q in enumerate(FLOW_DIRECTIONS):
-                total = moved(flows[...], flow_chunk(q))
-                for c in range(2):
-                    override[k, c] = total[:, c * LANES : (c + 1) * LANES]
+            total = moved(flows[...], matrices[...])
+            for k in range(len(FLOW_CHUNKS)):
+                override[k] = total[:, k * LANES : (k + 1) * LANES]
+            outward = []
+            for q, c in FLOW_CHUNKS:
+                y, z = cell_of(2, lanes() + c * LANES)
+                outward.append(flow_mask(q, y, z))
 
             def overridden(c, row, cycle, v):
-                y, z = cell_of(2, lanes() + c * LANES)
                 v = list(v)
-                for k, q in enumerate(FLOW_DIRECTIONS):
-                    value = override[k, c, pl.ds(48 * cycle + row - first, 8), :]
-                    v[q] = jnp.where(flow_mask(q, y, z), value, v[q])
+                for k, (q, chunk) in enumerate(FLOW_CHUNKS):
+                    if chunk == c:
+                        value = override[k, pl.ds(48 * cycle + row - first, 8), :]
+                        v[q] = jnp.where(outward[k], value, v[q])
                 return v
 
             masks = [interface_mask(level, c) for c in range(2)]
@@ -1002,8 +1032,7 @@
                 row_loop(first, 6, body)
 
             def last(row):
-                for c in range(2):
-                    v = pulled(post, level, row, c)
+                for c, v in enumerate(pulled(post, level, row, range(2))):
                     for q in range(19):
                         result[q, c, pl.ds(row - row0, 8), :] = v[q]
 
@@ -1029,80 +1058,28 @@
             scoped,
             pltpu.VMEM((19, 2, ROWS[2], LANES), F32),
             pltpu.VMEM((19, 2, ROWS[2], LANES), F32),
-            pltpu.VMEM((len(FLOW_DIRECTIONS), 2, 144, LANES), F32),
+            pltpu.VMEM((len(FLOW_CHUNKS), 144, LANES), F32),
             pltpu.VMEM((2, 20, 16, LANES), F32),
             pltpu.VMEM((19, 8, LANES), F32),
             pltpu.VMEM((20, 8, LANES), F32),
         )
 
 
-def finish_kernel(old_state, result, third_state, means, early, late, far, far_coarse, state):
+def prepare_kernel(early, far, far_coarse, means, covered, near):
     me = lax.axis_index("level")
 
-    @pl.when(me == 3)
-    def _():
-        state[...] = third_state[...]
-
     @pl.when(me == 2)
     def _():
-        def scoped(g, back):
-            for i in range(4):
-                total = moved(means[...], spread_chunk(i))
-                for c in range(2):
-                    back[i, c] = total[:, c * LANES : (c + 1) * LANES].reshape(20, 8, LANES)
+        for i in range(4):
+            total = moved(means[...], spread_chunk(i))
             for c in range(2):
-                y, z = cell_of(2, lanes() + c * LANES)
-                covered = (y >= Y_LOW) & (y <= Y_HIGH) & (z <= 1)
-
-                def insert(q, c=c, covered=covered):
-                    for i in range(4):
-                        rows = pl.ds(8 * i, 8)
-                        g[q, c, rows, :] = jnp.where(covered, back[i, c, q], result[q, c, rows, :])
-
-                loop(19, insert, 1)
-            store_level(2, g, 0, state)
-
-        pl.run_scoped(
-            scoped, pltpu.VMEM((19, 2, OWN[2], LANES), F32), pltpu.VMEM((4, 2, 20, 8, LANES), F32)
-        )
+                covered[2 * i + c] = total[:, c * LANES : (c + 1) * LANES]
 
     @pl.when(me == 1)
     def _():
-        def scoped(wide, inner, value):
-            lane = lanes()
-            deep = deep_late(lane & 63)
-            for q in range(19):
-                part = pltpu.roll(far[pl.ds(8 * (q // 8), 8), :], (4 - 8 * (q % 8)) % LANES, 1)
-                value[pl.ds(8 * q, 8), :] = jnp.where(deep, part, late[pl.ds(8 * q, 8), :])
-            value[pl.ds(152, 8), :] = jnp.zeros((8, LANES), F32)
-            total = moved(early[...].reshape(19 * 16, LANES), spread_zone_matrix())
-            for c in range(4):
-                wide[:, c] = total[:, c * LANES : (c + 1) * LANES].reshape(19, 16, LANES)
-            for half in range(2):
-                total = moved(value[...], late_back_chunk(half))
-                for c in range(2):
-                    part = total[:, c * LANES : (c + 1) * LANES].reshape(20, 8, LANES)
-                    inner[c, :, pl.ds(8 * half, 8), :] = part
-
-            def one(q):
-                for j in range(8):
-                    c = j % 4
-                    y, z = cell_of(1, lanes() + c * LANES)
-                    columns = pl.ds(j * LANES, LANES)
-                    rows = pl.ds(j // 4, 8, stride=2)
-                    value = jnp.where(near_first(y, z), wide[q, c, rows, :], old_state[q, :, columns])
-                    if c in (1, 2):
-                        value = jnp.where(covered_first(y, z), inner[c - 1, q, rows, :], value)
-                    state[q, :, columns] = value
-
-            loop(19, one)
-
-        pl.run_scoped(
-            scoped,
-            pltpu.VMEM((19, 4, 16, LANES), F32),
-            pltpu.VMEM((2, 20, 16, LANES), F32),
-            pltpu.VMEM((160, LANES), F32),
-        )
+        total = moved(early[...].reshape(19 * 16, LANES), spread_zone_matrix())
+        for c in range(4):
+            near[c] = total[:, c * LANES : (c + 1) * LANES]
 
     @pl.when(me == 0)
     def _():
@@ -1125,23 +1102,94 @@
             for q in range(19):
                 value[q] = v[q]
             total = moved(value[...].reshape(160, LANES), spread_covered_matrix())
+            for c in range(4):
+                covered[c] = total[:, c * LANES : (c + 1) * LANES]
+
+        pl.run_scoped(scoped, pltpu.VMEM((20, 8, LANES), F32))
+
+
+def finish_kernel(old_state, result, third_state, late, far, covered_values, near, state):
+    me = lax.axis_index("level")
+
+    @pl.when(me == 3)
+    def _():
+        state[...] = third_state[...]
+
+    @pl.when(me == 2)
+    def _():
+        def scoped(g):
+            for c in range(2):
+                y, z = cell_of(2, lanes() + c * LANES)
+                covered = (y >= Y_LOW) & (y <= Y_HIGH) & (z <= 1)
+
+                def insert(q, c=c, covered=covered):
+                    for i in range(4):
+                        rows = pl.ds(8 * i, 8)
+                        value = covered_values[2 * i + c, pl.ds(pl.multiple_of(8 * q, 8), 8), :]
+                        g[q, c, rows, :] = jnp.where(covered, value, result[q, c, rows, :])
+
+                loop(19, insert, 19)
+            store_level(2, g, 0, state)
+
+        pl.run_scoped(scoped, pltpu.VMEM((19, 2, OWN[2], LANES), F32))
+
+    @pl.when(me == 1)
+    def _():
+        def scoped(inner, value):
+            lane = lanes()
+            deep = deep_late(lane & 63)
             for q in range(19):
+                part = pltpu.roll(far[pl.ds(8 * (q // 8), 8), :], (4 - 8 * (q % 8)) % LANES, 1)
+                value[pl.ds(8 * q, 8), :] = jnp.where(deep, part, late[pl.ds(8 * q, 8), :])
+            value[pl.ds(152, 8), :] = jnp.zeros((8, LANES), F32)
+            for half in range(2):
+                total = moved(value[...], late_back_chunk(half))
+                for c in range(2):
+                    part = total[:, c * LANES : (c + 1) * LANES].reshape(20, 8, LANES)
+                    inner[c, :, pl.ds(8 * half, 8), :] = part
+
+            def one(q):
                 for j in range(8):
+                    c = j % 4
+                    y, z = cell_of(1, lanes() + c * LANES)
                     columns = pl.ds(j * LANES, LANES)
-                    if not 2 <= j < 6:
-                        state[q, :, columns] = old_state[q, :, columns]
-                    else:
-                        covered = (lane & 31) < 8
-                        part = total[8 * q : 8 * q + 8, (j - 2) * LANES : (j - 1) * LANES]
-                        state[q, :, columns] = jnp.where(covered, part, old_state[q, :, columns])
-
-        pl.run_scoped(scoped, pltpu.VMEM((20, 8, LANES), F32))
+                    rows = pl.ds(j // 4, 8, stride=2)
+                    ring = near[c, pl.ds(16 * q + j // 4, 8, stride=2), :]
+                    value = jnp.where(near_first(y, z), ring, old_state[q, :, columns])
+                    if c in (1, 2):
+                        value = jnp.where(covered_first(y, z), inner[c - 1, q, rows, :], value)
+                    state[q, :, columns] = value
+
+            loop(19, one)
+
+        pl.run_scoped(
+            scoped,
+            pltpu.VMEM((2, 20, 16, LANES), F32),
+            pltpu.VMEM((160, LANES), F32),
+        )
+
+    @pl.when(me == 0)
+    def _():
+        covered = (lanes() & 31) < 8
+
+        def one(q):
+            rows = pl.ds(pl.multiple_of(8 * q, 8), 8)
+            for j in range(8):
+                columns = pl.ds(j * LANES, LANES)
+                value = old_state[q, :, columns]
+                if 2 <= j < 6:
+                    value = jnp.where(covered, covered_values[j - 2, rows, :], value)
+                state[q, :, columns] = value
+
+        loop(19, one, 19)
 
 
 def call(kernel, shapes, args, micros):
     return pl.pallas_call(
         kernel,
-        out_shape=[jax.ShapeDtypeStruct(s, F32) for s in shapes],
+        out_shape=[
+            jax.ShapeDtypeStruct(s[:-1], BF16) if s[-1] is BF16 else jax.ShapeDtypeStruct(s, F32) for s in shapes
+        ],
         in_specs=[pl.BlockSpec(memory_space=pltpu.VMEM)] * len(args),
         out_specs=[pl.BlockSpec(memory_space=pltpu.VMEM)] * len(shapes),
         cost_estimate=pl.CostEstimate(
@@ -1198,22 +1246,28 @@
     )
     flows = lax.ppermute(flows, "level", [(3, 2)])
     early = lax.ppermute(early, "level", [(2, 1), (1, 0)])
-    third_state, means, far_first, far_coarse = call(
-        last_cycle_kernel, [full, (160, LANES), (40, LANES), (40, LANES)], [fine, fine_post], 4.0
+    third_state, means, far_first, far_coarse, matrices = call(
+        last_cycle_kernel,
+        [full, (160, LANES), (40, LANES), (40, LANES), (2 * LANES, len(FLOW_CHUNKS) * LANES, BF16)],
+        [fine, fine_post],
+        4.0,
     )
     far_coarse = lax.ppermute(far_coarse, "level", [(3, 0)])
     means = lax.ppermute(means, "level", [(3, 2)])
     result, late, late_mean = call(
         flow_kernel,
         [(19, 2, OWN[2], LANES), (160, LANES), (40, LANES)],
-        [flows, keep_post, keep_wide, ring],
+        [flows, keep_post, keep_wide, ring, matrices],
         2.5,
     )
     me = lax.axis_index("level")
     far = lax.ppermute(jnp.where(me == 3, far_first, late_mean), "level", [(3, 1), (2, 0)])
     late = lax.ppermute(late, "level", [(2, 1)])
+    covered, near = call(
+        prepare_kernel, [(8, 160, LANES), (4, 304, LANES)], [early, far, far_coarse, means], 4.0
+    )
     (state,) = call(
-        finish_kernel, [full], [state, result, third_state, means, early, late, far, far_coarse], 1.0
+        finish_kernel, [full], [state, result, third_state, late, far, covered, near], 1.0
     )
     return state[None]
 

time: 40.6 us -> 38.8 us (0.956)
  the two profiles are of different devices: /device:TPU:0 before, /device:TPU:10 now
where the time goes in v5:
time: 38.8 us; the launch traced here: 38.4 us
  starting transfers between devices  16.1 us (41%)
  waiting for transfers between devices  14.9 us (38%)
  Pallas kernels  5.44 us (14%)
  other arithmetic  1.89 us (5%)
    ppermute x1, waiting for transfers between devices, shards(): lax.ppermute(jnp.where(me == 3, far_first, late_mean), 'level', [(3, 1),...  8.78 us
    pallas_call x6, Pallas kernels, call(): pl.pallas_call(kernel, out_shape=[jax.ShapeDtypeStruct(s[:-1], BF16) if s...  5.44 us
    ppermute x1, starting transfers between devices, shards(): center = lax.ppermute(center, 'level', down)  3.37 us
    ppermute x1, starting transfers between devices, shards(): right = lax.ppermute(zone_left, both, diagonal(-1))  2.44 us
    ppermute x1, waiting for transfers between devices, shards(): right = lax.ppermute(zone_left, both, diagonal(-1))  2.42 us
    ppermute x1, waiting for transfers between devices, shards(): left = lax.ppermute(zone_right, both, diagonal(1))  2.08 us
    ppermute x1, starting transfers between devices, shards(): left = lax.ppermute(zone_right, both, diagonal(1))  1.95 us
    ppermute x1, starting transfers between devices, shards(): early = lax.ppermute(early, 'level', [(2, 1), (1, 0)])  1.92 us
  transfers between devices with their start and end apart: 11, of which 4 were waited for; matrix products, arithmetic and copies ran while one was open for 0% of the time, Pallas kernels for 1%

profile of v5, /device:TPU:10, one launch (start us, length us, event | category | flops | bytes accessed | tf_op | source)
XLA Modules:
  0.0 38.4 jit_solution(15700938452231524912)
XLA Ops:
  0.0 0.8 %convert_element_type.3 = f32[1,8,1024]{2,1,0:T(8,128)S(1)} convert(s32[1,8,1024]{2,1,0:T(8,128)} %param.3) | non-fusion elementwise | flops 8192 | bytes 65536 | tf_op jit(solution)/shard_map/convert_element_type | solution.py:1205
  0.8 1.1 %pad_maximum_fusion.own = f32[20,8,1024]{2,1,0:T(8,128)S(1)} fusion(f32[1,8,1024]{2,1,0:T(8,128)S(1)} %convert_element_type.3, f32[19,8,1024]{2,1,0:T(8,128)} %bitcast.2), kind=kLoop, calls=%fused_computation | loop fusion | flops 163840 | bytes 1310720 | tf_op jit(solution)/shard_map/concatenate | solution.py:1205
  1.9 1.3 %shard_map.28 = (f32[20,16,128]{2,1,0:T(8,128)S(1)}, f32[20,16,128]{2,1,0:T(8,128)S(1)}, f32[544,128]{1,0:T(8,128)S(1)}, f32[16,8,128]{2,1,0:T(8,128)S(1)}, f32[16,8,128]{2,1,0:T(8,128)S(1)}) custom-call(f32[20,8,1024]{2,1,0:T(8,128)S(1)} %pad_maximum_fusion.own), custom_call_target="tpu_custom_call" | custom-call | flops 1500000000 | bytes 5400000 | tf_op jit(solution)/shard_map/pallas_call | solution.py:1188
  3.2 3.4 %collective-permute-start.2 = (f32[544,128]{1,0:T(8,128)S(1)}, f32[544,128]{1,0:T(8,128)S(1)}, u32[]{:S(2)}, u32[]{:S(2)}) collective-permute-start(f32[544,128]{1,0:T(8,128)S(1)} %get-tuple-element.30), channel_id=1, source_target_pairs={{0,8},{8,16},{16,24},{1,9},{9,17},{17,25},{2,10},{10,18},{18,26},{... | collective-permute-start | bytes 835592 | tf_op jit(solution)/shard_map/ppermute | solution.py:1225
  6.6 0.1 collective-permute-start
  6.6 1.7 %collective-permute-start.1 = (f32[20,16,128]{2,1,0:T(8,128)S(1)}, f32[20,16,128]{2,1,0:T(8,128)S(1)}, u32[]{:S(2)}, u32[]{:S(2)}) collective-permute-start(f32[20,16,128]{2,1,0:T(8,128)S(1)} %get-tuple-element.29), channel_id=1, source_target_pairs={{0,7},{1,0},{2,1},{3,2},{4,3},{5,4},{6,5},{7,6},{8,15},{9,8},{10,9... | collective-permute-start | bytes 491528 | tf_op jit(solution)/shard_map/ppermute | solution.py:1229
  8.4 1.9 %collective-permute-start.3 = (f32[16,8,128]{2,1,0:T(8,128)S(1)}, f32[16,8,128]{2,1,0:T(8,128)S(1)}, u32[]{:S(2)}, u32[]{:S(2)}) collective-permute-start(f32[16,8,128]{2,1,0:T(8,128)S(1)} %get-tuple-element.31), channel_id=1, source_target_pairs={{0,9},{1,10},{2,11},{3,12},{4,13},{5,14},{6,15},{7,8},{8,17},{9,18... | collective-permute-start | bytes 196616 | tf_op jit(solution)/shard_map/ppermute | solution.py:1226
  10.3 2.4 %collective-permute-start.4 = (f32[16,8,128]{2,1,0:T(8,128)S(1)}, f32[16,8,128]{2,1,0:T(8,128)S(1)}, u32[]{:S(2)}, u32[]{:S(2)}) collective-permute-start(f32[16,8,128]{2,1,0:T(8,128)S(1)} %get-tuple-element.32), channel_id=1, source_target_pairs={{0,15},{1,8},{2,9},{3,10},{4,11},{5,12},{6,13},{7,14},{8,23},{9,16... | collective-permute-start | bytes 196616 | tf_op jit(solution)/shard_map/ppermute | solution.py:1227
  12.8 2.1 %collective-permute-done.3.left = f32[16,8,128]{2,1,0:T(8,128)S(1)} collective-permute-done((f32[16,8,128]{2,1,0:T(8,128)S(1)}, f32[16,8,128]{2,1,0:T(8,128)S(1)}, u32[]{:S(2)}, u32[]{:S(2)}) %collective-permute-start.3) | collective-permute-done | bytes 65568 | tf_op jit(solution)/shard_map/ppermute | solution.py:1226
  14.9 2.4 %collective-permute-done.4.right = f32[16,8,128]{2,1,0:T(8,128)S(1)} collective-permute-done((f32[16,8,128]{2,1,0:T(8,128)S(1)}, f32[16,8,128]{2,1,0:T(8,128)S(1)}, u32[]{:S(2)}, u32[]{:S(2)}) %collective-permute-start.4) | collective-permute-done | bytes 65568 | tf_op jit(solution)/shard_map/ppermute | solution.py:1227
  17.3 0.0 collective-permute-done.low
  17.3 0.0 collective-permute-done.1.high
  17.3 0.0 collective-permute-done.2.center
  17.3 2.6 %shard_map.29 = (f32[19,8,1024]{2,1,0:T(8,128)S(1)}, f32[20,1,112,128]{3,2,1,0:T(8,128)S(1)}, f32[19,64,128]{2,1,0:T(8,128)S(1)}, f32[144,128]{1,0:T(8,128)S(1)}...) custom-call(f32[20,8,1024]{2,1,0:T(8,128)S(1)} %pad_maximum_fusion.o, ...), custom_call_target="tpu_custom_call" | custom-call | flops 8000000000 | bytes 28800000 | tf_op jit(solution)/shard_map/pallas_call | solution.py:1188
  19.9 0.7 %collective-permute-start.5 = (f32[144,128]{1,0:T(8,128)S(1)}, f32[144,128]{1,0:T(8,128)S(1)}, u32[]{:S(2)}, u32[]{:S(2)}) collective-permute-start(f32[144,128]{1,0:T(8,128)S(1)} %get-tuple-element.34), channel_id=1, source_target_pairs={{24,16},{25,17},{26,18},{27,19},{28,20},{29,21},{30,22},{31,23}} | collective-permute-start | bytes 221192 | tf_op jit(solution)/shard_map/ppermute | solution.py:1247
  20.6 0.7 %collective-permute-start.10 = (f32[160,128]{1,0:T(8,128)S(1)}, f32[160,128]{1,0:T(8,128)S(1)}, u32[]{:S(2)}, u32[]{:S(2)}) collective-permute-start(f32[160,128]{1,0:T(8,128)S(1)} %get-tuple-element.48), channel_id=1, source_target_pairs={{24,16},{25,17},{26,18},{27,19},{28,20},{29,21},{30,22},{31,23}} | collective-permute-start | bytes 245768 | tf_op jit(solution)/shard_map/ppermute | solution.py:1256
  21.2 0.7 %collective-permute-start.9 = (f32[40,128]{1,0:T(8,128)S(1)}, f32[40,128]{1,0:T(8,128)S(1)}, u32[]{:S(2)}, u32[]{:S(2)}) collective-permute-start(f32[40,128]{1,0:T(8,128)S(1)} %get-tuple-element.47), channel_id=1, source_target_pairs={{24,0},{25,1},{26,2},{27,3},{28,4},{29,5},{30,6},{31,7}} | collective-permute-start | bytes 61448 | tf_op jit(solution)/shard_map/ppermute | solution.py:1255
  21.9 1.9 %collective-permute-start.8 = (f32[19,16,128]{2,1,0:T(8,128)S(1)}, f32[19,16,128]{2,1,0:T(8,128)S(1)}, u32[]{:S(2)}, u32[]{:S(2)}) collective-permute-start(f32[19,16,128]{2,1,0:T(8,128)S(1)} %get-tuple-element.46), channel_id=1, source_target_pairs={{16,8},{8,0},{17,9},{9,1},{18,10},{10,2},{19,11},{11,3},{20,12},{1... | collective-permute-start | bytes 466952 | tf_op jit(solution)/shard_map/ppermute | solution.py:1248
  23.8 0.0 collective-permute-done.5.flows
  23.9 1.3 %collective-permute-start.7 = (f32[40,128]{1,0:T(8,128)S(1)}, f32[40,128]{1,0:T(8,128)S(1)}, u32[]{:S(2)}, u32[]{:S(2)}) collective-permute-start(f32[40,128]{1,0:T(8,128)S(1)} %broadcast_select_fusion), channel_id=1, source_target_pairs={{24,8},{16,0},{25,9},{17,1},{26,10},{18,2},{27,11},{19,3},{28,12},... | collective-permute-start | bytes 61448 | tf_op jit(solution)/shard_map/ppermute | solution.py:1264
  25.2 1.3 %collective-permute-start.6 = (f32[160,128]{1,0:T(8,128)S(1)}, f32[160,128]{1,0:T(8,128)S(1)}, u32[]{:S(2)}, u32[]{:S(2)}) collective-permute-start(f32[160,128]{1,0:T(8,128)S(1)} %get-tuple-element.43), channel_id=1, source_target_pairs={{16,8},{17,9},{18,10},{19,11},{20,12},{21,13},{22,14},{23,15}} | collective-permute-start | bytes 245768 | tf_op jit(solution)/shard_map/ppermute | solution.py:1265
  26.5 0.0 collective-permute-done.9.far_coarse
  26.5 0.0 collective-permute-done.10.means
  26.5 8.8 %collective-permute-done.7.far = f32[40,128]{1,0:T(8,128)S(1)} collective-permute-done((f32[40,128]{1,0:T(8,128)S(1)}, f32[40,128]{1,0:T(8,128)S(1)}, u32[]{:S(2)}, u32[]{:S(2)}) %collective-permute-start.7) | collective-permute-done | bytes 20512 | tf_op jit(solution)/shard_map/ppermute | solution.py:1264
  35.3 0.0 collective-permute-done.8.early
  35.3 0.3 shard_map.32
  35.6 1.6 %collective-permute-done.6.late = f32[160,128]{1,0:T(8,128)S(1)} collective-permute-done((f32[160,128]{1,0:T(8,128)S(1)}, f32[160,128]{1,0:T(8,128)S(1)}, u32[]{:S(2)}, u32[]{:S(2)}) %collective-permute-start.6) | collective-permute-done | bytes 81952 | tf_op jit(solution)/shard_map/ppermute | solution.py:1265
  37.2 1.3 %shard_map.33 = f32[19,8,1024]{2,1,0:T(8,128)} custom-call(f32[19,8,1024]{2,1,0:T(8,128)S(1)} %get-tuple-element.33.old_state, f32[19,2,32,128]{3,2,1,0:T(8,128)S(1)} %get-tuple-element.41.result, f32[19,8,1024]{2,1,0:T(8,128)S(1)} %get-tuple-element.42.third_state, f32[160,128]{1,0:T(8,128)S(1)} %collective-permute-done.6.late, ...), custom_call_target="tpu_custom_call" | custom-call | flops 1000000000 | bytes 3600000 | tf_op jit(solution)/shard_map/pallas_call | solution.py:1188
  (3 shorter events, 0.0 us)
Async XLA Ops:
  3.2 14.1 %collective-permute-start.2 = (f32[544,128]{1,0:T(8,128)S(1)}, f32[544,128]{1,0:T(8,128)S(1)}, u32[]{:S(2)}, u32[]{:S(2)}) collective-permute-start(f32[544,128]{1,0:T(8,128)S(1)} %get-tuple-element.30), channel_id=1, source_target_pairs={{0,8},{8,16},{16,24},{1,9},{9,17},{17,25},{2,10},{10,18},{18,26},{... | collective-permute-start | bytes 835592 | tf_op jit(solution)/shard_map/ppermute | solution.py:1225
  6.6 10.7 %collective-permute-start = (f32[20,16,128]{2,1,0:T(8,128)S(1)}, f32[20,16,128]{2,1,0:T(8,128)S(1)}, u32[]{:S(2)}, u32[]{:S(2)}) collective-permute-start(f32[20,16,128]{2,1,0:T(8,128)S(1)} %get-tuple-element.28), channel_id=1, source_target_pairs={{0,1},{1,2},{2,3},{3,4},{4,5},{5,6},{6,7},{7,0},{8,9},{9,10},{10,1... | collective-permute-start | bytes 491528 | tf_op jit(solution)/shard_map/ppermute | solution.py:1228
  6.6 10.6 %collective-permute-start.1 = (f32[20,16,128]{2,1,0:T(8,128)S(1)}, f32[20,16,128]{2,1,0:T(8,128)S(1)}, u32[]{:S(2)}, u32[]{:S(2)}) collective-permute-start(f32[20,16,128]{2,1,0:T(8,128)S(1)} %get-tuple-element.29), channel_id=1, source_target_pairs={{0,7},{1,0},{2,1},{3,2},{4,3},{5,4},{6,5},{7,6},{8,15},{9,8},{10,9... | collective-permute-start | bytes 491528 | tf_op jit(solution)/shard_map/ppermute | solution.py:1229
  8.4 6.5 %collective-permute-start.3 = (f32[16,8,128]{2,1,0:T(8,128)S(1)}, f32[16,8,128]{2,1,0:T(8,128)S(1)}, u32[]{:S(2)}, u32[]{:S(2)}) collective-permute-start(f32[16,8,128]{2,1,0:T(8,128)S(1)} %get-tuple-element.31), channel_id=1, source_target_pairs={{0,9},{1,10},{2,11},{3,12},{4,13},{5,14},{6,15},{7,8},{8,17},{9,18... | collective-permute-start | bytes 196616 | tf_op jit(solution)/shard_map/ppermute | solution.py:1226
  10.3 7.0 %collective-permute-start.4 = (f32[16,8,128]{2,1,0:T(8,128)S(1)}, f32[16,8,128]{2,1,0:T(8,128)S(1)}, u32[]{:S(2)}, u32[]{:S(2)}) collective-permute-start(f32[16,8,128]{2,1,0:T(8,128)S(1)} %get-tuple-element.32), channel_id=1, source_target_pairs={{0,15},{1,8},{2,9},{3,10},{4,11},{5,12},{6,13},{7,14},{8,23},{9,16... | collective-permute-start | bytes 196616 | tf_op jit(solution)/shard_map/ppermute | solution.py:1227
  19.9 4.0 %collective-permute-start.5 = (f32[144,128]{1,0:T(8,128)S(1)}, f32[144,128]{1,0:T(8,128)S(1)}, u32[]{:S(2)}, u32[]{:S(2)}) collective-permute-start(f32[144,128]{1,0:T(8,128)S(1)} %get-tuple-element.34), channel_id=1, source_target_pairs={{24,16},{25,17},{26,18},{27,19},{28,20},{29,21},{30,22},{31,23}} | collective-permute-start | bytes 221192 | tf_op jit(solution)/shard_map/ppermute | solution.py:1247
  20.6 5.9 %collective-permute-start.10 = (f32[160,128]{1,0:T(8,128)S(1)}, f32[160,128]{1,0:T(8,128)S(1)}, u32[]{:S(2)}, u32[]{:S(2)}) collective-permute-start(f32[160,128]{1,0:T(8,128)S(1)} %get-tuple-element.48), channel_id=1, source_target_pairs={{24,16},{25,17},{26,18},{27,19},{28,20},{29,21},{30,22},{31,23}} | collective-permute-start | bytes 245768 | tf_op jit(solution)/shard_map/ppermute | solution.py:1256
  21.2 5.3 %collective-permute-start.9 = (f32[40,128]{1,0:T(8,128)S(1)}, f32[40,128]{1,0:T(8,128)S(1)}, u32[]{:S(2)}, u32[]{:S(2)}) collective-permute-start(f32[40,128]{1,0:T(8,128)S(1)} %get-tuple-element.47), channel_id=1, source_target_pairs={{24,0},{25,1},{26,2},{27,3},{28,4},{29,5},{30,6},{31,7}} | collective-permute-start | bytes 61448 | tf_op jit(solution)/shard_map/ppermute | solution.py:1255
  21.9 13.4 %collective-permute-start.8 = (f32[19,16,128]{2,1,0:T(8,128)S(1)}, f32[19,16,128]{2,1,0:T(8,128)S(1)}, u32[]{:S(2)}, u32[]{:S(2)}) collective-permute-start(f32[19,16,128]{2,1,0:T(8,128)S(1)} %get-tuple-element.46), channel_id=1, source_target_pairs={{16,8},{8,0},{17,9},{9,1},{18,10},{10,2},{19,11},{11,3},{20,12},{1... | collective-permute-start | bytes 466952 | tf_op jit(solution)/shard_map/ppermute | solution.py:1248
  23.9 11.4 %collective-permute-start.7 = (f32[40,128]{1,0:T(8,128)S(1)}, f32[40,128]{1,0:T(8,128)S(1)}, u32[]{:S(2)}, u32[]{:S(2)}) collective-permute-start(f32[40,128]{1,0:T(8,128)S(1)} %broadcast_select_fusion), channel_id=1, source_target_pairs={{24,8},{16,0},{25,9},{17,1},{26,10},{18,2},{27,11},{19,3},{28,12},... | collective-permute-start | bytes 61448 | tf_op jit(solution)/shard_map/ppermute | solution.py:1264
  25.2 12.0 %collective-permute-start.6 = (f32[160,128]{1,0:T(8,128)S(1)}, f32[160,128]{1,0:T(8,128)S(1)}, u32[]{:S(2)}, u32[]{:S(2)}) collective-permute-start(f32[160,128]{1,0:T(8,128)S(1)} %get-tuple-element.43), channel_id=1, source_target_pairs={{16,8},{17,9},{18,10},{19,11},{20,12},{21,13},{22,14},{23,15}} | collective-permute-start | bytes 245768 | tf_op jit(solution)/shard_map/ppermute | solution.py:1265

commit v6 on v5

--- a/solution.py
+++ b/solution.py
@@ -263,9 +263,9 @@
         out[pl.ds(8 * plane, 8), :] = total
 
 
-def late_means(late, deep, value, scratch):
+def late_means(late, weights, value, scratch):
     for half in range(2):
-        scratch[...] = moved(late[...], late_mean_matrix(half, deep)).reshape(20, 8, LANES)
+        scratch[...] = moved(late[...], weights[half]).reshape(20, 8, LANES)
         for q in range(19):
             value[q, pl.ds(4 * half, 4), :] = (
                 scratch[q, pl.ds(0, 4, stride=2), :] + scratch[q, pl.ds(1, 4, stride=2), :]
@@ -308,6 +308,9 @@
 FLOW_CHUNKS = tuple(
     (q, c) for q in FLOW_DIRECTIONS for c in range(2) if q in Z_OUT or q in (Y_DOWN, Y_UP)[c]
 )
+
+
+LATE_AT = len(FLOW_CHUNKS)
 
 
 def flow_chunk(q, c):
@@ -475,7 +478,7 @@
         return carry
 
     if unroll is None:
-        unroll = max(u for u in range(1, 7) if count % u == 0)
+        unroll = max(u for u in range(1, 13) if count % u == 0)
     lax.fori_loop(0, count, step, 0, unroll=unroll)
 
 
@@ -489,7 +492,7 @@
     return jnp.dot(jnp.concatenate([high, low], axis=1), matrix, preferred_element_type=F32)
 
 
-def load_level(level, own, low, high, buf):
+def load_level(level, own, flags, low, high, buf):
     factor, count, row0 = FACTOR[level], CHUNKS[level], ROW0[level]
     n = OWN[level]
 
@@ -502,7 +505,8 @@
                 buf[q, c, pl.ds(row0 - 2 * factor, 2 * factor), :] = low[q, rows, :]
                 buf[q, c, pl.ds(row0 + n, 2 * factor), :] = high[q, rows, :]
 
-    loop(20, lambda q: one(q, lambda j: own[q, :, pl.ds(j * LANES, LANES)]))
+    loop(19, lambda q: one(q, lambda j: own[q, :, pl.ds(j * LANES, LANES)]))
+    one(19, lambda j: flags[:, pl.ds(j * LANES, LANES)])
 
 
 def store_level(level, buf, row0, out):
@@ -597,7 +601,7 @@
             wide[q, c, pl.ds(first + 1, count, stride=2), :] = t
 
 
-def start_kernel(own, to_right, to_left, center, to_zone_right, to_zone_left):
+def start_kernel(own, flags, to_right, to_left, center, to_zone_right, to_zone_left):
     me = lax.axis_index("level")
 
     def halo(q, source):
@@ -605,7 +609,8 @@
             to_left[q, pl.ds(j, 2, stride=8), :] = source(pl.ds(0, 2), j)
             to_right[q, pl.ds(j, 2, stride=8), :] = source(pl.ds(SLAB - 2, 2), j)
 
-    loop(20, lambda q: halo(q, lambda rows, j: own[q, rows, pl.ds(j * LANES, LANES)]))
+    loop(19, lambda q: halo(q, lambda rows, j: own[q, rows, pl.ds(j * LANES, LANES)]))
+    halo(19, lambda rows, j: flags[rows, pl.ds(j * LANES, LANES)])
 
     for level in range(3):
 
@@ -616,27 +621,27 @@
             def scoped(buf, post, packed):
                 post[...] = jnp.zeros(post.shape, F32)
                 buf[19] = jnp.zeros(buf.shape[1:], F32)
-                load_level(level, own, None, None, buf)
+                load_level(level, own, flags, None, None, buf)
                 collide_rows(level, buf, buf, None, post, row0, n // 8)
                 pull_rows(level, post, buf, row0 - 8, n // 8 + 2)
                 def spanned(first, many, c):
                     return buf[pl.ds(first, many), c, pl.ds(row0 - 8, span), :].reshape(many * span, LANES)
 
-                main = folded = flags = None
+                main = folded = solid = None
                 for c in range(count):
                     part = moved(spanned(0, PLANES, c), pack_chunk(level, c))
                     main = part if main is None else main + part
                     part = moved(spanned(PLANES, 4, c), fold_chunk(level, c))
                     folded = part if folded is None else folded + part
                     part = moved(spanned(19, 1, c), flag_chunk(level, c))
-                    flags = part if flags is None else flags + part
+                    solid = part if solid is None else solid + part
                 for p in range(PLANES):
                     j, k = divmod(p, 3)
                     part = main[span * p : span * (p + 1)]
                     if j < 4:
                         part = part + folded[span * j : span * (j + 1), LANES * k : LANES * (k + 1)]
                     packed[p] = part
-                packed[PLANES] = flags
+                packed[PLANES] = solid
                 for p in range(PLANES + 1):
                     center[pl.ds(p * (OWN[2] + 2), n + 2), :] = packed[p, pl.ds(7, n + 2), :]
                     to_zone_right[p] = packed[p, pl.ds(n + 1, 8), :]
@@ -718,11 +723,11 @@
     row_loop(first, groups, lambda row: substep(pulled(pa, 3, row, [0], True)[0], row, pb))
 
 
-def finest_role(own, low, high, center, left, right, g, zpost, flows):
+def finest_role(own, flags, low, high, center, left, right, g, zpost, flows):
     def scoped(pa, pb, wide, zone, widen3, restrict3):
         widen3[...] = widen_matrix(3)
         restrict3[...] = restrict_chunk(3, 0)
-        load_level(3, own, low, high, g)
+        load_level(3, own, flags, low, high, g)
         load_zone(2, zone, 16, center, left, right, 8, 48)
         covered, rim = zone_masks(2, 0)
         interface_values(None, zone, rim, widen3, wide)
@@ -759,6 +764,20 @@
     def _():
         for k, (q, c) in enumerate(FLOW_CHUNKS):
             matrices[:, pl.ds(k * LANES, LANES)] = flow_chunk(q, c)
+        for half in range(2):
+            for c in range(2):
+                matrices[:, pl.ds((LATE_AT + 2 * half + c) * LANES, LANES)] = late_chunk(half, c)
+            matrices[:, pl.ds((LATE_AT + 4 + half) * LANES, LANES)] = late_mean_matrix(half, False)
+
+    @pl.when(lax.axis_index("level") == 1)
+    def _():
+        for half in range(2):
+            matrices[:, pl.ds(2 * half * LANES, 2 * LANES)] = late_back_chunk(half)
+
+    @pl.when(lax.axis_index("level") == 0)
+    def _():
+        matrices[:, pl.ds(0, LANES)] = mean_back_matrix()
+        matrices[:, pl.ds(LANES, 4 * LANES)] = spread_covered_matrix()
 
     @pl.when(lax.axis_index("level") == 3)
     def _():
@@ -815,7 +834,7 @@
                         part = pltpu.roll(value[pl.ds(8 * q, 8), :], (8 * k - 4) % LANES, 1)
                         total = jnp.where(((lane & 63) >> 3) == k, part, total)
                 far_first[pl.ds(8 * plane, 8), :] = total
-            late_means(value, True, flat.at[:, pl.ds(0, 8)], spread.at[pl.ds(0, 20), pl.ds(0, 8)])
+            late_means(value, [late_mean_matrix(half, True) for half in range(2)], flat.at[:, pl.ds(0, 8)], spread.at[pl.ds(0, 20), pl.ds(0, 8)])
             packed_planes([flat[q, pl.ds(0, 8), :] for q in range(19)], far_coarse, 32)
             store_level(3, out, 0, state)
 
@@ -850,12 +869,12 @@
     return total.reshape(flat.shape[0], rows, LANES)
 
 
-def second_role(own, low, high, center, left, right, keep_post, keep_wide, early, ring):
+def second_role(own, flags, low, high, center, left, right, keep_post, keep_wide, early, ring):
     level, row0 = 2, ROW0[2]
     first = row0 - 8
 
     def scoped(g, wide, zone, zpost, conv, spread, flat):
-        load_level(level, own, low, high, g)
+        load_level(level, own, flags, low, high, g)
         load_zone(1, zone, 16, center, left, right, 8, 32)
         covered, rim = zone_masks(1, 0)
         keep_post[19] = g[19]
@@ -908,12 +927,12 @@
     )
 
 
-def first_role(own, low, high, center, left, right, state, early):
+def first_role(own, flags, low, high, center, left, right, state, early):
     level, row0, n = 1, ROW0[1], OWN[1]
     first = row0 - 8
 
     def scoped(g, post, wide, zone, conv, spread, flat):
-        load_level(level, own, low, high, g)
+        load_level(level, own, flags, low, high, g)
         load_zone(0, zone, 12, center, left, right, 8, 16)
         y, z = zone_cell(0, lanes())
         convert_zone(0, zone, 8, 2, (z == 7) | (y == Y_LOW) | (y == Y_HIGH), conv)
@@ -943,11 +962,11 @@
     )
 
 
-def coarse_role(own, low, high, state):
+def coarse_role(own, flags, low, high, state):
     level, row0 = 0, ROW0[0]
 
     def scoped(g, post):
-        load_level(level, own, low, high, g)
+        load_level(level, own, flags, low, high, g)
         collide_rows(level, g, g, None, post, row0 - 8, 3)
         pull_rows(level, post, g, row0, 1)
         store_level(level, g, row0, state)
@@ -960,11 +979,11 @@
 
 
 def main_kernel(
-    own, low, high, center, left, right,
+    own, flags, low, high, center, left, right,
     state, fine, fine_post, flows, keep_post, keep_wide, early, ring,
 ):
     me = lax.axis_index("level")
-    arrived = (own, low, high, center, left, right)
+    arrived = (own, flags, low, high, center, left, right)
 
     @pl.when(me == 3)
     def _():
@@ -980,7 +999,7 @@
 
     @pl.when(me == 0)
     def _():
-        coarse_role(own, low, high, state)
+        coarse_role(own, flags, low, high, state)
 
 
 def flow_kernel(flows, keep_post, keep_wide, ring, matrices, result, late, late_mean):
@@ -989,8 +1008,8 @@
 
     @pl.when(lax.axis_index("level") == 2)
     def _():
-        def scoped(g, post, override, flat, value, scratch):
-            total = moved(flows[...], matrices[...])
+        def scoped(other, post, override, flat, value, scratch):
+            total = moved(flows[...], matrices[:, pl.ds(0, LATE_AT * LANES)])
             for k in range(len(FLOW_CHUNKS)):
                 override[k] = total[:, k * LANES : (k + 1) * LANES]
             outward = []
@@ -1015,19 +1034,15 @@
                         post[q, c, pl.ds(row, 8), :] = v[q]
 
             row_loop(first, 6, begin)
-            for cycle in (1, 2):
-                pull_rows(level, post, g, first, 6)
-
-                def body(row, cycle=cycle):
-                    for c in range(2):
-                        v = [
-                            jnp.where(masks[c], keep_wide[q, c, pl.ds(row, 8), :], g[q, c, pl.ds(row, 8), :])
-                            for q in range(19)
-                        ]
+            for cycle, source, dest in ((1, post, other), (2, other, post)):
+
+                def body(row, cycle=cycle, source=source, dest=dest):
+                    for c, v in enumerate(pulled(source, level, row, range(2))):
+                        v = [jnp.where(masks[c], keep_wide[q, c, pl.ds(row, 8), :], v[q]) for q in range(19)]
                         v = collided(v, keep_post[19, c, pl.ds(row, 8), :], level)
                         v = overridden(c, row, cycle, v)
                         for q in range(19):
-                            post[q, c, pl.ds(row, 8), :] = v[q]
+                            dest[q, c, pl.ds(row, 8), :] = v[q]
 
                 row_loop(first, 6, body)
 
@@ -1044,14 +1059,19 @@
             total = None
             for half in range(2):
                 for c in range(2):
-                    part = moved(flat[c, :, pl.ds(8 * half, 8), :].reshape(160, LANES), late_chunk(half, c))
+                    part = moved(
+                        flat[c, :, pl.ds(8 * half, 8), :].reshape(160, LANES),
+                        matrices[:, pl.ds((LATE_AT + 2 * half + c) * LANES, LANES)],
+                    )
                     total = part if total is None else total + part
             scale = child_scale(2)
             v = relax([total[8 * q : 8 * q + 8] for q in range(19)], 1.0 - scale, scale)
             for q in range(19):
                 late[pl.ds(8 * q, 8), :] = v[q]
             late[pl.ds(152, 8), :] = jnp.zeros((8, LANES), F32)
-            late_means(late, False, value, scratch)
+            late_means(
+                late, [matrices[:, pl.ds((LATE_AT + 4 + half) * LANES, LANES)] for half in range(2)], value, scratch
+            )
             packed_planes([value[q] + ring[q] for q in range(19)], late_mean, 32)
 
         pl.run_scoped(
@@ -1065,7 +1085,7 @@
         )
 
 
-def prepare_kernel(early, far, far_coarse, means, covered, near):
+def prepare_kernel(early, far, far_coarse, means, matrices, covered, near):
     me = lax.axis_index("level")
 
     @pl.when(me == 2)
@@ -1092,7 +1112,7 @@
                     part = pltpu.roll(part, LANES - 32 * (q % 4), 1)
                 value[q] = jnp.where(lane < 32, part, 0.0)
             value[19] = jnp.zeros((8, LANES), F32)
-            total = moved(value[...].reshape(160, LANES), mean_back_matrix())
+            total = moved(value[...].reshape(160, LANES), matrices[:, pl.ds(0, LANES)])
             scale = child_scale(1)
             v = relax(
                 [early[q, pl.ds(0, 8), :] + total[8 * q : 8 * q + 8] for q in range(19)],
@@ -1101,14 +1121,14 @@
             )
             for q in range(19):
                 value[q] = v[q]
-            total = moved(value[...].reshape(160, LANES), spread_covered_matrix())
+            total = moved(value[...].reshape(160, LANES), matrices[:, pl.ds(LANES, 4 * LANES)])
             for c in range(4):
                 covered[c] = total[:, c * LANES : (c + 1) * LANES]
 
         pl.run_scoped(scoped, pltpu.VMEM((20, 8, LANES), F32))
 
 
-def finish_kernel(old_state, result, third_state, late, far, covered_values, near, state):
+def finish_kernel(old_state, result, third_state, late, far, covered_values, near, matrices, state):
     me = lax.axis_index("level")
 
     @pl.when(me == 3)
@@ -1143,7 +1163,7 @@
                 value[pl.ds(8 * q, 8), :] = jnp.where(deep, part, late[pl.ds(8 * q, 8), :])
             value[pl.ds(152, 8), :] = jnp.zeros((8, LANES), F32)
             for half in range(2):
-                total = moved(value[...], late_back_chunk(half))
+                total = moved(value[...], matrices[:, pl.ds(2 * half * LANES, 2 * LANES)])
                 for c in range(2):
                     part = total[:, c * LANES : (c + 1) * LANES].reshape(20, 8, LANES)
                     inner[c, :, pl.ds(8 * half, 8), :] = part
@@ -1202,7 +1222,7 @@
 def shards(populations, solid):
     if populations.shape[1:] != (19, SLAB, NY * NZ):
         raise ValueError("unexpected slab")
-    own = jnp.concatenate([populations[0], solid.astype(F32)], axis=0)
+    own, flags = populations[0], solid[0].astype(F32)
     blocks = lax.axis_size("blocks")
     forward = [(i, (i + 1) % blocks) for i in range(blocks)]
     backward = [(i, (i - 1) % blocks) for i in range(blocks)]
@@ -1219,7 +1239,7 @@
     to_right, to_left, center, zone_right, zone_left = call(
         start_kernel,
         [(20, 16, LANES), (20, 16, LANES), (CENTER_ROWS, LANES), (PLANES + 1, 8, LANES), (PLANES + 1, 8, LANES)],
-        [own],
+        [own, flags],
         1.5,
     )
     center = lax.ppermute(center, "level", down)
@@ -1241,14 +1261,14 @@
             (19, 16, LANES),
             (19, 8, LANES),
         ],
-        [own, low, high, center, left, right],
+        [own, flags, low, high, center, left, right],
         8.0,
     )
     flows = lax.ppermute(flows, "level", [(3, 2)])
     early = lax.ppermute(early, "level", [(2, 1), (1, 0)])
     third_state, means, far_first, far_coarse, matrices = call(
         last_cycle_kernel,
-        [full, (160, LANES), (40, LANES), (40, LANES), (2 * LANES, len(FLOW_CHUNKS) * LANES, BF16)],
+        [full, (160, LANES), (40, LANES), (40, LANES), (2 * LANES, (LATE_AT + 6) * LANES, BF16)],
         [fine, fine_post],
         4.0,
     )
@@ -1264,10 +1284,10 @@
     far = lax.ppermute(jnp.where(me == 3, far_first, late_mean), "level", [(3, 1), (2, 0)])
     late = lax.ppermute(late, "level", [(2, 1)])
     covered, near = call(
-        prepare_kernel, [(8, 160, LANES), (4, 304, LANES)], [early, far, far_coarse, means], 4.0
+        prepare_kernel, [(8, 160, LANES), (4, 304, LANES)], [early, far, far_coarse, means, matrices], 4.0
     )
     (state,) = call(
-        finish_kernel, [full], [state, result, third_state, late, far, covered, near], 1.0
+        finish_kernel, [full], [state, result, third_state, late, far, covered, near, matrices], 1.0
     )
     return state[None]
 

time: 38.8 us -> 37.7 us (0.972)
  the two profiles are of different devices: /device:TPU:10 before, /device:TPU:0 now
where the time goes in v6:
time: 37.7 us; the launch traced here: 37.3 us
  starting transfers between devices  20.5 us (54%)
  waiting for transfers between devices  10.4 us (28%)
  Pallas kernels  4.38 us (12%)
  local copies, waits for them, and re-layouts  1.08 us (3%)
  other arithmetic  0.77 us (2%)
    ppermute x1, waiting for transfers between devices, shards(): far_coarse = lax.ppermute(far_coarse, 'level', [(3, 0)])  6.7 us
    ppermute x1, starting transfers between devices, shards(): right = lax.ppermute(zone_left, both, diagonal(-1))  5.34 us
    ppermute x1, starting transfers between devices, shards(): center = lax.ppermute(center, 'level', down)  4.63 us
    pallas_call x6, Pallas kernels, call(): pl.pallas_call(kernel, out_shape=[jax.ShapeDtypeStruct(s[:-1], BF16) if s...  4.38 us
    ppermute x1, starting transfers between devices, shards(): high = lax.ppermute(to_left, 'blocks', backward)  2.63 us
    ppermute x1, starting transfers between devices, shards(): left = lax.ppermute(zone_right, both, diagonal(1))  1.96 us
    ppermute x1, waiting for transfers between devices, shards(): right = lax.ppermute(zone_left, both, diagonal(-1))  1.87 us
    ppermute x1, waiting for transfers between devices, shards(): lax.ppermute(jnp.where(me == 3, far_first, late_mean), 'level', [(3, 1),...  1.82 us
  transfers between devices with their start and end apart: 11, of which 3 were waited for; matrix products, arithmetic and copies ran while one was open for 0% of the time, Pallas kernels for 1%

profile of v6, /device:TPU:0, one launch (start us, length us, event | category | flops | bytes accessed | tf_op | source)
XLA Modules:
  0.0 37.3 jit_solution(562988808577854873)
XLA Ops:
  0.0 0.8 %convert_bitcast_fusion.flags = f32[8,1024]{1,0:T(8,128)S(1)} fusion(s32[1,8,1024]{2,1,0:T(8,128)} %param.3), kind=kLoop, calls=%fused_computation | loop fusion | flops 8192 | bytes 65536 | tf_op jit(solution)/shard_map/convert_element_type | solution.py:1225
  0.8 0.0 copy-start
  0.8 1.1 %copy-done = f32[1,19,8,1024]{3,2,1,0:T(8,128)S(1)} copy-done((f32[1,19,8,1024]{3,2,1,0:T(8,128)S(1)}, f32[1,19,8,1024]{3,2,1,0:T(8,128)}, u32[]{:S(2)}) %copy-start) | copy-done | bytes 622616
  1.8 0.0 copy-start.1
  1.8 1.7 %shard_map.28 = (f32[20,16,128]{2,1,0:T(8,128)S(1)}, f32[20,16,128]{2,1,0:T(8,128)S(1)}, f32[544,128]{1,0:T(8,128)S(1)}, f32[16,8,128]{2,1,0:T(8,128)S(1)}, f32[16,8,128]{2,1,0:T(8,128)S(1)}) custom-call(f32[19,8,1024]{2,1,0:T(8,128)S(1)} %bitcast.4, f32[8,1024]{1,0:T(8,128)S(1)} %convert_bitcast_fusion.flags), custom_call_target="tpu_custom_call" | custom-call | flops 1500000000 | bytes 5400000 | tf_op jit(solution)/shard_map/pallas_call | solution.py:1208
  3.6 4.6 %collective-permute-start.2 = (f32[544,128]{1,0:T(8,128)S(1)}, f32[544,128]{1,0:T(8,128)S(1)}, u32[]{:S(2)}, u32[]{:S(2)}) collective-permute-start(f32[544,128]{1,0:T(8,128)S(1)} %get-tuple-element.30), channel_id=1, source_target_pairs={{0,8},{8,16},{16,24},{1,9},{9,17},{17,25},{2,10},{10,18},{18,26},{... | collective-permute-start | bytes 835592 | tf_op jit(solution)/shard_map/ppermute | solution.py:1245
  8.2 0.1 collective-permute-start
  8.3 2.6 %collective-permute-start.1 = (f32[20,16,128]{2,1,0:T(8,128)S(1)}, f32[20,16,128]{2,1,0:T(8,128)S(1)}, u32[]{:S(2)}, u32[]{:S(2)}) collective-permute-start(f32[20,16,128]{2,1,0:T(8,128)S(1)} %get-tuple-element.29), channel_id=1, source_target_pairs={{0,7},{1,0},{2,1},{3,2},{4,3},{5,4},{6,5},{7,6},{8,15},{9,8},{10,9... | collective-permute-start | bytes 491528 | tf_op jit(solution)/shard_map/ppermute | solution.py:1249
  10.9 2.0 %collective-permute-start.3 = (f32[16,8,128]{2,1,0:T(8,128)S(1)}, f32[16,8,128]{2,1,0:T(8,128)S(1)}, u32[]{:S(2)}, u32[]{:S(2)}) collective-permute-start(f32[16,8,128]{2,1,0:T(8,128)S(1)} %get-tuple-element.31), channel_id=1, source_target_pairs={{0,9},{1,10},{2,11},{3,12},{4,13},{5,14},{6,15},{7,8},{8,17},{9,18... | collective-permute-start | bytes 196616 | tf_op jit(solution)/shard_map/ppermute | solution.py:1246
  12.9 5.3 %collective-permute-start.4 = (f32[16,8,128]{2,1,0:T(8,128)S(1)}, f32[16,8,128]{2,1,0:T(8,128)S(1)}, u32[]{:S(2)}, u32[]{:S(2)}) collective-permute-start(f32[16,8,128]{2,1,0:T(8,128)S(1)} %get-tuple-element.32), channel_id=1, source_target_pairs={{0,15},{1,8},{2,9},{3,10},{4,11},{5,12},{6,13},{7,14},{8,23},{9,16... | collective-permute-start | bytes 196616 | tf_op jit(solution)/shard_map/ppermute | solution.py:1247
  18.2 0.0 collective-permute-done.3.left
  18.2 1.9 %collective-permute-done.4.right = f32[16,8,128]{2,1,0:T(8,128)S(1)} collective-permute-done((f32[16,8,128]{2,1,0:T(8,128)S(1)}, f32[16,8,128]{2,1,0:T(8,128)S(1)}, u32[]{:S(2)}, u32[]{:S(2)}) %collective-permute-start.4) | collective-permute-done | bytes 65568 | tf_op jit(solution)/shard_map/ppermute | solution.py:1247
  20.1 0.0 collective-permute-done.low
  20.1 0.0 collective-permute-done.1.high
  20.1 0.0 collective-permute-done.2.center
  20.1 0.0 copy-done.1
  20.1 1.2 %shard_map.29 = (f32[19,8,1024]{2,1,0:T(8,128)S(1)}, f32[20,1,112,128]{3,2,1,0:T(8,128)S(1)}, f32[19,64,128]{2,1,0:T(8,128)S(1)}, f32[144,128]{1,0:T(8,128)S(1)}...) custom-call(f32[19,8,1024]{2,1,0:T(8,128)S(1)} %bitcast.5, ...), custom_call_target="tpu_custom_call" | custom-call | flops 8000000000 | bytes 28800000 | tf_op jit(solution)/shard_map/pallas_call | solution.py:1208
  21.3 0.7 %collective-permute-start.5 = (f32[144,128]{1,0:T(8,128)S(1)}, f32[144,128]{1,0:T(8,128)S(1)}, u32[]{:S(2)}, u32[]{:S(2)}) collective-permute-start(f32[144,128]{1,0:T(8,128)S(1)} %get-tuple-element.34), channel_id=1, source_target_pairs={{24,16},{25,17},{26,18},{27,19},{28,20},{29,21},{30,22},{31,23}} | collective-permute-start | bytes 221192 | tf_op jit(solution)/shard_map/ppermute | solution.py:1267
  22.0 0.1 shard_map.30
  22.1 0.7 %collective-permute-start.10 = (f32[160,128]{1,0:T(8,128)S(1)}, f32[160,128]{1,0:T(8,128)S(1)}, u32[]{:S(2)}, u32[]{:S(2)}) collective-permute-start(f32[160,128]{1,0:T(8,128)S(1)} %get-tuple-element.48), channel_id=1, source_target_pairs={{24,16},{25,17},{26,18},{27,19},{28,20},{29,21},{30,22},{31,23}} | collective-permute-start | bytes 245768 | tf_op jit(solution)/shard_map/ppermute | solution.py:1276
  22.8 1.3 %collective-permute-start.9 = (f32[40,128]{1,0:T(8,128)S(1)}, f32[40,128]{1,0:T(8,128)S(1)}, u32[]{:S(2)}, u32[]{:S(2)}) collective-permute-start(f32[40,128]{1,0:T(8,128)S(1)} %get-tuple-element.47), channel_id=1, source_target_pairs={{24,0},{25,1},{26,2},{27,3},{28,4},{29,5},{30,6},{31,7}} | collective-permute-start | bytes 61448 | tf_op jit(solution)/shard_map/ppermute | solution.py:1275
  24.1 1.3 %collective-permute-start.8 = (f32[19,16,128]{2,1,0:T(8,128)S(1)}, f32[19,16,128]{2,1,0:T(8,128)S(1)}, u32[]{:S(2)}, u32[]{:S(2)}) collective-permute-start(f32[19,16,128]{2,1,0:T(8,128)S(1)} %get-tuple-element.46), channel_id=1, source_target_pairs={{16,8},{8,0},{17,9},{9,1},{18,10},{10,2},{19,11},{11,3},{20,12},{1... | collective-permute-start | bytes 466952 | tf_op jit(solution)/shard_map/ppermute | solution.py:1268
  25.4 0.0 collective-permute-done.5.flows
  25.4 1.3 %collective-permute-start.7 = (f32[40,128]{1,0:T(8,128)S(1)}, f32[40,128]{1,0:T(8,128)S(1)}, u32[]{:S(2)}, u32[]{:S(2)}) collective-permute-start(f32[40,128]{1,0:T(8,128)S(1)} %broadcast_select_fusion), channel_id=1, source_target_pairs={{24,8},{16,0},{25,9},{17,1},{26,10},{18,2},{27,11},{19,3},{28,12},... | collective-permute-start | bytes 61448 | tf_op jit(solution)/shard_map/ppermute | solution.py:1284
  26.7 0.7 %collective-permute-start.6 = (f32[160,128]{1,0:T(8,128)S(1)}, f32[160,128]{1,0:T(8,128)S(1)}, u32[]{:S(2)}, u32[]{:S(2)}) collective-permute-start(f32[160,128]{1,0:T(8,128)S(1)} %get-tuple-element.43), channel_id=1, source_target_pairs={{16,8},{17,9},{18,10},{19,11},{20,12},{21,13},{22,14},{23,15}} | collective-permute-start | bytes 245768 | tf_op jit(solution)/shard_map/ppermute | solution.py:1285
  27.4 6.7 %collective-permute-done.9.far_coarse = f32[40,128]{1,0:T(8,128)S(1)} collective-permute-done((f32[40,128]{1,0:T(8,128)S(1)}, f32[40,128]{1,0:T(8,128)S(1)}, u32[]{:S(2)}, u32[]{:S(2)}) %collective-permute-start.9) | collective-permute-done | bytes 20512 | tf_op jit(solution)/shard_map/ppermute | solution.py:1275
  34.1 0.0 collective-permute-done.10.means
  34.1 1.8 %collective-permute-done.7.far = f32[40,128]{1,0:T(8,128)S(1)} collective-permute-done((f32[40,128]{1,0:T(8,128)S(1)}, f32[40,128]{1,0:T(8,128)S(1)}, u32[]{:S(2)}, u32[]{:S(2)}) %collective-permute-start.7) | collective-permute-done | bytes 20512 | tf_op jit(solution)/shard_map/ppermute | solution.py:1284
  35.9 0.0 collective-permute-done.8.early
  35.9 0.4 %shard_map.32 = (f32[8,160,128]{2,1,0:T(8,128)S(1)}, f32[4,304,128]{2,1,0:T(8,128)S(1)}) custom-call(f32[19,16,128]{2,1,0:T(8,128)S(1)} %collective-permute-done.8.early, f32[40,128]{1,0:T(8,128)S(1)} %collective-permute-done.7.far, f32[40,128]{1,0:T(8,128)S(1)} %collective-permute-done.9.far_coarse, f32[160,128]{1,0:T(8,128)S(1)} %collective-permute-done.10.means, ...), custom_call_target="tpu_custom_call" | custom-call | flops 4000000000 | bytes 14400000 | tf_op jit(solution)/shard_map/pallas_call | solution.py:1208
  36.4 0.0 collective-permute-done.6.late
  36.4 0.9 %shard_map.33 = f32[19,8,1024]{2,1,0:T(8,128)} custom-call(f32[19,8,1024]{2,1,0:T(8,128)S(1)} %get-tuple-element.33.old_state, f32[19,2,32,128]{3,2,1,0:T(8,128)S(1)} %get-tuple-element.41.result, f32[19,8,1024]{2,1,0:T(8,128)S(1)} %get-tuple-element.42.third_state, f32[160,128]{1,0:T(8,128)S(1)} %collective-permute-done.6.late, ...), custom_call_target="tpu_custom_call" | custom-call | flops 1000000000 | bytes 3600000 | tf_op jit(solution)/shard_map/pallas_call | solution.py:1208
  (2 shorter events, 0.0 us)
Async XLA Ops:
  0.8 1.1 %copy-start = (f32[1,19,8,1024]{3,2,1,0:T(8,128)S(1)}, f32[1,19,8,1024]{3,2,1,0:T(8,128)}, u32[]{:S(2)}) copy-start(f32[1,19,8,1024]{3,2,1,0:T(8,128)} %param.2) | copy-start | bytes 1867780
  1.8 18.3 %copy-start.1 = (f32[1,19,8,1024]{3,2,1,0:T(8,128)S(1)}, f32[1,19,8,1024]{3,2,1,0:T(8,128)}, u32[]{:S(2)}) copy-start(f32[1,19,8,1024]{3,2,1,0:T(8,128)} %param.2) | copy-start | bytes 1867780
  3.6 16.5 %collective-permute-start.2 = (f32[544,128]{1,0:T(8,128)S(1)}, f32[544,128]{1,0:T(8,128)S(1)}, u32[]{:S(2)}, u32[]{:S(2)}) collective-permute-start(f32[544,128]{1,0:T(8,128)S(1)} %get-tuple-element.30), channel_id=1, source_target_pairs={{0,8},{8,16},{16,24},{1,9},{9,17},{17,25},{2,10},{10,18},{18,26},{... | collective-permute-start | bytes 835592 | tf_op jit(solution)/shard_map/ppermute | solution.py:1245
  8.2 11.9 %collective-permute-start = (f32[20,16,128]{2,1,0:T(8,128)S(1)}, f32[20,16,128]{2,1,0:T(8,128)S(1)}, u32[]{:S(2)}, u32[]{:S(2)}) collective-permute-start(f32[20,16,128]{2,1,0:T(8,128)S(1)} %get-tuple-element.28), channel_id=1, source_target_pairs={{0,1},{1,2},{2,3},{3,4},{4,5},{5,6},{6,7},{7,0},{8,9},{9,10},{10,1... | collective-permute-start | bytes 491528 | tf_op jit(solution)/shard_map/ppermute | solution.py:1248
  8.3 11.8 %collective-permute-start.1 = (f32[20,16,128]{2,1,0:T(8,128)S(1)}, f32[20,16,128]{2,1,0:T(8,128)S(1)}, u32[]{:S(2)}, u32[]{:S(2)}) collective-permute-start(f32[20,16,128]{2,1,0:T(8,128)S(1)} %get-tuple-element.29), channel_id=1, source_target_pairs={{0,7},{1,0},{2,1},{3,2},{4,3},{5,4},{6,5},{7,6},{8,15},{9,8},{10,9... | collective-permute-start | bytes 491528 | tf_op jit(solution)/shard_map/ppermute | solution.py:1249
  10.9 7.3 %collective-permute-start.3 = (f32[16,8,128]{2,1,0:T(8,128)S(1)}, f32[16,8,128]{2,1,0:T(8,128)S(1)}, u32[]{:S(2)}, u32[]{:S(2)}) collective-permute-start(f32[16,8,128]{2,1,0:T(8,128)S(1)} %get-tuple-element.31), channel_id=1, source_target_pairs={{0,9},{1,10},{2,11},{3,12},{4,13},{5,14},{6,15},{7,8},{8,17},{9,18... | collective-permute-start | bytes 196616 | tf_op jit(solution)/shard_map/ppermute | solution.py:1246
  12.9 7.2 %collective-permute-start.4 = (f32[16,8,128]{2,1,0:T(8,128)S(1)}, f32[16,8,128]{2,1,0:T(8,128)S(1)}, u32[]{:S(2)}, u32[]{:S(2)}) collective-permute-start(f32[16,8,128]{2,1,0:T(8,128)S(1)} %get-tuple-element.32), channel_id=1, source_target_pairs={{0,15},{1,8},{2,9},{3,10},{4,11},{5,12},{6,13},{7,14},{8,23},{9,16... | collective-permute-start | bytes 196616 | tf_op jit(solution)/shard_map/ppermute | solution.py:1247
  21.3 4.0 %collective-permute-start.5 = (f32[144,128]{1,0:T(8,128)S(1)}, f32[144,128]{1,0:T(8,128)S(1)}, u32[]{:S(2)}, u32[]{:S(2)}) collective-permute-start(f32[144,128]{1,0:T(8,128)S(1)} %get-tuple-element.34), channel_id=1, source_target_pairs={{24,16},{25,17},{26,18},{27,19},{28,20},{29,21},{30,22},{31,23}} | collective-permute-start | bytes 221192 | tf_op jit(solution)/shard_map/ppermute | solution.py:1267
  22.1 12.0 %collective-permute-start.10 = (f32[160,128]{1,0:T(8,128)S(1)}, f32[160,128]{1,0:T(8,128)S(1)}, u32[]{:S(2)}, u32[]{:S(2)}) collective-permute-start(f32[160,128]{1,0:T(8,128)S(1)} %get-tuple-element.48), channel_id=1, source_target_pairs={{24,16},{25,17},{26,18},{27,19},{28,20},{29,21},{30,22},{31,23}} | collective-permute-start | bytes 245768 | tf_op jit(solution)/shard_map/ppermute | solution.py:1276
  22.8 11.3 %collective-permute-start.9 = (f32[40,128]{1,0:T(8,128)S(1)}, f32[40,128]{1,0:T(8,128)S(1)}, u32[]{:S(2)}, u32[]{:S(2)}) collective-permute-start(f32[40,128]{1,0:T(8,128)S(1)} %get-tuple-element.47), channel_id=1, source_target_pairs={{24,0},{25,1},{26,2},{27,3},{28,4},{29,5},{30,6},{31,7}} | collective-permute-start | bytes 61448 | tf_op jit(solution)/shard_map/ppermute | solution.py:1275
  24.1 11.9 %collective-permute-start.8 = (f32[19,16,128]{2,1,0:T(8,128)S(1)}, f32[19,16,128]{2,1,0:T(8,128)S(1)}, u32[]{:S(2)}, u32[]{:S(2)}) collective-permute-start(f32[19,16,128]{2,1,0:T(8,128)S(1)} %get-tuple-element.46), channel_id=1, source_target_pairs={{16,8},{8,0},{17,9},{9,1},{18,10},{10,2},{19,11},{11,3},{20,12},{1... | collective-permute-start | bytes 466952 | tf_op jit(solution)/shard_map/ppermute | solution.py:1268
  25.4 10.5 %collective-permute-start.7 = (f32[40,128]{1,0:T(8,128)S(1)}, f32[40,128]{1,0:T(8,128)S(1)}, u32[]{:S(2)}, u32[]{:S(2)}) collective-permute-start(f32[40,128]{1,0:T(8,128)S(1)} %broadcast_select_fusion), channel_id=1, source_target_pairs={{24,8},{16,0},{25,9},{17,1},{26,10},{18,2},{27,11},{19,3},{28,12},... | collective-permute-start | bytes 61448 | tf_op jit(solution)/shard_map/ppermute | solution.py:1284
  26.7 9.6 %collective-permute-start.6 = (f32[160,128]{1,0:T(8,128)S(1)}, f32[160,128]{1,0:T(8,128)S(1)}, u32[]{:S(2)}, u32[]{:S(2)}) collective-permute-start(f32[160,128]{1,0:T(8,128)S(1)} %get-tuple-element.43), channel_id=1, source_target_pairs={{16,8},{17,9},{18,10},{19,11},{20,12},{21,13},{22,14},{23,15}} | collective-permute-start | bytes 245768 | tf_op jit(solution)/shard_map/ppermute | solution.py:1285

commit v7 on v6

--- a/solution.py
+++ b/solution.py
@@ -657,6 +657,10 @@
         pl.when(me == level)(push)
 
 
+FLOW_SPANS = ((5, 38), (54, 36), (103, 34))
+FLOW_ROWS = 112
+
+
 def pack_flows(post, out, row):
     lane = lanes()
     total = jnp.zeros((8, LANES), F32)
@@ -724,7 +728,7 @@
 
 
 def finest_role(own, flags, low, high, center, left, right, g, zpost, flows):
-    def scoped(pa, pb, wide, zone, widen3, restrict3):
+    def scoped(pa, pb, wide, zone, widen3, restrict3, all_flows):
         widen3[...] = widen_matrix(3)
         restrict3[...] = restrict_chunk(3, 0)
         load_level(3, own, flags, low, high, g)
@@ -741,9 +745,14 @@
 
             finest_cycle(g, pa, pb, wide, first, groups)
             row_loop(first, groups, step_out)
-            restrict_and_collide(g, zone, covered, restrict3, zpost, flows, 48 * cycle)
+            restrict_and_collide(g, zone, covered, restrict3, zpost, all_flows, 48 * cycle)
             if cycle < 2:
                 interface_values(zpost, zone, rim, widen3, wide)
+        at = 0
+        for first, count in FLOW_SPANS:
+            flows[pl.ds(at, count), :] = all_flows[pl.ds(first, count), :]
+            at += count
+        flows[pl.ds(at, FLOW_ROWS - at), :] = jnp.zeros((FLOW_ROWS - at, LANES), F32)
 
     rows = ROWS[3]
     pl.run_scoped(
@@ -754,6 +763,7 @@
         pltpu.VMEM((20, 64, LANES), F32),
         pltpu.VMEM((2 * LANES, LANES), BF16),
         pltpu.VMEM((2 * LANES, LANES), BF16),
+        pltpu.VMEM((144, LANES), F32),
     )
 
 
@@ -1008,8 +1018,13 @@
 
     @pl.when(lax.axis_index("level") == 2)
     def _():
-        def scoped(other, post, override, flat, value, scratch):
-            total = moved(flows[...], matrices[:, pl.ds(0, LATE_AT * LANES)])
+        def scoped(other, post, override, flat, value, scratch, all_flows):
+            all_flows[...] = jnp.zeros(all_flows.shape, F32)
+            at = 0
+            for start, count in FLOW_SPANS:
+                all_flows[pl.ds(start, count), :] = flows[pl.ds(at, count), :]
+                at += count
+            total = moved(all_flows[...], matrices[:, pl.ds(0, LATE_AT * LANES)])
             for k in range(len(FLOW_CHUNKS)):
                 override[k] = total[:, k * LANES : (k + 1) * LANES]
             outward = []
@@ -1082,6 +1097,7 @@
             pltpu.VMEM((2, 20, 16, LANES), F32),
             pltpu.VMEM((19, 8, LANES), F32),
             pltpu.VMEM((20, 8, LANES), F32),
+            pltpu.VMEM((144, LANES), F32),
         )
 
 
@@ -1255,7 +1271,7 @@
             full,
             (20, 1, ROWS[3], LANES),
             (19, 64, LANES),
-            (144, LANES),
+            (FLOW_ROWS, LANES),
             (20, 2, ROWS[2], LANES),
             (19, 2, ROWS[2], LANES),
             (19, 16, LANES),

time: 37.7 us -> 37.5 us (level)
  the two profiles are of different devices: /device:TPU:0 before, /device:TPU:11 now
where the time goes in v7:
time: 37.5 us; the launch traced here: 37.1 us
  starting transfers between devices  18.1 us (48%)
  waiting for transfers between devices  11.3 us (30%)
  Pallas kernels  5.7 us (15%)
  local copies, waits for them, and re-layouts  1.08 us (3%)
  other arithmetic  0.77 us (2%)
    pallas_call x6, Pallas kernels, call(): pl.pallas_call(kernel, out_shape=[jax.ShapeDtypeStruct(s[:-1], BF16) if s...  5.7 us
    ppermute x1, waiting for transfers between devices, shards(): right = lax.ppermute(zone_left, both, diagonal(-1))  5.44 us
    ppermute x1, starting transfers between devices, shards(): left = lax.ppermute(zone_right, both, diagonal(1))  4.46 us
    ppermute x1, waiting for transfers between devices, shards(): lax.ppermute(jnp.where(me == 3, far_first, late_mean), 'level', [(3, 1),...  3.88 us
    ppermute x1, starting transfers between devices, shards(): center = lax.ppermute(center, 'level', down)  3.13 us
    ppermute x1, starting transfers between devices, shards(): low = lax.ppermute(to_right, 'blocks', forward)  2.1 us
    ppermute x1, waiting for transfers between devices, shards(): late = lax.ppermute(late, 'level', [(2, 1)])  1.97 us
    ppermute x1, starting transfers between devices, shards(): right = lax.ppermute(zone_left, both, diagonal(-1))  1.92 us
  transfers between devices with their start and end apart: 11, of which 3 were waited for; matrix products, arithmetic and copies ran while one was open for 0% of the time, Pallas kernels for 1%

profile of v7, /device:TPU:11, one launch (start us, length us, event | category | flops | bytes accessed | tf_op | source)
XLA Modules:
  0.0 37.1 jit_solution(6139682821691974883)
XLA Ops:
  0.0 0.8 %convert_bitcast_fusion.flags = f32[8,1024]{1,0:T(8,128)S(1)} fusion(s32[1,8,1024]{2,1,0:T(8,128)} %param.3), kind=kLoop, calls=%fused_computation | loop fusion | flops 8192 | bytes 65536 | tf_op jit(solution)/shard_map/convert_element_type | solution.py:1241
  0.8 0.0 copy-start
  0.8 1.1 %copy-done = f32[1,19,8,1024]{3,2,1,0:T(8,128)S(1)} copy-done((f32[1,19,8,1024]{3,2,1,0:T(8,128)S(1)}, f32[1,19,8,1024]{3,2,1,0:T(8,128)}, u32[]{:S(2)}) %copy-start) | copy-done | bytes 622616
  1.8 0.0 copy-start.1
  1.8 1.4 %shard_map.28 = (f32[20,16,128]{2,1,0:T(8,128)S(1)}, f32[20,16,128]{2,1,0:T(8,128)S(1)}, f32[544,128]{1,0:T(8,128)S(1)}, f32[16,8,128]{2,1,0:T(8,128)S(1)}, f32[16,8,128]{2,1,0:T(8,128)S(1)}) custom-call(f32[19,8,1024]{2,1,0:T(8,128)S(1)} %bitcast.4, f32[8,1024]{1,0:T(8,128)S(1)} %convert_bitcast_fusion.flags), custom_call_target="tpu_custom_call" | custom-call | flops 1500000000 | bytes 5400000 | tf_op jit(solution)/shard_map/pallas_call | solution.py:1224
  3.3 3.1 %collective-permute-start.2 = (f32[544,128]{1,0:T(8,128)S(1)}, f32[544,128]{1,0:T(8,128)S(1)}, u32[]{:S(2)}, u32[]{:S(2)}) collective-permute-start(f32[544,128]{1,0:T(8,128)S(1)} %get-tuple-element.30), channel_id=1, source_target_pairs={{0,8},{8,16},{16,24},{1,9},{9,17},{17,25},{2,10},{10,18},{18,26},{... | collective-permute-start | bytes 835592 | tf_op jit(solution)/shard_map/ppermute | solution.py:1261
  6.4 2.1 %collective-permute-start = (f32[20,16,128]{2,1,0:T(8,128)S(1)}, f32[20,16,128]{2,1,0:T(8,128)S(1)}, u32[]{:S(2)}, u32[]{:S(2)}) collective-permute-start(f32[20,16,128]{2,1,0:T(8,128)S(1)} %get-tuple-element.28), channel_id=1, source_target_pairs={{0,1},{1,2},{2,3},{3,4},{4,5},{5,6},{6,7},{7,0},{8,9},{9,10},{10,1... | collective-permute-start | bytes 491528 | tf_op jit(solution)/shard_map/ppermute | solution.py:1264
  8.5 0.0 collective-permute-start.1
  8.5 4.5 %collective-permute-start.3 = (f32[16,8,128]{2,1,0:T(8,128)S(1)}, f32[16,8,128]{2,1,0:T(8,128)S(1)}, u32[]{:S(2)}, u32[]{:S(2)}) collective-permute-start(f32[16,8,128]{2,1,0:T(8,128)S(1)} %get-tuple-element.31), channel_id=1, source_target_pairs={{0,9},{1,10},{2,11},{3,12},{4,13},{5,14},{6,15},{7,8},{8,17},{9,18... | collective-permute-start | bytes 196616 | tf_op jit(solution)/shard_map/ppermute | solution.py:1262
  13.0 1.9 %collective-permute-start.4 = (f32[16,8,128]{2,1,0:T(8,128)S(1)}, f32[16,8,128]{2,1,0:T(8,128)S(1)}, u32[]{:S(2)}, u32[]{:S(2)}) collective-permute-start(f32[16,8,128]{2,1,0:T(8,128)S(1)} %get-tuple-element.32), channel_id=1, source_target_pairs={{0,15},{1,8},{2,9},{3,10},{4,11},{5,12},{6,13},{7,14},{8,23},{9,16... | collective-permute-start | bytes 196616 | tf_op jit(solution)/shard_map/ppermute | solution.py:1263
  14.9 0.0 collective-permute-done.3.left
  14.9 5.4 %collective-permute-done.4.right = f32[16,8,128]{2,1,0:T(8,128)S(1)} collective-permute-done((f32[16,8,128]{2,1,0:T(8,128)S(1)}, f32[16,8,128]{2,1,0:T(8,128)S(1)}, u32[]{:S(2)}, u32[]{:S(2)}) %collective-permute-start.4) | collective-permute-done | bytes 65568 | tf_op jit(solution)/shard_map/ppermute | solution.py:1263
  20.4 0.0 collective-permute-done.low
  20.4 0.0 collective-permute-done.1.high
  20.4 0.0 collective-permute-done.2.center
  20.4 0.0 copy-done.1
  20.4 2.7 %shard_map.29 = (f32[19,8,1024]{2,1,0:T(8,128)S(1)}, f32[20,1,112,128]{3,2,1,0:T(8,128)S(1)}, f32[19,64,128]{2,1,0:T(8,128)S(1)}, f32[112,128]{1,0:T(8,128)S(1)}...) custom-call(f32[19,8,1024]{2,1,0:T(8,128)S(1)} %bitcast.5, ...), custom_call_target="tpu_custom_call" | custom-call | flops 8000000000 | bytes 28800000 | tf_op jit(solution)/shard_map/pallas_call | solution.py:1224
  23.0 0.7 %collective-permute-start.5 = (f32[112,128]{1,0:T(8,128)S(1)}, f32[112,128]{1,0:T(8,128)S(1)}, u32[]{:S(2)}, u32[]{:S(2)}) collective-permute-start(f32[112,128]{1,0:T(8,128)S(1)} %get-tuple-element.34), channel_id=1, source_target_pairs={{24,16},{25,17},{26,18},{27,19},{28,20},{29,21},{30,22},{31,23}} | collective-permute-start | bytes 172040 | tf_op jit(solution)/shard_map/ppermute | solution.py:1283
  23.7 0.1 shard_map.30
  23.8 0.7 %collective-permute-start.10 = (f32[160,128]{1,0:T(8,128)S(1)}, f32[160,128]{1,0:T(8,128)S(1)}, u32[]{:S(2)}, u32[]{:S(2)}) collective-permute-start(f32[160,128]{1,0:T(8,128)S(1)} %get-tuple-element.48), channel_id=1, source_target_pairs={{24,16},{25,17},{26,18},{27,19},{28,20},{29,21},{30,22},{31,23}} | collective-permute-start | bytes 245768 | tf_op jit(solution)/shard_map/ppermute | solution.py:1292
  24.5 0.7 %collective-permute-start.9 = (f32[40,128]{1,0:T(8,128)S(1)}, f32[40,128]{1,0:T(8,128)S(1)}, u32[]{:S(2)}, u32[]{:S(2)}) collective-permute-start(f32[40,128]{1,0:T(8,128)S(1)} %get-tuple-element.47), channel_id=1, source_target_pairs={{24,0},{25,1},{26,2},{27,3},{28,4},{29,5},{30,6},{31,7}} | collective-permute-start | bytes 61448 | tf_op jit(solution)/shard_map/ppermute | solution.py:1291
  25.1 1.9 %collective-permute-start.8 = (f32[19,16,128]{2,1,0:T(8,128)S(1)}, f32[19,16,128]{2,1,0:T(8,128)S(1)}, u32[]{:S(2)}, u32[]{:S(2)}) collective-permute-start(f32[19,16,128]{2,1,0:T(8,128)S(1)} %get-tuple-element.46), channel_id=1, source_target_pairs={{16,8},{8,0},{17,9},{9,1},{18,10},{10,2},{19,11},{11,3},{20,12},{1... | collective-permute-start | bytes 466952 | tf_op jit(solution)/shard_map/ppermute | solution.py:1284
  27.1 0.0 collective-permute-done.5.flows
  27.1 1.3 %collective-permute-start.7 = (f32[40,128]{1,0:T(8,128)S(1)}, f32[40,128]{1,0:T(8,128)S(1)}, u32[]{:S(2)}, u32[]{:S(2)}) collective-permute-start(f32[40,128]{1,0:T(8,128)S(1)} %broadcast_select_fusion), channel_id=1, source_target_pairs={{24,8},{16,0},{25,9},{17,1},{26,10},{18,2},{27,11},{19,3},{28,12},... | collective-permute-start | bytes 61448 | tf_op jit(solution)/shard_map/ppermute | solution.py:1300
  28.4 1.3 %collective-permute-start.6 = (f32[160,128]{1,0:T(8,128)S(1)}, f32[160,128]{1,0:T(8,128)S(1)}, u32[]{:S(2)}, u32[]{:S(2)}) collective-permute-start(f32[160,128]{1,0:T(8,128)S(1)} %get-tuple-element.43), channel_id=1, source_target_pairs={{16,8},{17,9},{18,10},{19,11},{20,12},{21,13},{22,14},{23,15}} | collective-permute-start | bytes 245768 | tf_op jit(solution)/shard_map/ppermute | solution.py:1301
  29.7 0.0 collective-permute-done.9.far_coarse
  29.7 3.9 %collective-permute-done.7.far = f32[40,128]{1,0:T(8,128)S(1)} collective-permute-done((f32[40,128]{1,0:T(8,128)S(1)}, f32[40,128]{1,0:T(8,128)S(1)}, u32[]{:S(2)}, u32[]{:S(2)}) %collective-permute-start.7) | collective-permute-done | bytes 20512 | tf_op jit(solution)/shard_map/ppermute | solution.py:1300
  33.6 0.0 collective-permute-done.10.means
  33.6 0.0 collective-permute-done.8.early
  33.6 0.3 shard_map.32
  33.9 2.0 %collective-permute-done.6.late = f32[160,128]{1,0:T(8,128)S(1)} collective-permute-done((f32[160,128]{1,0:T(8,128)S(1)}, f32[160,128]{1,0:T(8,128)S(1)}, u32[]{:S(2)}, u32[]{:S(2)}) %collective-permute-start.6) | collective-permute-done | bytes 81952 | tf_op jit(solution)/shard_map/ppermute | solution.py:1301
  35.9 1.3 %shard_map.33 = f32[19,8,1024]{2,1,0:T(8,128)} custom-call(f32[19,8,1024]{2,1,0:T(8,128)S(1)} %get-tuple-element.33.old_state, f32[19,2,32,128]{3,2,1,0:T(8,128)S(1)} %get-tuple-element.41.result, f32[19,8,1024]{2,1,0:T(8,128)S(1)} %get-tuple-element.42.third_state, f32[160,128]{1,0:T(8,128)S(1)} %collective-permute-done.6.late, ...), custom_call_target="tpu_custom_call" | custom-call | flops 1000000000 | bytes 3600000 | tf_op jit(solution)/shard_map/pallas_call | solution.py:1224
  (2 shorter events, 0.0 us)
Async XLA Ops:
  0.8 1.1 %copy-start = (f32[1,19,8,1024]{3,2,1,0:T(8,128)S(1)}, f32[1,19,8,1024]{3,2,1,0:T(8,128)}, u32[]{:S(2)}) copy-start(f32[1,19,8,1024]{3,2,1,0:T(8,128)} %param.2) | copy-start | bytes 1867780
  1.8 18.5 %copy-start.1 = (f32[1,19,8,1024]{3,2,1,0:T(8,128)S(1)}, f32[1,19,8,1024]{3,2,1,0:T(8,128)}, u32[]{:S(2)}) copy-start(f32[1,19,8,1024]{3,2,1,0:T(8,128)} %param.2) | copy-start | bytes 1867780
  3.3 17.1 %collective-permute-start.2 = (f32[544,128]{1,0:T(8,128)S(1)}, f32[544,128]{1,0:T(8,128)S(1)}, u32[]{:S(2)}, u32[]{:S(2)}) collective-permute-start(f32[544,128]{1,0:T(8,128)S(1)} %get-tuple-element.30), channel_id=1, source_target_pairs={{0,8},{8,16},{16,24},{1,9},{9,17},{17,25},{2,10},{10,18},{18,26},{... | collective-permute-start | bytes 835592 | tf_op jit(solution)/shard_map/ppermute | solution.py:1261
  6.4 14.0 %collective-permute-start = (f32[20,16,128]{2,1,0:T(8,128)S(1)}, f32[20,16,128]{2,1,0:T(8,128)S(1)}, u32[]{:S(2)}, u32[]{:S(2)}) collective-permute-start(f32[20,16,128]{2,1,0:T(8,128)S(1)} %get-tuple-element.28), channel_id=1, source_target_pairs={{0,1},{1,2},{2,3},{3,4},{4,5},{5,6},{6,7},{7,0},{8,9},{9,10},{10,1... | collective-permute-start | bytes 491528 | tf_op jit(solution)/shard_map/ppermute | solution.py:1264
  8.5 11.9 %collective-permute-start.1 = (f32[20,16,128]{2,1,0:T(8,128)S(1)}, f32[20,16,128]{2,1,0:T(8,128)S(1)}, u32[]{:S(2)}, u32[]{:S(2)}) collective-permute-start(f32[20,16,128]{2,1,0:T(8,128)S(1)} %get-tuple-element.29), channel_id=1, source_target_pairs={{0,7},{1,0},{2,1},{3,2},{4,3},{5,4},{6,5},{7,6},{8,15},{9,8},{10,9... | collective-permute-start | bytes 491528 | tf_op jit(solution)/shard_map/ppermute | solution.py:1265
  8.5 6.4 %collective-permute-start.3 = (f32[16,8,128]{2,1,0:T(8,128)S(1)}, f32[16,8,128]{2,1,0:T(8,128)S(1)}, u32[]{:S(2)}, u32[]{:S(2)}) collective-permute-start(f32[16,8,128]{2,1,0:T(8,128)S(1)} %get-tuple-element.31), channel_id=1, source_target_pairs={{0,9},{1,10},{2,11},{3,12},{4,13},{5,14},{6,15},{7,8},{8,17},{9,18... | collective-permute-start | bytes 196616 | tf_op jit(solution)/shard_map/ppermute | solution.py:1262
  13.0 7.4 %collective-permute-start.4 = (f32[16,8,128]{2,1,0:T(8,128)S(1)}, f32[16,8,128]{2,1,0:T(8,128)S(1)}, u32[]{:S(2)}, u32[]{:S(2)}) collective-permute-start(f32[16,8,128]{2,1,0:T(8,128)S(1)} %get-tuple-element.32), channel_id=1, source_target_pairs={{0,15},{1,8},{2,9},{3,10},{4,11},{5,12},{6,13},{7,14},{8,23},{9,16... | collective-permute-start | bytes 196616 | tf_op jit(solution)/shard_map/ppermute | solution.py:1263
  23.0 4.0 %collective-permute-start.5 = (f32[112,128]{1,0:T(8,128)S(1)}, f32[112,128]{1,0:T(8,128)S(1)}, u32[]{:S(2)}, u32[]{:S(2)}) collective-permute-start(f32[112,128]{1,0:T(8,128)S(1)} %get-tuple-element.34), channel_id=1, source_target_pairs={{24,16},{25,17},{26,18},{27,19},{28,20},{29,21},{30,22},{31,23}} | collective-permute-start | bytes 172040 | tf_op jit(solution)/shard_map/ppermute | solution.py:1283
  23.8 9.8 %collective-permute-start.10 = (f32[160,128]{1,0:T(8,128)S(1)}, f32[160,128]{1,0:T(8,128)S(1)}, u32[]{:S(2)}, u32[]{:S(2)}) collective-permute-start(f32[160,128]{1,0:T(8,128)S(1)} %get-tuple-element.48), channel_id=1, source_target_pairs={{24,16},{25,17},{26,18},{27,19},{28,20},{29,21},{30,22},{31,23}} | collective-permute-start | bytes 245768 | tf_op jit(solution)/shard_map/ppermute | solution.py:1292
  24.5 5.3 %collective-permute-start.9 = (f32[40,128]{1,0:T(8,128)S(1)}, f32[40,128]{1,0:T(8,128)S(1)}, u32[]{:S(2)}, u32[]{:S(2)}) collective-permute-start(f32[40,128]{1,0:T(8,128)S(1)} %get-tuple-element.47), channel_id=1, source_target_pairs={{24,0},{25,1},{26,2},{27,3},{28,4},{29,5},{30,6},{31,7}} | collective-permute-start | bytes 61448 | tf_op jit(solution)/shard_map/ppermute | solution.py:1291
  25.1 8.5 %collective-permute-start.8 = (f32[19,16,128]{2,1,0:T(8,128)S(1)}, f32[19,16,128]{2,1,0:T(8,128)S(1)}, u32[]{:S(2)}, u32[]{:S(2)}) collective-permute-start(f32[19,16,128]{2,1,0:T(8,128)S(1)} %get-tuple-element.46), channel_id=1, source_target_pairs={{16,8},{8,0},{17,9},{9,1},{18,10},{10,2},{19,11},{11,3},{20,12},{1... | collective-permute-start | bytes 466952 | tf_op jit(solution)/shard_map/ppermute | solution.py:1284
  27.1 6.5 %collective-permute-start.7 = (f32[40,128]{1,0:T(8,128)S(1)}, f32[40,128]{1,0:T(8,128)S(1)}, u32[]{:S(2)}, u32[]{:S(2)}) collective-permute-start(f32[40,128]{1,0:T(8,128)S(1)} %broadcast_select_fusion), channel_id=1, source_target_pairs={{24,8},{16,0},{25,9},{17,1},{26,10},{18,2},{27,11},{19,3},{28,12},... | collective-permute-start | bytes 61448 | tf_op jit(solution)/shard_map/ppermute | solution.py:1300
  28.4 7.4 %collective-permute-start.6 = (f32[160,128]{1,0:T(8,128)S(1)}, f32[160,128]{1,0:T(8,128)S(1)}, u32[]{:S(2)}, u32[]{:S(2)}) collective-permute-start(f32[160,128]{1,0:T(8,128)S(1)} %get-tuple-element.43), channel_id=1, source_target_pairs={{16,8},{17,9},{18,10},{19,11},{20,12},{21,13},{22,14},{23,15}} | collective-permute-start | bytes 245768 | tf_op jit(solution)/shard_map/ppermute | solution.py:1301
